TPU v7x, 32 devices: a whole 2x2x4 slice. The times are simulated.
32 devices in a mesh: seq: 8 (over y, x, core), chan: 4 (over z).
Axes of the slice: x: 2, y: 2, z: 4, core: 2. Of those that a mesh axis runs over, the one named last changes fastest.
Arguments:
- query_proj: bfloat16 [4096, 1024], P('chan', 'seq'), may hold values from -6 to 6
- key_proj: bfloat16 [4096, 1024], P('chan', 'seq'), may hold values from -6 to 6
- value_proj: bfloat16 [4096, 1024], P('chan', 'seq'), may hold values from -6 to 6
- cotangent: bfloat16 [4096, 1024], P('chan', 'seq'), may hold values from -6 to 6
- filter_taps: bfloat16 [1024, 1024], P('seq'), may hold values from -6 to 6
Outputs:
- gated_out: bfloat16 [4096, 1024], P('chan', 'seq')
- query_grad: bfloat16 [4096, 1024], P('chan', 'seq')
- key_grad: bfloat16 [4096, 1024], P('chan', 'seq')
- value_grad: bfloat16 [4096, 1024], P('chan', 'seq')
- filter_grad: float32 [1024, 1024], P('seq', 'chan')
All inputs are finite; a program needn't handle non-finite values.
Results may differ from a plain program's by a relative error of at most 0.0057.
Values may be sent and summed in bfloat16 or wider, within the bound.
No kernel may reach another device: no remote copies, remote signals or barrier semaphores. Data moves between devices by JAX's collectives and lax.ppermute only.
A program may use at most 64 MiB of HBM per device.

v0:
```python
import math

import jax
import jax.numpy as jnp
import ml_dtypes
import numpy as np
from jax import lax
from jax.experimental import pallas as pl
from jax.experimental.pallas import tpu as pltpu
from jax.sharding import PartitionSpec as P

BLOCK = 256
LANES = 128


def transform_tables(scale):
    freq = np.arange(BLOCK) + 0.5
    freq = np.concatenate([freq[0::2], freq[1::2]])
    angle = 2.0 * np.pi * np.outer(np.arange(BLOCK), freq) / (2 * BLOCK)
    forward = np.concatenate([np.cos(angle), -np.sin(angle)], axis=1)
    inverse = np.concatenate([np.cos(angle).T, -np.sin(angle).T], axis=0) * (scale / BLOCK)
    high = forward.astype(ml_dtypes.bfloat16)
    low = (forward - high.astype(np.float64)).astype(ml_dtypes.bfloat16)
    return high, low, inverse.astype(ml_dtypes.bfloat16)


def dot(left, right):
    return jnp.dot(left, right, preferred_element_type=jnp.float32)


def total(terms):
    real, imag = terms[0]
    for more_real, more_imag in terms[1:]:
        real, imag = real + more_real, imag + more_imag
    return real, imag


def times(left, right):
    return left[0] * right[0] - left[1] * right[1], left[0] * right[1] + left[1] * right[0]


def times_conj(left, right):
    return left[0] * right[0] + left[1] * right[1], left[1] * right[0] - left[0] * right[1]


def conv_kernel(cols_ref, taps_ref, high_ref, low_ref, inv_ref, out_ref, lag_ref, spec, filt, prod):
    chans, length = taps_ref.shape
    count = length // BLOCK
    width = lag_ref.shape[2]
    per = BLOCK // LANES
    for a in range(count):
        signal = jnp.concatenate([cols_ref[per * a + u] for u in range(per)], axis=1)
        spec[a] = dot(signal, high_ref[...]) + dot(signal, low_ref[...])
        taps = taps_ref[:, a * BLOCK : (a + 1) * BLOCK]
        filt[a] = dot(taps, high_ref[...]) + dot(taps, low_ref[...])
    tile = 16 if chans % 16 == 0 else chans

    def products(row):
        rows, others = pl.ds(row, tile), pl.ds(chans + row, tile)
        for half in range(BLOCK // LANES):
            sign = 1.0 if half < BLOCK // LANES // 2 else -1.0
            re, im = pl.ds(half * LANES, LANES), pl.ds(BLOCK + half * LANES, LANES)
            mixed = [(spec[a, rows, re], spec[a, rows, im]) for a in range(count)]
            pulled = [(spec[a, others, re], spec[a, others, im]) for a in range(count)]
            taps = [(filt[a, rows, re], filt[a, rows, im]) for a in range(count)]

            def put(which, c, value):
                prod[which, c, rows, re] = value[0].astype(jnp.bfloat16)
                prod[which, c, rows, im] = value[1].astype(jnp.bfloat16)

            before = None
            for c in range(count):
                here = total([times(mixed[a], taps[c - a]) for a in range(c + 1)])
                put(0, c, here if c == 0 else (here[0] - sign * before[1], here[1] + sign * before[0]))
                before = here
            for which, other in ((1, taps), (2, mixed)):
                after = None
                for c in reversed(range(count)):
                    here = total([times_conj(pulled[a], other[a - c]) for a in range(c, count)])
                    put(which, c, here if after is None else (here[0] + sign * after[1], here[1] - sign * after[0]))
                    after = here

    if chans == tile:
        products(0)
    else:

        def step(i, carry):
            products(pl.multiple_of(i * tile, tile))
            return carry

        lax.fori_loop(0, chans // tile, step, 0)
    for c in range(count):
        for which in range(3):
            result = dot(prod[which, c], inv_ref[...])
            for u in range(per):
                part = result[:, u * LANES : (u + 1) * LANES]
                at = per * c + u
                if which < 2:
                    out_ref[at, which * chans : (which + 1) * chans] = part.astype(jnp.bfloat16)
                else:
                    begin = at * LANES
                    lag_ref[begin // width, :, begin % width : begin % width + LANES] = part.astype(lag_ref.dtype)


def convolve(cols, taps, pieces):
    chans, length = taps.shape
    count = length // BLOCK
    high, low, inverse = transform_tables(1.0 / math.sqrt(length))
    vmem = pl.BlockSpec(memory_space=pltpu.VMEM)
    return pl.pallas_call(
        conv_kernel,
        out_shape=(
            jax.ShapeDtypeStruct(cols.shape, jnp.bfloat16),
            jax.ShapeDtypeStruct((pieces, chans, length // pieces), jnp.bfloat16),
        ),
        in_specs=[vmem] * 5,
        out_specs=(vmem, vmem),
        scratch_shapes=[
            pltpu.VMEM((count, 2 * chans, 2 * BLOCK), jnp.float32),
            pltpu.VMEM((count, chans, 2 * BLOCK), jnp.float32),
            pltpu.VMEM((3, count, chans, 2 * BLOCK), jnp.bfloat16),
        ],
        compiler_params=pltpu.CompilerParams(vmem_limit_bytes=24 * 1024 * 1024),
        name="convolve",
    )(cols, taps, jnp.asarray(high), jnp.asarray(low), jnp.asarray(inverse))


def on_device(query, key, value, upstream, taps):
    seq, chan = lax.axis_size("seq"), lax.axis_size("chan")
    wide, positions = query.shape
    chans = wide // seq
    mixed = (key * value).reshape(seq, chans, positions)
    pulled = (upstream * query).reshape(seq, chans, positions)
    sent = jnp.concatenate([mixed, pulled], axis=1)
    cols = lax.all_to_all(sent, "seq", split_axis=0, concat_axis=0)
    out_cols, lag = convolve(cols, taps, chan)
    rows = lax.all_to_all(out_cols, "seq", split_axis=0, concat_axis=0)
    lags = lax.all_to_all(lag, "chan", split_axis=0, concat_axis=0)
    filter_grad = jnp.sum(lags.astype(jnp.float32), axis=0)
    conv = rows[:, :chans].reshape(wide, positions)
    back = rows[:, chans:].reshape(wide, positions)
    return query * conv, upstream * conv, back * value, back * key, filter_grad


def solution(mesh):
    block = P("chan", "seq")
    return jax.shard_map(
        on_device,
        mesh=mesh,
        in_specs=(block, block, block, block, P("seq", None)),
        out_specs=(block, block, block, block, P("seq", "chan")),
        check_vma=False,
    )
```

profile of v0, /device:TPU:0, one launch (start us, length us, event | category | flops | bytes accessed | tf_op | source)
XLA Modules:
  0.0 47.6 jit_solution(611079487714862867)
XLA Ops:
  0.6 0.0 copy-start.7
  0.6 0.0 copy-start.4
  0.7 1.2 %mul.19 = bf16[1024,128]{1,0:T(8,128)(2,1)S(1)} multiply(bf16[1024,128]{1,0:T(8,128)(2,1)} %param.11, bf16[1024,128]{1,0:T(8,128)(2,1)} %param.8) | non-fusion elementwise | flops 131072 | bytes 786432 | tf_op jit(solution)/shard_map/mul | solution.py:133
  1.8 0.0 copy-done.7
  1.8 0.0 copy-done.4
  1.8 0.1 mul.18
  2.0 0.0 copy-start
  2.0 0.0 copy-start.1
  2.0 0.0 copy-start.2
  2.0 0.0 copy-start.3
  2.0 14.8 %all_to_all.15.cols_ref = bf16[8,256,128]{2,1,0:T(8,128)(2,1)S(1)} all-to-all(bf16[8,256,128]{2,1,0:T(8,128)(2,1)S(1)} %pad_maximum_fusion), channel_id=1, replica_groups=mesh['seq'=8,'chan'=4] {'seq'}, dimensions={0} | all-to-all | bytes 1048576 | tf_op jit(solution)/shard_map/all_to_all | solution.py:135
  16.9 0.0 copy-done
  16.9 0.0 copy-done.1
  16.9 0.0 copy-done.2
  16.9 0.0 copy-done.3
  16.9 3.5 %convolve.1 = (bf16[8,256,128]{2,1,0:T(8,128)(2,1)}, bf16[4,128,256]{2,1,0:T(8,128)(2,1)S(1)}) custom-call(bf16[8,256,128]{2,1,0:T(8,128)(2,1)S(1)} %all_to_all.15.cols_ref, bf16[128,1024]{1,0:T(8,128)(2,1)S(1)} %copy-done, bf16[256,512]{1,0:T(8,128)(2,1)S(1)} %copy-done.3, bf16[256,512]{1,0:T(8,128)(2,1)S(1)} %copy-done.2, bf16[512,256]{1,0:T(8,128)(2,1)S(1)} %copy-done.1), custom_call_target="tpu_custom_call" | custom-call | tf_op jit(solution)/shard_map/convolve/pallas_call | solution.py:110
  20.4 12.9 %all_to_all.16 = bf16[4,128,256]{2,1,0:T(8,128)(2,1)S(1)} all-to-all(bf16[4,128,256]{2,1,0:T(8,128)(2,1)S(1)} %get-tuple-element.8), channel_id=1, replica_groups=mesh['seq'=8,'chan'=4] {'chan'}, dimensions={0} | all-to-all | bytes 524288 | tf_op jit(solution)/shard_map/all_to_all | solution.py:138
  33.3 3.5 %all-to-all-start.1 = ((bf16[8,256,128]{2,1,0:T(8,128)(2,1)}), bf16[8,256,128]{2,1,0:T(8,128)(2,1)S(1)}, u32[]{:S(2)}, u32[]{:S(2)}) async-start(bf16[8,256,128]{2,1,0:T(8,128)(2,1)} %get-tuple-element.7), calls=%async_computation.1 | async-start | bytes 1048576 | tf_op jit(solution)/shard_map/all_to_all | solution.py:137
  36.8 0.7 %convert_reduce_fusion = f32[128,256]{1,0:T(8,128)} fusion(bf16[4,128,256]{2,1,0:T(8,128)(2,1)S(1)} %all_to_all.16), kind=kLoop, calls=%fused_computation.1 | loop fusion | flops 229376 | bytes 393216 | tf_op jit(solution)/shard_map/reduce_sum | solution.py:139
  37.5 0.0 copy-start.5
  37.5 0.0 copy-start.6
  37.5 9.0 %all-to-all-done.1 = bf16[8,256,128]{2,1,0:T(8,128)(2,1)S(1)} async-done(((bf16[8,256,128]{2,1,0:T(8,128)(2,1)}), bf16[8,256,128]{2,1,0:T(8,128)(2,1)S(1)}, u32[]{:S(2)}, u32[]{:S(2)}) %all-to-all-start.1) | async-done | bytes 524320 | tf_op jit(solution)/shard_map/all_to_all | solution.py:137
  46.5 0.0 copy-done.5
  46.5 0.0 copy-done.6
  46.5 1.0 %bitcast_multiply_fusion = (bf16[1024,128]{1,0:T(8,128)(2,1)}, bf16[1024,128]{1,0:T(8,128)(2,1)}, bf16[1024,128]{1,0:T(8,128)(2,1)}, bf16[1024,128]{1,0:T(8,128)(2,1)}) fusion(bf16[1024,128]{1,0:T(8,128)(2,1)S(1)} %copy-done.4, bf16[8,128,128]{2,1,0:T(8,128)(2,1)S(1)} %get-tuple-element.9, bf16[1024,128]{1,0:T(8,128)(2,1)S(1)} %copy-done.7, ...), kind=kLoop, calls=%fused_computation.2 | loop fusion | flops 524288 | bytes 2621440 | tf_op jit(solution)/shard_map/mul | solution.py:142
  (2 shorter events, 0.1 us)
Async XLA Ops:
  0.6 1.2 %copy-start.7 = (bf16[1024,128]{1,0:T(8,128)(2,1)S(1)}, bf16[1024,128]{1,0:T(8,128)(2,1)}, u32[]{:S(2)}) copy-start(bf16[1024,128]{1,0:T(8,128)(2,1)} %param.10) | copy-start | bytes 786436
  0.6 1.2 %copy-start.4 = (bf16[1024,128]{1,0:T(8,128)(2,1)S(1)}, bf16[1024,128]{1,0:T(8,128)(2,1)}, u32[]{:S(2)}) copy-start(bf16[1024,128]{1,0:T(8,128)(2,1)} %param.9) | copy-start | bytes 786436
  2.0 14.9 %copy-start = (bf16[128,1024]{1,0:T(8,128)(2,1)S(1)}, bf16[128,1024]{1,0:T(8,128)(2,1)}, u32[]{:S(2)}) copy-start(bf16[128,1024]{1,0:T(8,128)(2,1)} %taps_ref.1) | copy-start | bytes 786436
  2.0 14.9 %copy-start.1 = (bf16[512,256]{1,0:T(8,128)(2,1)S(1)}, bf16[512,256]{1,0:T(8,128)(2,1)}, u32[]{:S(2)}) copy-start(bf16[512,256]{1,0:T(8,128)(2,1)} %constant.10.clone.inv_ref) | copy-start | bytes 786436
  2.0 14.9 %copy-start.2 = (bf16[256,512]{1,0:T(8,128)(2,1)S(1)}, bf16[256,512]{1,0:T(8,128)(2,1)}, u32[]{:S(2)}) copy-start(bf16[256,512]{1,0:T(8,128)(2,1)} %constant.9.clone.low_ref) | copy-start | bytes 786436
  2.0 14.9 %copy-start.3 = (bf16[256,512]{1,0:T(8,128)(2,1)S(1)}, bf16[256,512]{1,0:T(8,128)(2,1)}, u32[]{:S(2)}) copy-start(bf16[256,512]{1,0:T(8,128)(2,1)} %constant.8.clone.high_ref) | copy-start | bytes 786436
  33.3 13.2 %all-to-all-start.1 = ((bf16[8,256,128]{2,1,0:T(8,128)(2,1)}), bf16[8,256,128]{2,1,0:T(8,128)(2,1)S(1)}, u32[]{:S(2)}, u32[]{:S(2)}) async-start(bf16[8,256,128]{2,1,0:T(8,128)(2,1)} %get-tuple-element.7), calls=%async_computation.1 | async-start | bytes 1048576 | tf_op jit(solution)/shard_map/all_to_all | solution.py:137
  37.5 9.0 %copy-start.5 = (bf16[1024,128]{1,0:T(8,128)(2,1)S(1)}, bf16[1024,128]{1,0:T(8,128)(2,1)}, u32[]{:S(2)}) copy-start(bf16[1024,128]{1,0:T(8,128)(2,1)} %param.11) | copy-start | bytes 786436
  37.5 9.0 %copy-start.6 = (bf16[1024,128]{1,0:T(8,128)(2,1)S(1)}, bf16[1024,128]{1,0:T(8,128)(2,1)}, u32[]{:S(2)}) copy-start(bf16[1024,128]{1,0:T(8,128)(2,1)} %param.8) | copy-start | bytes 786436
where the time goes:
time: 47.9 us; the launch traced here: 47.6 us
  blocking collectives  27.7 us (58%)
  waiting for transfers between devices  8.98 us (19%)
  Pallas kernels  3.55 us (7%)
  starting transfers between devices  3.49 us (7%)
  other arithmetic  2.97 us (6%)
  between operations  0.76 us (2%)
    all_to_all x1, blocking collectives, on_device(): cols = lax.all_to_all(sent, 'seq', split_axis=0, concat_axis=0)  14.8 us
    all_to_all x1, blocking collectives, on_device(): lags = lax.all_to_all(lag, 'chan', split_axis=0, concat_axis=0)  12.9 us
    all_to_all x1, waiting for transfers between devices, on_device(): rows = lax.all_to_all(out_cols, 'seq', split_axis=0, concat_axis=0)  8.98 us
    pallas_call x1, Pallas kernels, convolve(): pl.pallas_call(conv_kernel, out_shape=(jax.ShapeDtypeStruct(cols.shape, j...  3.55 us
    all_to_all x1, starting transfers between devices, on_device(): rows = lax.all_to_all(out_cols, 'seq', split_axis=0, concat_axis=0)  3.49 us
    mul x1, other arithmetic, on_device(): pulled = (upstream * query).reshape(seq, chans, positions)  1.16 us
    mul x1, other arithmetic, on_device(): back * key  1.01 us
  transfers between devices with their start and end apart: 1, of which 1 were waited for; matrix products, arithmetic and copies ran while one was open for 1% of the time, Pallas kernels for 0%

commit v1 on v0

v1 whole, which is shorter than its diff:
```python
import functools
import math

import jax
import jax.numpy as jnp
import ml_dtypes
import numpy as np
from jax import lax
from jax.experimental import pallas as pl
from jax.experimental.pallas import tpu as pltpu
from jax.sharding import PartitionSpec as P

BLOCK = 256
LANES = 128


def transform_tables(scale):
    freq = np.arange(BLOCK) + 0.5
    freq = np.concatenate([freq[0::2], freq[1::2]])
    angle = 2.0 * np.pi * np.outer(np.arange(BLOCK), freq) / (2 * BLOCK)
    forward = np.concatenate([np.cos(angle), -np.sin(angle)], axis=1)
    inverse = np.concatenate([np.cos(angle).T, -np.sin(angle).T], axis=0) * (scale / BLOCK)
    high = forward.astype(ml_dtypes.bfloat16)
    low = (forward - high.astype(np.float64)).astype(ml_dtypes.bfloat16)
    return high, low, inverse.astype(ml_dtypes.bfloat16)


def dot(left, right):
    return jnp.dot(left, right, preferred_element_type=jnp.float32)


def total(terms):
    real, imag = terms[0]
    for more_real, more_imag in terms[1:]:
        real, imag = real + more_real, imag + more_imag
    return real, imag


def times(left, right):
    return left[0] * right[0] - left[1] * right[1], left[0] * right[1] + left[1] * right[0]


def times_conj(left, right):
    return left[0] * right[0] + left[1] * right[1], left[1] * right[0] - left[0] * right[1]


def place():
    me = lax.axis_index("seq")
    return me // 2, me % 2


def forward(block, high_ref, low_ref):
    return dot(block, high_ref[...]) + dot(block, low_ref[...])


def tiles(chans, body):
    tile = 16 if chans % 16 == 0 else chans

    def step(i, carry):
        rows = pl.ds(pl.multiple_of(i * tile, tile), tile)
        for half in range(BLOCK // LANES):
            sign = 1.0 if half < BLOCK // LANES // 2 else -1.0
            body(rows, pl.ds(half * LANES, LANES), pl.ds(BLOCK + half * LANES, LANES), sign)
        return carry

    lax.fori_loop(0, chans // tile, step, 0)


def spectra(ref, rows, re, im):
    return [(ref[a, rows, re], ref[a, rows, im]) for a in range(ref.shape[0])]


def convolve_tile(signal, taps, sign, put):
    before = None
    for c in range(len(signal)):
        here = total([times(signal[a], taps[c - a]) for a in range(c + 1)])
        put(c, here if c == 0 else (here[0] - sign * before[1], here[1] + sign * before[0]))
        before = here


def correlate_tile(signal, other, sign, put):
    after = None
    for c in reversed(range(len(signal))):
        here = total([times_conj(signal[a], other[a - c]) for a in range(c, len(signal))])
        put(c, here if after is None else (here[0] + sign * after[1], here[1] - sign * after[0]))
        after = here


def putter(prod, rows, re, im):
    def put(c, value):
        prod[c, rows, re] = value[0].astype(jnp.bfloat16)
        prod[c, rows, im] = value[1].astype(jnp.bfloat16)

    return put


def gate_kernel(*refs):
    sources, held, (own_ref, other_ref, sems) = refs[:4], refs[4:8], refs[8:]
    chip, core = place()
    copies = [pltpu.make_async_copy(a, b, sems.at[i]) for i, (a, b) in enumerate(zip(sources, held))]
    for copy in copies:
        copy.start()
    for i in range(2):
        left, right = held[2 * i], held[2 * i + 1]
        copies[2 * i].wait()
        copies[2 * i + 1].wait()
        for k in range(own_ref.shape[0]):
            mine, theirs = 2 * (chip ^ k) + core, 2 * (chip ^ k) + 1 - core
            own_ref[k, i] = left[mine] * right[mine]
            other_ref[k, i] = left[theirs] * right[theirs]


def taps_kernel(taps_ref, high_ref, low_ref, filt_ref):
    for a in range(filt_ref.shape[0]):
        filt_ref[a] = forward(taps_ref[:, a * BLOCK : (a + 1) * BLOCK], high_ref, low_ref)


def sides_kernel(*refs):
    count = len(refs) - 9
    cols_refs, refs = refs[:count], refs[count:]
    filt_ref, high_ref, low_ref, inv_ref, own_ref, other_ref, mix_ref, pull_ref, prod = refs
    chip, core = place()
    for i, spec_ref in enumerate((mix_ref, pull_ref)):
        for k in range(count):
            block = jnp.concatenate([cols_refs[k][core, i], cols_refs[k][1 - core, i]], axis=1)
            spec_ref[chip ^ k] = forward(block, high_ref, low_ref)

    def body(rows, re, im, sign):
        taps = spectra(filt_ref, rows, re, im)
        convolve_tile(spectra(mix_ref, rows, re, im), taps, sign, putter(prod.at[0], rows, re, im))
        correlate_tile(spectra(pull_ref, rows, re, im), taps, sign, putter(prod.at[1], rows, re, im))

    tiles(filt_ref.shape[1], body)
    for k in range(count):
        for i in range(2):
            result = dot(prod[i, chip ^ k], inv_ref[...]).astype(jnp.bfloat16)
            first, second = result[:, :LANES], result[:, LANES:]
            own_ref[k, i] = jnp.where(core == 0, first, second)
            other_ref[k, i] = jnp.where(core == 0, second, first)


def lag_kernel(pull_ref, mix_ref, inv_ref, lag_ref, prod):
    width = lag_ref.shape[2]
    slot = lax.axis_index("chan")

    def body(rows, re, im, sign):
        correlate_tile(spectra(pull_ref, rows, re, im), spectra(mix_ref, rows, re, im), sign, putter(prod, rows, re, im))

    tiles(prod.shape[1], body)
    for c in range(prod.shape[0]):
        result = dot(prod[c], inv_ref[...]).astype(jnp.bfloat16)
        for u in range(BLOCK // LANES):
            begin = c * BLOCK + u * LANES
            lag_ref[slot ^ (begin // width), :, begin % width : begin % width + LANES] = result[:, u * LANES : (u + 1) * LANES]


def grads_kernel(count, *refs):
    rows_refs, (query_ref, key_ref, value_ref, upstream_ref) = refs[:count], refs[count : count + 4]
    lag_ref, got_refs = refs[count + 4], refs[count + 5 : -9]
    outs, filter_out, (held, sems, sums, sum_sem) = refs[-9:-5], refs[-5], refs[-4:]
    chip, core = place()
    total_lag = lag_ref[0].astype(jnp.float32)
    for got in got_refs:
        total_lag = total_lag + got[...].astype(jnp.float32)
    sums[...] = total_lag
    copies = [pltpu.make_async_copy(sums, filter_out, sum_sem)]
    copies[0].start()
    for k in range(count):
        there = 2 * (chip ^ k)
        for at in range(2):
            group = there + at
            conv, back = rows_refs[k][core ^ at, 0], rows_refs[k][core ^ at, 1]
            held[0, 2 * k + at] = conv * query_ref[group]
            held[1, 2 * k + at] = conv * upstream_ref[group]
            held[2, 2 * k + at] = back * value_ref[group]
            held[3, 2 * k + at] = back * key_ref[group]
        for i, out in enumerate(outs):
            copy = pltpu.make_async_copy(held.at[i, pl.ds(2 * k, 2)], out.at[pl.ds(there, 2)], sems.at[i, k])
            copy.start()
            copies.append(copy)
    for copy in copies:
        copy.wait()


VMEM = pl.BlockSpec(memory_space=pltpu.VMEM)
ANY = pl.BlockSpec(memory_space=pl.ANY)
HBM = pl.BlockSpec(memory_space=pltpu.HBM)
LIMIT = 16 * 1024 * 1024


def call(kernel, args, outs, scratch, name, space=VMEM, out_space=VMEM, after=(), flops=0):
    def body(*refs):
        kernel(*refs[: len(args)], *refs[len(args) + len(after) :])

    return pl.pallas_call(
        body,
        out_shape=tuple(jax.ShapeDtypeStruct(shape, kind) for shape, kind in outs),
        in_specs=[space] * len(args) + [ANY] * len(after),
        out_specs=(out_space,) * len(outs),
        scratch_shapes=scratch,
        compiler_params=pltpu.CompilerParams(vmem_limit_bytes=LIMIT),
        cost_estimate=pl.CostEstimate(flops=flops, bytes_accessed=0, transcendentals=0) if flops else None,
        name=name,
    )(*args, *after)


def swap(array, axis, k):
    return lax.ppermute(array, axis, [(i, i ^ k) for i in range(lax.axis_size(axis))])


def exchange(own, other):
    got = swap(other, "seq", 1)
    parts = [jnp.stack([own[k], got[k]]) for k in range(own.shape[0])]
    return [parts[0]] + [swap(parts[k], "seq", 2 * k) for k in range(1, len(parts))]


def on_device(query, key, value, upstream, taps):
    seq, chan = lax.axis_size("seq"), lax.axis_size("chan")
    wide, positions = query.shape
    chans, length = taps.shape
    count = seq // 2
    query, key, value, upstream = (x.reshape(seq, chans, positions) for x in (query, key, value, upstream))
    high, low, inverse = (jnp.asarray(x) for x in transform_tables(1.0 / math.sqrt(length)))
    half = ((count, 2, chans, positions), jnp.bfloat16)
    whole = ((seq, chans, positions), jnp.bfloat16)
    wave = ((count, chans, 2 * BLOCK), jnp.float32)
    key, value, upstream, query, own, other = call(
        gate_kernel,
        tuple(pltpu.with_memory_space_constraint(x, pltpu.HBM) for x in (key, value, upstream, query)),
        (whole,) * 4 + (half,) * 2,
        [pltpu.SemaphoreType.DMA((4,))],
        "gate",
        HBM,
    )
    cols = exchange(own, other)
    (filt,) = call(taps_kernel, (taps, high, low), (wave,), [], "taps")
    own, other, mix_wave, pull_wave = call(
        sides_kernel,
        (*cols, filt, high, low, inverse),
        (half, half, wave, wave),
        [pltpu.VMEM((2, count, chans, 2 * BLOCK), jnp.bfloat16)],
        "sides",
    )
    rows = exchange(own, other)
    pieces = ((chan, chans, length // chan), jnp.bfloat16)
    prod = pltpu.VMEM((count, chans, 2 * BLOCK), jnp.bfloat16)
    (lag,) = call(lag_kernel, (pull_wave, mix_wave, inverse), (pieces,), [prod], "lag", after=(own,))
    got = [swap(lag[k], "chan", k) for k in range(1, chan)]
    sums = ((chans, length // chan), jnp.float32)
    *outs, filter_grad = call(
        functools.partial(grads_kernel, count),
        (*rows, query, key, value, upstream, lag, *got),
        (whole,) * 4 + (sums,),
        [
            pltpu.VMEM((4, seq, chans, positions), jnp.bfloat16),
            pltpu.SemaphoreType.DMA((4, count)),
            pltpu.VMEM(*sums),
            pltpu.SemaphoreType.DMA,
        ],
        "grads",
        out_space=HBM,
    )
    return (*(x.reshape(wide, positions) for x in outs), filter_grad)


def solution(mesh):
    block = P("chan", "seq")
    return jax.shard_map(
        on_device,
        mesh=mesh,
        in_specs=(block, block, block, block, P("seq", None)),
        out_specs=(block, block, block, block, P("seq", "chan")),
        check_vma=False,
    )
```

time: 47.9 us -> 32.1 us (0.67)
  blocking collectives: 27.7 us -> 0 us
  starting transfers between devices: 3.49 us -> 13.7 us
  other arithmetic: 2.97 us -> 0.12 us
  waiting for transfers between devices: 8.98 us -> 11.6 us
  Pallas kernels: 3.55 us -> 5.67 us
    all_to_all x2 -> x0, blocking collectives: 27.7 us -> none  [the longest x1 14.8 us: on_device(): cols = lax.all_to_all(sent, 'seq', split_axis=0, concat_axis=0)]
    ppermute x0 -> x11, starting transfers between devices: none -> 13.7 us  [swap(): lax.ppermute(array, axis, [(i, i ^ k) for i in range(lax.axis_size(axis))])]
    ppermute x0 -> x11, waiting for transfers between devices: none -> 11.6 us  [swap(): lax.ppermute(array, axis, [(i, i ^ k) for i in range(lax.axis_size(axis))])]
    all_to_all x1 -> x0, waiting for transfers between devices: 8.98 us -> none  [on_device(): rows = lax.all_to_all(out_cols, 'seq', split_axis=0, concat_axis=0)]
    all_to_all x1 -> x0, starting transfers between devices: 3.49 us -> none  [on_device(): rows = lax.all_to_all(out_cols, 'seq', split_axis=0, concat_axis=0)]
    mul x3 -> x0, other arithmetic: 2.24 us -> none  [the longest x1 1.16 us: on_device(): pulled = (upstream * query).reshape(seq, chans, positions)]
    pallas_call x1 -> x5, Pallas kernels: 3.55 us -> 5.67 us  [call(): pl.pallas_call(body, out_shape=tuple((jax.ShapeDtypeStruct(shape, kind) f...]
    reduce_sum x1 -> x0, other arithmetic: 0.69 us -> none  [on_device(): filter_grad = jnp.sum(lags.astype(jnp.float32), axis=0)]
  transfers between devices with their start and end apart: 1 -> 11, of which waited for: 1 -> 5; matrix products, arithmetic and copies ran while one was open for 1% -> 1% of each run, Pallas kernels for 0% -> 4%
where the time goes in v1:
time: 32.1 us; the launch traced here: 32 us
  starting transfers between devices  13.7 us (43%)
  waiting for transfers between devices  11.6 us (36%)
  Pallas kernels  5.67 us (18%)
  between operations  0.8 us (2%)
    ppermute x11, starting transfers between devices, swap(): lax.ppermute(array, axis, [(i, i ^ k) for i in range(lax.axis_size(axis))])  13.7 us
    ppermute x11, waiting for transfers between devices, swap(): lax.ppermute(array, axis, [(i, i ^ k) for i in range(lax.axis_size(axis))])  11.6 us
    pallas_call x5, Pallas kernels, call(): pl.pallas_call(body, out_shape=tuple((jax.ShapeDtypeStruct(shape, kind) f...  5.67 us
  transfers between devices with their start and end apart: 11, of which 5 were waited for; matrix products, arithmetic and copies ran while one was open for 1% of the time, Pallas kernels for 4%

profile of v1, /device:TPU:0, one launch (start us, length us, event | category | flops | bytes accessed | tf_op | source)
XLA Modules:
  0.0 32.0 jit_solution(17107181598835788586)
XLA Ops:
  0.6 1.3 %gate.1 = (bf16[8,128,128]{2,1,0:T(8,128)(2,1)S(1)}, bf16[8,128,128]{2,1,0:T(8,128)(2,1)S(1)}, bf16[8,128,128]{2,1,0:T(8,128)(2,1)S(1)}, bf16[8,128,128]{2,1,0:T...) custom-call(bf16[8,128,128]{2,1,0:T(8,128)(2,1)} %bitcast.14, ...), custom_call_target="tpu_custom_call" | custom-call | tf_op jit(solution)/shard_map/gate/pallas_call | solution.py:195
  1.9 0.5 %collective-permute-start = (bf16[4,2,128,128]{3,2,1,0:T(8,128)(2,1)S(1)}, bf16[4,2,128,128]{3,2,1,0:T(8,128)(2,1)S(1)}, u32[]{:S(2)}, u32[]{:S(2)}) collective-permute-start(bf16[4,2,128,128]{3,2,1,0:T(8,128)(2,1)S(1)} %get-tuple-element.21), channel_id=1, source_target_pairs={{0,4},{4,0},{8,12},{12,8},{16,20},{20,16},{24,28},{28,24},{1,5},{5... | collective-permute-start | bytes 786440 | tf_op jit(solution)/shard_map/ppermute | solution.py:208
  2.5 1.1 %collective-permute-done = bf16[4,2,128,128]{3,2,1,0:T(8,128)(2,1)S(1)} collective-permute-done((bf16[4,2,128,128]{3,2,1,0:T(8,128)(2,1)S(1)}, bf16[4,2,128,128]{3,2,1,0:T(8,128)(2,1)S(1)}, u32[]{:S(2)}, u32[]{:S(2)}) %collective-permute-start) | collective-permute-done | bytes 262176 | tf_op jit(solution)/shard_map/ppermute | solution.py:208
  3.6 0.0 copy-start.3
  3.7 2.9 %collective-permute-start.1 = (bf16[2,2,128,128]{3,2,1,0:T(8,128)(2,1)S(1)}, bf16[2,2,128,128]{3,2,1,0:T(8,128)(2,1)S(1)}, u32[]{:S(2)}, u32[]{:S(2)}) collective-permute-start(bf16[2,2,128,128]{3,2,1,0:T(8,128)(2,1)S(1)} %pad_maximum_fusion.1), channel_id=1, source_target_pairs={{0,8},{4,12},{8,0},{12,4},{16,24},{20,28},{24,16},{28,20},{1,9},{5... | collective-permute-start | bytes 393224 | tf_op jit(solution)/shard_map/ppermute | solution.py:208
  6.6 0.0 copy-start
  6.6 0.0 copy-start.1
  6.6 1.6 %collective-permute-start.2 = (bf16[2,2,128,128]{3,2,1,0:T(8,128)(2,1)S(1)}, bf16[2,2,128,128]{3,2,1,0:T(8,128)(2,1)S(1)}, u32[]{:S(2)}, u32[]{:S(2)}) collective-permute-start(bf16[2,2,128,128]{3,2,1,0:T(8,128)(2,1)S(1)} %pad_maximum_fusion.2), channel_id=1, source_target_pairs={{0,16},{4,20},{8,24},{12,28},{16,0},{20,4},{24,8},{28,12},{1,17},{... | collective-permute-start | bytes 393224 | tf_op jit(solution)/shard_map/ppermute | solution.py:208
  8.2 0.1 collective-permute-start.3
  8.3 0.0 copy-done.3
  8.3 0.0 copy-done
  8.3 0.0 copy-done.1
  8.3 0.4 %taps.1.refs_4_ = f32[4,128,512]{2,1,0:T(8,128)S(1)} custom-call(bf16[128,1024]{1,0:T(8,128)(2,1)S(1)} %copy-done.3, bf16[256,512]{1,0:T(8,128)(2,1)S(1)} %copy-done.1, bf16[256,512]{1,0:T(8,128)(2,1)S(1)} %copy-done), custom_call_target="tpu_custom_call" | custom-call | tf_op jit(solution)/shard_map/taps/pallas_call | solution.py:195
  8.8 0.0 copy-start.2
  8.8 1.6 %collective-permute-done.1.refs_1_ = bf16[2,2,128,128]{3,2,1,0:T(8,128)(2,1)S(1)} collective-permute-done((bf16[2,2,128,128]{3,2,1,0:T(8,128)(2,1)S(1)}, bf16[2,2,128,128]{3,2,1,0:T(8,128)(2,1)S(1)}, u32[]{:S(2)}, u32[]{:S(2)}) %collective-permute-start.1) | collective-permute-done | bytes 131104 | tf_op jit(solution)/shard_map/ppermute | solution.py:208
  10.4 4.3 %collective-permute-done.2.refs_2_ = bf16[2,2,128,128]{3,2,1,0:T(8,128)(2,1)S(1)} collective-permute-done((bf16[2,2,128,128]{3,2,1,0:T(8,128)(2,1)S(1)}, bf16[2,2,128,128]{3,2,1,0:T(8,128)(2,1)S(1)}, u32[]{:S(2)}, u32[]{:S(2)}) %collective-permute-start.2) | collective-permute-done | bytes 131104 | tf_op jit(solution)/shard_map/ppermute | solution.py:208
  14.7 0.0 collective-permute-done.3.refs_3_
  14.7 0.0 copy-done.2
  14.7 2.0 %sides.1 = (bf16[4,2,128,128]{3,2,1,0:T(8,128)(2,1)S(1)}, bf16[4,2,128,128]{3,2,1,0:T(8,128)(2,1)S(1)}, f32[4,128,512]{2,1,0:T(8,128)S(1)}, f32[4,128,512]{2,1,0:T(8,128)S(1)}) custom-call(bf16[2,2,128,128]{3,2,1,0:T(8,128)(2,1)S(1)} %pad_maximum_fusion.refs_0_, bf16[2,2,128,128]{3,2,1,0:T(8,128)(2,1)S(1)} %collective-permute-done.1.refs_1_, ...), custom_call_target="tpu_custom_call" | custom-call | tf_op jit(solution)/shard_map/sides/pallas_call | solution.py:195
  16.7 0.1 collective-permute-start.4
  16.8 0.8 %lag.1.refs_8_ = bf16[4,128,256]{2,1,0:T(8,128)(2,1)S(1)} custom-call(f32[4,128,512]{2,1,0:T(8,128)S(1)} %get-tuple-element.28.refs_0_, f32[4,128,512]{2,1,0:T(8,128)S(1)} %get-tuple-element.29.refs_1_, bf16[512,256]{1,0:T(8,128)(2,1)S(1)} %copy-done.2, bf16[4,2,128,128]{3,2,1,0:T(8,128)(2,1)S(1)} %get-tuple-element.22.refs_3_), custom_call_target="tpu_custom_call" | custom-call | tf_op jit(solution)/shard_map/lag/pallas_call | solution.py:195
  17.6 3.7 %collective-permute-start.10 = (bf16[128,256]{1,0:T(8,128)(2,1)S(1)}, bf16[128,256]{1,0:T(8,128)(2,1)S(1)}, u32[]{:S(2)}, u32[]{:S(2)}) collective-permute-start(bf16[128,256]{1,0:T(8,128)(2,1)S(1)} %get-tuple-element.35), channel_id=1, source_target_pairs={{0,3},{1,2},{2,1},{3,0},{4,7},{5,6},{6,5},{7,4},{8,11},{9,10},{10,... | collective-permute-start | bytes 196616 | tf_op jit(solution)/shard_map/ppermute | solution.py:208
  21.3 0.0 collective-permute-done.4
  21.3 1.2 %collective-permute-start.5 = (bf16[2,2,128,128]{3,2,1,0:T(8,128)(2,1)S(1)}, bf16[2,2,128,128]{3,2,1,0:T(8,128)(2,1)S(1)}, u32[]{:S(2)}, u32[]{:S(2)}) collective-permute-start(bf16[2,2,128,128]{3,2,1,0:T(8,128)(2,1)S(1)} %pad_maximum_fusion.5), channel_id=1, source_target_pairs={{0,8},{4,12},{8,0},{12,4},{16,24},{20,28},{24,16},{28,20},{1,9},{5... | collective-permute-start | bytes 393224 | tf_op jit(solution)/shard_map/ppermute | solution.py:208
  22.6 1.0 %collective-permute-start.6 = (bf16[2,2,128,128]{3,2,1,0:T(8,128)(2,1)S(1)}, bf16[2,2,128,128]{3,2,1,0:T(8,128)(2,1)S(1)}, u32[]{:S(2)}, u32[]{:S(2)}) collective-permute-start(bf16[2,2,128,128]{3,2,1,0:T(8,128)(2,1)S(1)} %pad_maximum_fusion.6), channel_id=1, source_target_pairs={{0,16},{4,20},{8,24},{12,28},{16,0},{20,4},{24,8},{28,12},{1,17},{... | collective-permute-start | bytes 393224 | tf_op jit(solution)/shard_map/ppermute | solution.py:208
  23.6 1.5 %collective-permute-start.7 = (bf16[2,2,128,128]{3,2,1,0:T(8,128)(2,1)S(1)}, bf16[2,2,128,128]{3,2,1,0:T(8,128)(2,1)S(1)}, u32[]{:S(2)}, u32[]{:S(2)}) collective-permute-start(bf16[2,2,128,128]{3,2,1,0:T(8,128)(2,1)S(1)} %pad_maximum_fusion.7), channel_id=1, source_target_pairs={{0,24},{4,28},{8,16},{12,20},{16,8},{20,12},{24,0},{28,4},{1,25},{... | collective-permute-start | bytes 393224 | tf_op jit(solution)/shard_map/ppermute | solution.py:208
  25.1 0.0 collective-permute-start.9
  25.1 0.0 collective-permute-done.10.refs_11_
  25.1 1.2 %collective-permute-start.8 = (bf16[128,256]{1,0:T(8,128)(2,1)S(1)}, bf16[128,256]{1,0:T(8,128)(2,1)S(1)}, u32[]{:S(2)}, u32[]{:S(2)}) collective-permute-start(bf16[128,256]{1,0:T(8,128)(2,1)S(1)} %get-tuple-element.37), channel_id=1, source_target_pairs={{0,1},{1,0},{2,3},{3,2},{4,5},{5,4},{6,7},{7,6},{8,9},{9,8},{10,11... | collective-permute-start | bytes 196616 | tf_op jit(solution)/shard_map/ppermute | solution.py:208
  26.3 4.0 %collective-permute-done.9.refs_10_ = bf16[128,256]{1,0:T(8,128)(2,1)S(1)} collective-permute-done((bf16[128,256]{1,0:T(8,128)(2,1)S(1)}, bf16[128,256]{1,0:T(8,128)(2,1)S(1)}, u32[]{:S(2)}, u32[]{:S(2)}) %collective-permute-start.9) | collective-permute-done | bytes 65568 | tf_op jit(solution)/shard_map/ppermute | solution.py:208
  30.2 0.0 collective-permute-done.8.refs_9_
  30.2 0.0 collective-permute-done.5.refs_1_
  30.2 0.0 collective-permute-done.6.refs_2_
  30.2 0.5 %collective-permute-done.7.refs_3_ = bf16[2,2,128,128]{3,2,1,0:T(8,128)(2,1)S(1)} collective-permute-done((bf16[2,2,128,128]{3,2,1,0:T(8,128)(2,1)S(1)}, bf16[2,2,128,128]{3,2,1,0:T(8,128)(2,1)S(1)}, u32[]{:S(2)}, u32[]{:S(2)}) %collective-permute-start.7) | collective-permute-done | bytes 131104 | tf_op jit(solution)/shard_map/ppermute | solution.py:208
  30.8 1.2 %grads.1 = (bf16[8,128,128]{2,1,0:T(8,128)(2,1)}, bf16[8,128,128]{2,1,0:T(8,128)(2,1)}, bf16[8,128,128]{2,1,0:T(8,128)(2,1)}, bf16[8,128,128]{2,1,0:T(8,128)(2,1)}, f32[128,256]{1,0:T(8,128)}) custom-call(bf16[2,2,128,128]{3,2,1,0:T(8,128)(2,1)S(1)} %pad_maximum_fusion.4.refs_0_, bf16[2,2,128,128]{3,2,1,0:T(8,128)(2,1)S(1)} %collective-permute-done.5.refs_1_, ...), custom_call_target="tpu_custom_call" | custom-call | tf_op jit(solution)/shard_map/grads/pallas_call | solution.py:195
  (13 shorter events, 0.2 us)
Async XLA Ops:
  1.9 1.7 %collective-permute-start = (bf16[4,2,128,128]{3,2,1,0:T(8,128)(2,1)S(1)}, bf16[4,2,128,128]{3,2,1,0:T(8,128)(2,1)S(1)}, u32[]{:S(2)}, u32[]{:S(2)}) collective-permute-start(bf16[4,2,128,128]{3,2,1,0:T(8,128)(2,1)S(1)} %get-tuple-element.21), channel_id=1, source_target_pairs={{0,4},{4,0},{8,12},{12,8},{16,20},{20,16},{24,28},{28,24},{1,5},{5... | collective-permute-start | bytes 786440 | tf_op jit(solution)/shard_map/ppermute | solution.py:208
  3.6 4.7 %copy-start.3 = (bf16[128,1024]{1,0:T(8,128)(2,1)S(1)}, bf16[128,1024]{1,0:T(8,128)(2,1)}, u32[]{:S(2)}) copy-start(bf16[128,1024]{1,0:T(8,128)(2,1)} %refs_0_.1) | copy-start | bytes 786436
  3.7 6.8 %collective-permute-start.1 = (bf16[2,2,128,128]{3,2,1,0:T(8,128)(2,1)S(1)}, bf16[2,2,128,128]{3,2,1,0:T(8,128)(2,1)S(1)}, u32[]{:S(2)}, u32[]{:S(2)}) collective-permute-start(bf16[2,2,128,128]{3,2,1,0:T(8,128)(2,1)S(1)} %pad_maximum_fusion.1), channel_id=1, source_target_pairs={{0,8},{4,12},{8,0},{12,4},{16,24},{20,28},{24,16},{28,20},{1,9},{5... | collective-permute-start | bytes 393224 | tf_op jit(solution)/shard_map/ppermute | solution.py:208
  6.6 1.7 %copy-start = (bf16[256,512]{1,0:T(8,128)(2,1)S(1)}, bf16[256,512]{1,0:T(8,128)(2,1)}, u32[]{:S(2)}) copy-start(bf16[256,512]{1,0:T(8,128)(2,1)} %constant.7.clone.refs_2_.refs_6_) | copy-start | bytes 786436
  6.6 1.7 %copy-start.1 = (bf16[256,512]{1,0:T(8,128)(2,1)S(1)}, bf16[256,512]{1,0:T(8,128)(2,1)}, u32[]{:S(2)}) copy-start(bf16[256,512]{1,0:T(8,128)(2,1)} %constant.6.clone.refs_1_.refs_5_) | copy-start | bytes 786436
  6.6 8.1 %collective-permute-start.2 = (bf16[2,2,128,128]{3,2,1,0:T(8,128)(2,1)S(1)}, bf16[2,2,128,128]{3,2,1,0:T(8,128)(2,1)S(1)}, u32[]{:S(2)}, u32[]{:S(2)}) collective-permute-start(bf16[2,2,128,128]{3,2,1,0:T(8,128)(2,1)S(1)} %pad_maximum_fusion.2), channel_id=1, source_target_pairs={{0,16},{4,20},{8,24},{12,28},{16,0},{20,4},{24,8},{28,12},{1,17},{... | collective-permute-start | bytes 393224 | tf_op jit(solution)/shard_map/ppermute | solution.py:208
  8.2 6.5 %collective-permute-start.3 = (bf16[2,2,128,128]{3,2,1,0:T(8,128)(2,1)S(1)}, bf16[2,2,128,128]{3,2,1,0:T(8,128)(2,1)S(1)}, u32[]{:S(2)}, u32[]{:S(2)}) collective-permute-start(bf16[2,2,128,128]{3,2,1,0:T(8,128)(2,1)S(1)} %pad_maximum_fusion.3), channel_id=1, source_target_pairs={{0,24},{4,28},{8,16},{12,20},{16,8},{20,12},{24,0},{28,4},{1,25},{... | collective-permute-start | bytes 393224 | tf_op jit(solution)/shard_map/ppermute | solution.py:208
  8.8 6.0 %copy-start.2 = (bf16[512,256]{1,0:T(8,128)(2,1)S(1)}, bf16[512,256]{1,0:T(8,128)(2,1)}, u32[]{:S(2)}) copy-start(bf16[512,256]{1,0:T(8,128)(2,1)} %constant.8.clone.refs_7_.refs_2_) | copy-start | bytes 786436
  16.7 4.6 %collective-permute-start.4 = (bf16[4,2,128,128]{3,2,1,0:T(8,128)(2,1)S(1)}, bf16[4,2,128,128]{3,2,1,0:T(8,128)(2,1)S(1)}, u32[]{:S(2)}, u32[]{:S(2)}) collective-permute-start(bf16[4,2,128,128]{3,2,1,0:T(8,128)(2,1)S(1)} %get-tuple-element.23), channel_id=1, source_target_pairs={{0,4},{4,0},{8,12},{12,8},{16,20},{20,16},{24,28},{28,24},{1,5},{5... | collective-permute-start | bytes 786440 | tf_op jit(solution)/shard_map/ppermute | solution.py:208
  17.6 7.5 %collective-permute-start.10 = (bf16[128,256]{1,0:T(8,128)(2,1)S(1)}, bf16[128,256]{1,0:T(8,128)(2,1)S(1)}, u32[]{:S(2)}, u32[]{:S(2)}) collective-permute-start(bf16[128,256]{1,0:T(8,128)(2,1)S(1)} %get-tuple-element.35), channel_id=1, source_target_pairs={{0,3},{1,2},{2,1},{3,0},{4,7},{5,6},{6,5},{7,4},{8,11},{9,10},{10,... | collective-permute-start | bytes 196616 | tf_op jit(solution)/shard_map/ppermute | solution.py:208
  21.3 8.9 %collective-permute-start.5 = (bf16[2,2,128,128]{3,2,1,0:T(8,128)(2,1)S(1)}, bf16[2,2,128,128]{3,2,1,0:T(8,128)(2,1)S(1)}, u32[]{:S(2)}, u32[]{:S(2)}) collective-permute-start(bf16[2,2,128,128]{3,2,1,0:T(8,128)(2,1)S(1)} %pad_maximum_fusion.5), channel_id=1, source_target_pairs={{0,8},{4,12},{8,0},{12,4},{16,24},{20,28},{24,16},{28,20},{1,9},{5... | collective-permute-start | bytes 393224 | tf_op jit(solution)/shard_map/ppermute | solution.py:208
  22.6 7.7 %collective-permute-start.6 = (bf16[2,2,128,128]{3,2,1,0:T(8,128)(2,1)S(1)}, bf16[2,2,128,128]{3,2,1,0:T(8,128)(2,1)S(1)}, u32[]{:S(2)}, u32[]{:S(2)}) collective-permute-start(bf16[2,2,128,128]{3,2,1,0:T(8,128)(2,1)S(1)} %pad_maximum_fusion.6), channel_id=1, source_target_pairs={{0,16},{4,20},{8,24},{12,28},{16,0},{20,4},{24,8},{28,12},{1,17},{... | collective-permute-start | bytes 393224 | tf_op jit(solution)/shard_map/ppermute | solution.py:208
  23.6 7.2 %collective-permute-start.7 = (bf16[2,2,128,128]{3,2,1,0:T(8,128)(2,1)S(1)}, bf16[2,2,128,128]{3,2,1,0:T(8,128)(2,1)S(1)}, u32[]{:S(2)}, u32[]{:S(2)}) collective-permute-start(bf16[2,2,128,128]{3,2,1,0:T(8,128)(2,1)S(1)} %pad_maximum_fusion.7), channel_id=1, source_target_pairs={{0,24},{4,28},{8,16},{12,20},{16,8},{20,12},{24,0},{28,4},{1,25},{... | collective-permute-start | bytes 393224 | tf_op jit(solution)/shard_map/ppermute | solution.py:208
  25.1 5.2 %collective-permute-start.9 = (bf16[128,256]{1,0:T(8,128)(2,1)S(1)}, bf16[128,256]{1,0:T(8,128)(2,1)S(1)}, u32[]{:S(2)}, u32[]{:S(2)}) collective-permute-start(bf16[128,256]{1,0:T(8,128)(2,1)S(1)} %get-tuple-element.36), channel_id=1, source_target_pairs={{0,2},{1,3},{2,0},{3,1},{4,6},{5,7},{6,4},{7,5},{8,10},{9,11},{10,... | collective-permute-start | bytes 196616 | tf_op jit(solution)/shard_map/ppermute | solution.py:208
  25.1 5.2 %collective-permute-start.8 = (bf16[128,256]{1,0:T(8,128)(2,1)S(1)}, bf16[128,256]{1,0:T(8,128)(2,1)S(1)}, u32[]{:S(2)}, u32[]{:S(2)}) collective-permute-start(bf16[128,256]{1,0:T(8,128)(2,1)S(1)} %get-tuple-element.37), channel_id=1, source_target_pairs={{0,1},{1,0},{2,3},{3,2},{4,5},{5,4},{6,7},{7,6},{8,9},{9,8},{10,11... | collective-permute-start | bytes 196616 | tf_op jit(solution)/shard_map/ppermute | solution.py:208

commit v2 on v1

--- a/solution.py
+++ b/solution.py
@@ -117,7 +117,7 @@
 
 def sides_kernel(*refs):
     count = len(refs) - 9
-    cols_refs, refs = refs[:count], refs[count:]
+    cols_refs, refs = refs[:count][::-1], refs[count:]
     filt_ref, high_ref, low_ref, inv_ref, own_ref, other_ref, mix_ref, pull_ref, prod = refs
     chip, core = place()
     for i, spec_ref in enumerate((mix_ref, pull_ref)):
@@ -139,6 +139,11 @@
             other_ref[k, i] = jnp.where(core == 0, second, first)
 
 
+def reversed_bits(number, size):
+    bits = size.bit_length() - 1
+    return sum((number // 2**i % 2) * 2 ** (bits - 1 - i) for i in range(bits))
+
+
 def lag_kernel(pull_ref, mix_ref, inv_ref, lag_ref, prod):
     width = lag_ref.shape[2]
     slot = lax.axis_index("chan")
@@ -151,18 +156,16 @@
         result = dot(prod[c], inv_ref[...]).astype(jnp.bfloat16)
         for u in range(BLOCK // LANES):
             begin = c * BLOCK + u * LANES
-            lag_ref[slot ^ (begin // width), :, begin % width : begin % width + LANES] = result[:, u * LANES : (u + 1) * LANES]
+            at = reversed_bits(slot ^ (begin // width), lag_ref.shape[0])
+            lag_ref[at, :, begin % width : begin % width + LANES] = result[:, u * LANES : (u + 1) * LANES]
 
 
 def grads_kernel(count, *refs):
-    rows_refs, (query_ref, key_ref, value_ref, upstream_ref) = refs[:count], refs[count : count + 4]
-    lag_ref, got_refs = refs[count + 4], refs[count + 5 : -9]
+    rows_refs, (query_ref, key_ref, value_ref, upstream_ref) = refs[:count][::-1], refs[count : count + 4]
+    kept_ref, got_ref = refs[count + 4 : count + 6]
     outs, filter_out, (held, sems, sums, sum_sem) = refs[-9:-5], refs[-5], refs[-4:]
     chip, core = place()
-    total_lag = lag_ref[0].astype(jnp.float32)
-    for got in got_refs:
-        total_lag = total_lag + got[...].astype(jnp.float32)
-    sums[...] = total_lag
+    sums[...] = kept_ref[0].astype(jnp.float32) + got_ref[0].astype(jnp.float32)
     copies = [pltpu.make_async_copy(sums, filter_out, sum_sem)]
     copies[0].start()
     for k in range(count):
@@ -211,7 +214,19 @@
 def exchange(own, other):
     got = swap(other, "seq", 1)
     parts = [jnp.stack([own[k], got[k]]) for k in range(own.shape[0])]
-    return [parts[0]] + [swap(parts[k], "seq", 2 * k) for k in range(1, len(parts))]
+    moved = [swap(parts[k], "seq", 2 * k) for k in reversed(range(1, len(parts)))]
+    return moved + [parts[0]], got
+
+
+def scatter_sum(pieces):
+    size, step = pieces.shape[0], 1
+    while True:
+        kept, sent = pieces[: size // 2], pieces[size // 2 :].astype(jnp.bfloat16)
+        got = swap(sent, "chan", step)
+        if size == 2:
+            return kept, got
+        pieces = kept.astype(jnp.float32) + got.astype(jnp.float32)
+        size, step = size // 2, step * 2
 
 
 def on_device(query, key, value, upstream, taps):
@@ -232,7 +247,7 @@
         "gate",
         HBM,
     )
-    cols = exchange(own, other)
+    cols, _ = exchange(own, other)
     (filt,) = call(taps_kernel, (taps, high, low), (wave,), [], "taps")
     own, other, mix_wave, pull_wave = call(
         sides_kernel,
@@ -241,15 +256,16 @@
         [pltpu.VMEM((2, count, chans, 2 * BLOCK), jnp.bfloat16)],
         "sides",
     )
-    rows = exchange(own, other)
+    rows, swapped = exchange(own, other)
     pieces = ((chan, chans, length // chan), jnp.bfloat16)
     prod = pltpu.VMEM((count, chans, 2 * BLOCK), jnp.bfloat16)
     (lag,) = call(lag_kernel, (pull_wave, mix_wave, inverse), (pieces,), [prod], "lag", after=(own,))
-    got = [swap(lag[k], "chan", k) for k in range(1, chan)]
+    lag, _ = lax.optimization_barrier((lag, swapped))
+    kept, got = scatter_sum(lag)
     sums = ((chans, length // chan), jnp.float32)
     *outs, filter_grad = call(
         functools.partial(grads_kernel, count),
-        (*rows, query, key, value, upstream, lag, *got),
+        (*rows, query, key, value, upstream, kept, got),
         (whole,) * 4 + (sums,),
         [
             pltpu.VMEM((4, seq, chans, positions), jnp.bfloat16),

time: 32.1 us -> 30.3 us (0.944)
  waiting for transfers between devices: 11.6 us -> 10 us
  starting transfers between devices: 13.7 us -> 13.2 us
    ppermute x11 -> x10, waiting for transfers between devices: 11.6 us -> 10 us  [swap(): lax.ppermute(array, axis, [(i, i ^ k) for i in range(lax.axis_size(axis))])]
    ppermute x11 -> x10, starting transfers between devices: 13.7 us -> 13.2 us  [swap(): lax.ppermute(array, axis, [(i, i ^ k) for i in range(lax.axis_size(axis))])]
  transfers between devices with their start and end apart: 11 -> 10, of which waited for: 5 -> 9; matrix products, arithmetic and copies ran while one was open for 1% -> 1% of each run, Pallas kernels for 4% -> 4%
where the time goes in v2:
time: 30.3 us; the launch traced here: 30.2 us
  starting transfers between devices  13.2 us (44%)
  waiting for transfers between devices  10 us (33%)
  Pallas kernels  5.67 us (19%)
  between operations  0.77 us (3%)
  local copies, waits for them, and re-layouts  0.37 us (1%)
    ppermute x10, starting transfers between devices, swap(): lax.ppermute(array, axis, [(i, i ^ k) for i in range(lax.axis_size(axis))])  13.2 us
    ppermute x10, waiting for transfers between devices, swap(): lax.ppermute(array, axis, [(i, i ^ k) for i in range(lax.axis_size(axis))])  10 us
    pallas_call x5, Pallas kernels, call(): pl.pallas_call(body, out_shape=tuple((jax.ShapeDtypeStruct(shape, kind) f...  5.67 us
  transfers between devices with their start and end apart: 10, of which 9 were waited for; matrix products, arithmetic and copies ran while one was open for 1% of the time, Pallas kernels for 4%

profile of v2, /device:TPU:0, one launch (start us, length us, event | category | flops | bytes accessed | tf_op | source)
XLA Modules:
  0.0 30.2 jit_solution(6135312640489375331)
XLA Ops:
  0.6 1.3 %gate.1 = (bf16[8,128,128]{2,1,0:T(8,128)(2,1)S(1)}, bf16[8,128,128]{2,1,0:T(8,128)(2,1)S(1)}, bf16[8,128,128]{2,1,0:T(8,128)(2,1)S(1)}, bf16[8,128,128]{2,1,0:T...) custom-call(bf16[8,128,128]{2,1,0:T(8,128)(2,1)} %bitcast.8, ...), custom_call_target="tpu_custom_call" | custom-call | tf_op jit(solution)/shard_map/gate/pallas_call | solution.py:198
  1.9 0.5 %collective-permute-start = (bf16[4,2,128,128]{3,2,1,0:T(8,128)(2,1)S(1)}, bf16[4,2,128,128]{3,2,1,0:T(8,128)(2,1)S(1)}, u32[]{:S(2)}, u32[]{:S(2)}) collective-permute-start(bf16[4,2,128,128]{3,2,1,0:T(8,128)(2,1)S(1)} %get-tuple-element.22), channel_id=1, source_target_pairs={{0,4},{4,0},{8,12},{12,8},{16,20},{20,16},{24,28},{28,24},{1,5},{5... | collective-permute-start | bytes 786440 | tf_op jit(solution)/shard_map/ppermute | solution.py:211
  2.5 1.1 %collective-permute-done = bf16[4,2,128,128]{3,2,1,0:T(8,128)(2,1)S(1)} collective-permute-done((bf16[4,2,128,128]{3,2,1,0:T(8,128)(2,1)S(1)}, bf16[4,2,128,128]{3,2,1,0:T(8,128)(2,1)S(1)}, u32[]{:S(2)}, u32[]{:S(2)}) %collective-permute-start) | collective-permute-done | bytes 262176 | tf_op jit(solution)/shard_map/ppermute | solution.py:211
  3.6 0.0 copy-start.3
  3.7 3.9 %collective-permute-start.1 = (bf16[2,2,128,128]{3,2,1,0:T(8,128)(2,1)S(1)}, bf16[2,2,128,128]{3,2,1,0:T(8,128)(2,1)S(1)}, u32[]{:S(2)}, u32[]{:S(2)}) collective-permute-start(bf16[2,2,128,128]{3,2,1,0:T(8,128)(2,1)S(1)} %pad_maximum_fusion), channel_id=1, source_target_pairs={{0,24},{4,28},{8,16},{12,20},{16,8},{20,12},{24,0},{28,4},{1,25},{... | collective-permute-start | bytes 393224 | tf_op jit(solution)/shard_map/ppermute | solution.py:211
  7.5 0.0 copy-start
  7.5 0.0 copy-start.1
  7.6 0.6 %collective-permute-start.2 = (bf16[2,2,128,128]{3,2,1,0:T(8,128)(2,1)S(1)}, bf16[2,2,128,128]{3,2,1,0:T(8,128)(2,1)S(1)}, u32[]{:S(2)}, u32[]{:S(2)}) collective-permute-start(bf16[2,2,128,128]{3,2,1,0:T(8,128)(2,1)S(1)} %pad_maximum_fusion.1), channel_id=1, source_target_pairs={{0,16},{4,20},{8,24},{12,28},{16,0},{20,4},{24,8},{28,12},{1,17},{... | collective-permute-start | bytes 393224 | tf_op jit(solution)/shard_map/ppermute | solution.py:211
  8.2 0.2 collective-permute-start.3
  8.3 0.0 copy-done.3
  8.3 0.2 copy-done
  8.5 0.1 copy-done.1
  8.6 0.4 %taps.1.refs_4_ = f32[4,128,512]{2,1,0:T(8,128)S(1)} custom-call(bf16[128,1024]{1,0:T(8,128)(2,1)S(1)} %copy-done.3, bf16[256,512]{1,0:T(8,128)(2,1)S(1)} %copy-done.1, bf16[256,512]{1,0:T(8,128)(2,1)S(1)} %copy-done), custom_call_target="tpu_custom_call" | custom-call | tf_op jit(solution)/shard_map/taps/pallas_call | solution.py:198
  9.0 0.0 copy-start.2
  9.0 2.4 %collective-permute-done.1.refs_0_ = bf16[2,2,128,128]{3,2,1,0:T(8,128)(2,1)S(1)} collective-permute-done((bf16[2,2,128,128]{3,2,1,0:T(8,128)(2,1)S(1)}, bf16[2,2,128,128]{3,2,1,0:T(8,128)(2,1)S(1)}, u32[]{:S(2)}, u32[]{:S(2)}) %collective-permute-start.1) | collective-permute-done | bytes 131104 | tf_op jit(solution)/shard_map/ppermute | solution.py:211
  11.4 2.7 %collective-permute-done.2.refs_1_ = bf16[2,2,128,128]{3,2,1,0:T(8,128)(2,1)S(1)} collective-permute-done((bf16[2,2,128,128]{3,2,1,0:T(8,128)(2,1)S(1)}, bf16[2,2,128,128]{3,2,1,0:T(8,128)(2,1)S(1)}, u32[]{:S(2)}, u32[]{:S(2)}) %collective-permute-start.2) | collective-permute-done | bytes 131104 | tf_op jit(solution)/shard_map/ppermute | solution.py:211
  14.1 0.3 collective-permute-done.3.refs_2_
  14.4 0.0 copy-done.2
  14.4 2.0 %sides.1 = (bf16[4,2,128,128]{3,2,1,0:T(8,128)(2,1)S(1)}, bf16[4,2,128,128]{3,2,1,0:T(8,128)(2,1)S(1)}, f32[4,128,512]{2,1,0:T(8,128)S(1)}, f32[4,128,512]{2,1,0:T(8,128)S(1)}) custom-call(bf16[2,2,128,128]{3,2,1,0:T(8,128)(2,1)S(1)} %collective-permute-done.1.refs_0_, bf16[2,2,128,128]{3,2,1,0:T(8,128)(2,1)S(1)} %collective-permute-done.2.refs_1_, ...), custom_call_target="tpu_custom_call" | custom-call | tf_op jit(solution)/shard_map/sides/pallas_call | solution.py:198
  16.4 0.1 collective-permute-start.4
  16.5 0.8 %lag.1 = bf16[4,128,256]{2,1,0:T(8,128)(2,1)S(1)} custom-call(f32[4,128,512]{2,1,0:T(8,128)S(1)} %get-tuple-element.29.refs_0_, f32[4,128,512]{2,1,0:T(8,128)S(1)} %get-tuple-element.30.refs_1_, bf16[512,256]{1,0:T(8,128)(2,1)S(1)} %copy-done.2, bf16[4,2,128,128]{3,2,1,0:T(8,128)(2,1)S(1)} %get-tuple-element.23.refs_3_), custom_call_target="tpu_custom_call" | custom-call | tf_op jit(solution)/shard_map/lag/pallas_call | solution.py:198
  17.3 0.7 %collective-permute-done.4 = bf16[4,2,128,128]{3,2,1,0:T(8,128)(2,1)S(1)} collective-permute-done((bf16[4,2,128,128]{3,2,1,0:T(8,128)(2,1)S(1)}, bf16[4,2,128,128]{3,2,1,0:T(8,128)(2,1)S(1)}, u32[]{:S(2)}, u32[]{:S(2)}) %collective-permute-start.4) | collective-permute-done | bytes 262176 | tf_op jit(solution)/shard_map/ppermute | solution.py:211
  18.0 1.6 %collective-permute-start.8 = (bf16[2,128,256]{2,1,0:T(8,128)(2,1)S(1)}, bf16[2,128,256]{2,1,0:T(8,128)(2,1)S(1)}, u32[]{:S(2)}, u32[]{:S(2)}) collective-permute-start(bf16[2,128,256]{2,1,0:T(8,128)(2,1)S(1)} %slice.78), channel_id=1, source_target_pairs={{0,1},{1,0},{2,3},{3,2},{4,5},{5,4},{6,7},{7,6},{8,9},{9,8},{10,11... | collective-permute-start | bytes 393224 | tf_op jit(solution)/shard_map/ppermute | solution.py:211
  19.7 1.8 %collective-permute-start.5 = (bf16[2,2,128,128]{3,2,1,0:T(8,128)(2,1)S(1)}, bf16[2,2,128,128]{3,2,1,0:T(8,128)(2,1)S(1)}, u32[]{:S(2)}, u32[]{:S(2)}) collective-permute-start(bf16[2,2,128,128]{3,2,1,0:T(8,128)(2,1)S(1)} %pad_maximum_fusion.4), channel_id=1, source_target_pairs={{0,24},{4,28},{8,16},{12,20},{16,8},{20,12},{24,0},{28,4},{1,25},{... | collective-permute-start | bytes 393224 | tf_op jit(solution)/shard_map/ppermute | solution.py:211
  21.5 1.3 %collective-permute-start.6 = (bf16[2,2,128,128]{3,2,1,0:T(8,128)(2,1)S(1)}, bf16[2,2,128,128]{3,2,1,0:T(8,128)(2,1)S(1)}, u32[]{:S(2)}, u32[]{:S(2)}) collective-permute-start(bf16[2,2,128,128]{3,2,1,0:T(8,128)(2,1)S(1)} %pad_maximum_fusion.5), channel_id=1, source_target_pairs={{0,16},{4,20},{8,24},{12,28},{16,0},{20,4},{24,8},{28,12},{1,17},{... | collective-permute-start | bytes 393224 | tf_op jit(solution)/shard_map/ppermute | solution.py:211
  22.9 0.6 %collective-permute-start.7 = (bf16[2,2,128,128]{3,2,1,0:T(8,128)(2,1)S(1)}, bf16[2,2,128,128]{3,2,1,0:T(8,128)(2,1)S(1)}, u32[]{:S(2)}, u32[]{:S(2)}) collective-permute-start(bf16[2,2,128,128]{3,2,1,0:T(8,128)(2,1)S(1)} %pad_maximum_fusion.6), channel_id=1, source_target_pairs={{0,8},{4,12},{8,0},{12,4},{16,24},{20,28},{24,16},{28,20},{1,9},{5... | collective-permute-start | bytes 393224 | tf_op jit(solution)/shard_map/ppermute | solution.py:211
  23.4 0.2 collective-permute-done.8
  23.7 2.7 %collective-permute-start.9 = (bf16[1,128,256]{2,1,0:T(8,128)(2,1)S(1)}, bf16[1,128,256]{2,1,0:T(8,128)(2,1)S(1)}, u32[]{:S(2)}, u32[]{:S(2)}) collective-permute-start(bf16[1,128,256]{2,1,0:T(8,128)(2,1)S(1)} %slice.93), channel_id=1, source_target_pairs={{0,2},{1,3},{2,0},{3,1},{4,6},{5,7},{6,4},{7,5},{8,10},{9,11},{10,... | collective-permute-start | bytes 196616 | tf_op jit(solution)/shard_map/ppermute | solution.py:211
  26.4 0.5 %collective-permute-done.5.refs_0_ = bf16[2,2,128,128]{3,2,1,0:T(8,128)(2,1)S(1)} collective-permute-done((bf16[2,2,128,128]{3,2,1,0:T(8,128)(2,1)S(1)}, bf16[2,2,128,128]{3,2,1,0:T(8,128)(2,1)S(1)}, u32[]{:S(2)}, u32[]{:S(2)}) %collective-permute-start.5) | collective-permute-done | bytes 131104 | tf_op jit(solution)/shard_map/ppermute | solution.py:211
  26.8 1.9 %collective-permute-done.6.refs_1_ = bf16[2,2,128,128]{3,2,1,0:T(8,128)(2,1)S(1)} collective-permute-done((bf16[2,2,128,128]{3,2,1,0:T(8,128)(2,1)S(1)}, bf16[2,2,128,128]{3,2,1,0:T(8,128)(2,1)S(1)}, u32[]{:S(2)}, u32[]{:S(2)}) %collective-permute-start.6) | collective-permute-done | bytes 131104 | tf_op jit(solution)/shard_map/ppermute | solution.py:211
  28.7 0.0 collective-permute-done.7.refs_2_
  28.7 0.2 collective-permute-done.9.refs_9_
  29.0 1.2 %grads.1 = (bf16[8,128,128]{2,1,0:T(8,128)(2,1)}, bf16[8,128,128]{2,1,0:T(8,128)(2,1)}, bf16[8,128,128]{2,1,0:T(8,128)(2,1)}, bf16[8,128,128]{2,1,0:T(8,128)(2,1)}, f32[128,256]{1,0:T(8,128)}) custom-call(bf16[2,2,128,128]{3,2,1,0:T(8,128)(2,1)S(1)} %collective-permute-done.5.refs_0_, bf16[2,2,128,128]{3,2,1,0:T(8,128)(2,1)S(1)} %collective-permute-done.6.refs_1_, ...), custom_call_target="tpu_custom_call" | custom-call | tf_op jit(solution)/shard_map/grads/pallas_call | solution.py:198
  (16 shorter events, 0.2 us)
Async XLA Ops:
  1.9 1.7 %collective-permute-start = (bf16[4,2,128,128]{3,2,1,0:T(8,128)(2,1)S(1)}, bf16[4,2,128,128]{3,2,1,0:T(8,128)(2,1)S(1)}, u32[]{:S(2)}, u32[]{:S(2)}) collective-permute-start(bf16[4,2,128,128]{3,2,1,0:T(8,128)(2,1)S(1)} %get-tuple-element.22), channel_id=1, source_target_pairs={{0,4},{4,0},{8,12},{12,8},{16,20},{20,16},{24,28},{28,24},{1,5},{5... | collective-permute-start | bytes 786440 | tf_op jit(solution)/shard_map/ppermute | solution.py:211
  3.6 4.7 %copy-start.3 = (bf16[128,1024]{1,0:T(8,128)(2,1)S(1)}, bf16[128,1024]{1,0:T(8,128)(2,1)}, u32[]{:S(2)}) copy-start(bf16[128,1024]{1,0:T(8,128)(2,1)} %refs_0_.1) | copy-start | bytes 786436
  3.7 7.8 %collective-permute-start.1 = (bf16[2,2,128,128]{3,2,1,0:T(8,128)(2,1)S(1)}, bf16[2,2,128,128]{3,2,1,0:T(8,128)(2,1)S(1)}, u32[]{:S(2)}, u32[]{:S(2)}) collective-permute-start(bf16[2,2,128,128]{3,2,1,0:T(8,128)(2,1)S(1)} %pad_maximum_fusion), channel_id=1, source_target_pairs={{0,24},{4,28},{8,16},{12,20},{16,8},{20,12},{24,0},{28,4},{1,25},{... | collective-permute-start | bytes 393224 | tf_op jit(solution)/shard_map/ppermute | solution.py:211
  7.5 0.9 %copy-start = (bf16[256,512]{1,0:T(8,128)(2,1)S(1)}, bf16[256,512]{1,0:T(8,128)(2,1)}, u32[]{:S(2)}) copy-start(bf16[256,512]{1,0:T(8,128)(2,1)} %constant.7.clone.refs_2_.refs_6_) | copy-start | bytes 786436
  7.5 1.0 %copy-start.1 = (bf16[256,512]{1,0:T(8,128)(2,1)S(1)}, bf16[256,512]{1,0:T(8,128)(2,1)}, u32[]{:S(2)}) copy-start(bf16[256,512]{1,0:T(8,128)(2,1)} %constant.6.clone.refs_1_.refs_5_) | copy-start | bytes 786436
  7.6 6.6 %collective-permute-start.2 = (bf16[2,2,128,128]{3,2,1,0:T(8,128)(2,1)S(1)}, bf16[2,2,128,128]{3,2,1,0:T(8,128)(2,1)S(1)}, u32[]{:S(2)}, u32[]{:S(2)}) collective-permute-start(bf16[2,2,128,128]{3,2,1,0:T(8,128)(2,1)S(1)} %pad_maximum_fusion.1), channel_id=1, source_target_pairs={{0,16},{4,20},{8,24},{12,28},{16,0},{20,4},{24,8},{28,12},{1,17},{... | collective-permute-start | bytes 393224 | tf_op jit(solution)/shard_map/ppermute | solution.py:211
  8.2 6.3 %collective-permute-start.3 = (bf16[2,2,128,128]{3,2,1,0:T(8,128)(2,1)S(1)}, bf16[2,2,128,128]{3,2,1,0:T(8,128)(2,1)S(1)}, u32[]{:S(2)}, u32[]{:S(2)}) collective-permute-start(bf16[2,2,128,128]{3,2,1,0:T(8,128)(2,1)S(1)} %pad_maximum_fusion.2), channel_id=1, source_target_pairs={{0,8},{4,12},{8,0},{12,4},{16,24},{20,28},{24,16},{28,20},{1,9},{5... | collective-permute-start | bytes 393224 | tf_op jit(solution)/shard_map/ppermute | solution.py:211
  9.0 5.4 %copy-start.2 = (bf16[512,256]{1,0:T(8,128)(2,1)S(1)}, bf16[512,256]{1,0:T(8,128)(2,1)}, u32[]{:S(2)}) copy-start(bf16[512,256]{1,0:T(8,128)(2,1)} %constant.8.clone.refs_7_.refs_2_) | copy-start | bytes 786436
  16.4 1.6 %collective-permute-start.4 = (bf16[4,2,128,128]{3,2,1,0:T(8,128)(2,1)S(1)}, bf16[4,2,128,128]{3,2,1,0:T(8,128)(2,1)S(1)}, u32[]{:S(2)}, u32[]{:S(2)}) collective-permute-start(bf16[4,2,128,128]{3,2,1,0:T(8,128)(2,1)S(1)} %get-tuple-element.24), channel_id=1, source_target_pairs={{0,4},{4,0},{8,12},{12,8},{16,20},{20,16},{24,28},{28,24},{1,5},{5... | collective-permute-start | bytes 786440 | tf_op jit(solution)/shard_map/ppermute | solution.py:211
  18.0 5.6 %collective-permute-start.8 = (bf16[2,128,256]{2,1,0:T(8,128)(2,1)S(1)}, bf16[2,128,256]{2,1,0:T(8,128)(2,1)S(1)}, u32[]{:S(2)}, u32[]{:S(2)}) collective-permute-start(bf16[2,128,256]{2,1,0:T(8,128)(2,1)S(1)} %slice.78), channel_id=1, source_target_pairs={{0,1},{1,0},{2,3},{3,2},{4,5},{5,4},{6,7},{7,6},{8,9},{9,8},{10,11... | collective-permute-start | bytes 393224 | tf_op jit(solution)/shard_map/ppermute | solution.py:211
  19.7 7.1 %collective-permute-start.5 = (bf16[2,2,128,128]{3,2,1,0:T(8,128)(2,1)S(1)}, bf16[2,2,128,128]{3,2,1,0:T(8,128)(2,1)S(1)}, u32[]{:S(2)}, u32[]{:S(2)}) collective-permute-start(bf16[2,2,128,128]{3,2,1,0:T(8,128)(2,1)S(1)} %pad_maximum_fusion.4), channel_id=1, source_target_pairs={{0,24},{4,28},{8,16},{12,20},{16,8},{20,12},{24,0},{28,4},{1,25},{... | collective-permute-start | bytes 393224 | tf_op jit(solution)/shard_map/ppermute | solution.py:211
  21.5 7.2 %collective-permute-start.6 = (bf16[2,2,128,128]{3,2,1,0:T(8,128)(2,1)S(1)}, bf16[2,2,128,128]{3,2,1,0:T(8,128)(2,1)S(1)}, u32[]{:S(2)}, u32[]{:S(2)}) collective-permute-start(bf16[2,2,128,128]{3,2,1,0:T(8,128)(2,1)S(1)} %pad_maximum_fusion.5), channel_id=1, source_target_pairs={{0,16},{4,20},{8,24},{12,28},{16,0},{20,4},{24,8},{28,12},{1,17},{... | collective-permute-start | bytes 393224 | tf_op jit(solution)/shard_map/ppermute | solution.py:211
  22.9 5.9 %collective-permute-start.7 = (bf16[2,2,128,128]{3,2,1,0:T(8,128)(2,1)S(1)}, bf16[2,2,128,128]{3,2,1,0:T(8,128)(2,1)S(1)}, u32[]{:S(2)}, u32[]{:S(2)}) collective-permute-start(bf16[2,2,128,128]{3,2,1,0:T(8,128)(2,1)S(1)} %pad_maximum_fusion.6), channel_id=1, source_target_pairs={{0,8},{4,12},{8,0},{12,4},{16,24},{20,28},{24,16},{28,20},{1,9},{5... | collective-permute-start | bytes 393224 | tf_op jit(solution)/shard_map/ppermute | solution.py:211
  23.7 5.3 %collective-permute-start.9 = (bf16[1,128,256]{2,1,0:T(8,128)(2,1)S(1)}, bf16[1,128,256]{2,1,0:T(8,128)(2,1)S(1)}, u32[]{:S(2)}, u32[]{:S(2)}) collective-permute-start(bf16[1,128,256]{2,1,0:T(8,128)(2,1)S(1)} %slice.93), channel_id=1, source_target_pairs={{0,2},{1,3},{2,0},{3,1},{4,6},{5,7},{6,4},{7,5},{8,10},{9,11},{10,... | collective-permute-start | bytes 196616 | tf_op jit(solution)/shard_map/ppermute | solution.py:211

commit v3 on v2

--- a/solution.py
+++ b/solution.py
@@ -63,7 +63,7 @@
             body(rows, pl.ds(half * LANES, LANES), pl.ds(BLOCK + half * LANES, LANES), sign)
         return carry
 
-    lax.fori_loop(0, chans // tile, step, 0)
+    lax.fori_loop(0, chans // tile, step, 0, unroll=True)
 
 
 def spectra(ref, rows, re, im):
@@ -115,15 +115,53 @@
         filt_ref[a] = forward(taps_ref[:, a * BLOCK : (a + 1) * BLOCK], high_ref, low_ref)
 
 
-def sides_kernel(*refs):
-    count = len(refs) - 9
-    cols_refs, refs = refs[:count][::-1], refs[count:]
-    filt_ref, high_ref, low_ref, inv_ref, own_ref, other_ref, mix_ref, pull_ref, prod = refs
+def far(k):
+    return k.bit_count() > 1
+
+
+def early(count):
+    return [k for k in range(count) if k == 0 or far(k)]
+
+
+def late(count):
+    return [k for k in range(count) if k and not far(k)]
+
+
+def early_pieces(refs, count):
+    size = len(early(count))
+    pieces = [(refs[2 * i], refs[2 * i + 1]) for i in range(size)]
+    pieces[0] = pieces[0][0].at[0], pieces[0][1].at[0]
+    return list(zip(early(count), pieces)), refs[2 * size :]
+
+
+def late_pieces(refs, count):
+    size = len(late(count))
+    return [(k, (refs[i].at[0], refs[i].at[1])) for i, k in enumerate(late(count))], refs[size:]
+
+
+def transform(pair, i, high_ref, low_ref):
+    chip, core = place()
+    mine, theirs = pair[0][i], pair[1][i]
+    halves = [jnp.where(core == 0, mine, theirs), jnp.where(core == 0, theirs, mine)]
+    return forward(jnp.concatenate(halves, axis=1), high_ref, low_ref)
+
+
+def early_kernel(count, *refs):
+    pieces, (high_ref, low_ref, wave_ref) = early_pieces(refs, count)
+    for at, (k, pair) in enumerate(pieces):
+        for i in range(2):
+            wave_ref[at, i] = transform(pair, i, high_ref, low_ref)
+
+
+def sides_kernel(count, *refs):
+    pieces, refs = late_pieces(refs, count)
+    wave_ref, filt_ref, high_ref, low_ref, inv_ref, own_ref, other_ref, mix_ref, pull_ref, prod = refs
     chip, core = place()
     for i, spec_ref in enumerate((mix_ref, pull_ref)):
-        for k in range(count):
-            block = jnp.concatenate([cols_refs[k][core, i], cols_refs[k][1 - core, i]], axis=1)
-            spec_ref[chip ^ k] = forward(block, high_ref, low_ref)
+        for at, k in enumerate(early(count)):
+            spec_ref[chip ^ k] = wave_ref[at, i]
+        for k, pair in pieces:
+            spec_ref[chip ^ k] = transform(pair, i, high_ref, low_ref)
 
     def body(rows, re, im, sign):
         taps = spectra(filt_ref, rows, re, im)
@@ -211,11 +249,16 @@
     return lax.ppermute(array, axis, [(i, i ^ k) for i in range(lax.axis_size(axis))])
 
 
-def exchange(own, other):
+def exchange(own, other, split):
+    count = own.shape[0]
     got = swap(other, "seq", 1)
-    parts = [jnp.stack([own[k], got[k]]) for k in range(own.shape[0])]
-    moved = [swap(parts[k], "seq", 2 * k) for k in reversed(range(1, len(parts)))]
-    return moved + [parts[0]], got
+    if not split:
+        parts = [jnp.stack([own[k], got[k]]) for k in range(count)]
+        return [*(swap(parts[k], "seq", 2 * k) for k in reversed(range(1, count))), parts[0]], got
+    first = [own, got]
+    for k in early(count)[1:]:
+        first += [swap(own[k], "seq", 2 * k), swap(got[k], "seq", 2 * k)]
+    return first, [swap(jnp.stack([own[k], got[k]]), "seq", 2 * k) for k in late(count)]
 
 
 def scatter_sum(pieces):
@@ -247,16 +290,18 @@
         "gate",
         HBM,
     )
-    cols, _ = exchange(own, other)
+    first, rest = exchange(own, other, True)
     (filt,) = call(taps_kernel, (taps, high, low), (wave,), [], "taps")
+    waves = ((len(early(count)), 2, chans, 2 * BLOCK), jnp.float32)
+    (begun,) = call(functools.partial(early_kernel, count), (*first, high, low), (waves,), [], "early", flops=int(2e+09))
     own, other, mix_wave, pull_wave = call(
-        sides_kernel,
-        (*cols, filt, high, low, inverse),
+        functools.partial(sides_kernel, count),
+        (*rest, begun, filt, high, low, inverse),
         (half, half, wave, wave),
         [pltpu.VMEM((2, count, chans, 2 * BLOCK), jnp.bfloat16)],
         "sides",
     )
-    rows, swapped = exchange(own, other)
+    rows, swapped = exchange(own, other, False)
     pieces = ((chan, chans, length // chan), jnp.bfloat16)
     prod = pltpu.VMEM((count, chans, 2 * BLOCK), jnp.bfloat16)
     (lag,) = call(lag_kernel, (pull_wave, mix_wave, inverse), (pieces,), [prod], "lag", after=(own,))

time: 30.3 us -> 30 us (0.990)
  starting transfers between devices: 13.2 us -> 15.8 us
  waiting for transfers between devices: 10 us -> 7.45 us
    ppermute x10 -> x11, starting transfers between devices: 13.2 us -> 15.8 us  [swap(): lax.ppermute(array, axis, [(i, i ^ k) for i in range(lax.axis_size(axis))])]
    ppermute x10 -> x11, waiting for transfers between devices: 10 us -> 7.45 us  [swap(): lax.ppermute(array, axis, [(i, i ^ k) for i in range(lax.axis_size(axis))])]
    pallas_call x5 -> x6, Pallas kernels: 5.67 us -> 5.65 us  [call(): pl.pallas_call(body, out_shape=tuple((jax.ShapeDtypeStruct(shape, kind) f...]
  transfers between devices with their start and end apart: 10 -> 11, of which waited for: 9 -> 8; matrix products, arithmetic and copies ran while one was open for 1% -> 1% of each run, Pallas kernels for 4% -> 5%
where the time goes in v3:
time: 30 us; the launch traced here: 29.9 us
  starting transfers between devices  15.8 us (53%)
  waiting for transfers between devices  7.45 us (25%)
  Pallas kernels  5.65 us (19%)
  between operations  0.8 us (3%)
    ppermute x11, starting transfers between devices, swap(): lax.ppermute(array, axis, [(i, i ^ k) for i in range(lax.axis_size(axis))])  15.8 us
    ppermute x11, waiting for transfers between devices, swap(): lax.ppermute(array, axis, [(i, i ^ k) for i in range(lax.axis_size(axis))])  7.45 us
    pallas_call x6, Pallas kernels, call(): pl.pallas_call(body, out_shape=tuple((jax.ShapeDtypeStruct(shape, kind) f...  5.65 us
  transfers between devices with their start and end apart: 11, of which 8 were waited for; matrix products, arithmetic and copies ran while one was open for 1% of the time, Pallas kernels for 5%

profile of v3, /device:TPU:0, one launch (start us, length us, event | category | flops | bytes accessed | tf_op | source)
XLA Modules:
  0.0 29.9 jit_solution(17333600818197262605)
XLA Ops:
  0.6 0.0 copy-start.1
  0.6 0.0 copy-start.3
  0.7 1.3 %gate.1 = (bf16[8,128,128]{2,1,0:T(8,128)(2,1)S(1)}, bf16[8,128,128]{2,1,0:T(8,128)(2,1)S(1)}, bf16[8,128,128]{2,1,0:T(8,128)(2,1)S(1)}, bf16[8,128,128]{2,1,0:T...) custom-call(bf16[8,128,128]{2,1,0:T(8,128)(2,1)} %bitcast.12, ...), custom_call_target="tpu_custom_call" | custom-call | tf_op jit(solution)/shard_map/gate/pallas_call | solution.py:236
  2.0 0.0 copy-start
  2.0 0.5 %collective-permute-start = (bf16[4,2,128,128]{3,2,1,0:T(8,128)(2,1)S(1)}, bf16[4,2,128,128]{3,2,1,0:T(8,128)(2,1)S(1)}, u32[]{:S(2)}, u32[]{:S(2)}) collective-permute-start(bf16[4,2,128,128]{3,2,1,0:T(8,128)(2,1)S(1)} %get-tuple-element.22), channel_id=1, source_target_pairs={{0,4},{4,0},{8,12},{12,8},{16,20},{20,16},{24,28},{28,24},{1,5},{5... | collective-permute-start | bytes 786440 | tf_op jit(solution)/shard_map/ppermute | solution.py:249
  2.5 3.5 %collective-permute-start.3 = (bf16[2,128,128]{2,1,0:T(8,128)(2,1)S(1)}, bf16[2,128,128]{2,1,0:T(8,128)(2,1)S(1)}, u32[]{:S(2)}, u32[]{:S(2)}) collective-permute-start(bf16[2,128,128]{2,1,0:T(8,128)(2,1)S(1)} %get-tuple-element.48), channel_id=1, source_target_pairs={{0,24},{4,28},{8,16},{12,20},{16,8},{20,12},{24,0},{28,4},{1,25},{... | collective-permute-start | bytes 196616 | tf_op jit(solution)/shard_map/ppermute | solution.py:249
  6.1 0.0 copy-done.1
  6.1 0.0 copy-done.3
  6.1 0.0 copy-done
  6.1 0.4 %taps.1.refs_3_ = f32[4,128,512]{2,1,0:T(8,128)S(1)} custom-call(bf16[128,1024]{1,0:T(8,128)(2,1)S(1)} %copy-done.3, bf16[256,512]{1,0:T(8,128)(2,1)S(1)} %copy-done.1, bf16[256,512]{1,0:T(8,128)(2,1)S(1)} %copy-done), custom_call_target="tpu_custom_call" | custom-call | tf_op jit(solution)/shard_map/taps/pallas_call | solution.py:236
  6.5 0.0 collective-permute-done.refs_1_
  6.6 1.0 %collective-permute-start.4 = (bf16[2,128,128]{2,1,0:T(8,128)(2,1)S(1)}, bf16[2,128,128]{2,1,0:T(8,128)(2,1)S(1)}, u32[]{:S(2)}, u32[]{:S(2)}) collective-permute-start(bf16[2,128,128]{2,1,0:T(8,128)(2,1)S(1)} %get-tuple-element.45), channel_id=1, source_target_pairs={{0,24},{4,28},{8,16},{12,20},{16,8},{20,12},{24,0},{28,4},{1,25},{... | collective-permute-start | bytes 196616 | tf_op jit(solution)/shard_map/ppermute | solution.py:249
  7.6 1.1 %collective-permute-start.1 = (bf16[2,2,128,128]{3,2,1,0:T(8,128)(2,1)S(1)}, bf16[2,2,128,128]{3,2,1,0:T(8,128)(2,1)S(1)}, u32[]{:S(2)}, u32[]{:S(2)}) collective-permute-start(bf16[2,2,128,128]{3,2,1,0:T(8,128)(2,1)S(1)} %pad_maximum_fusion), channel_id=1, source_target_pairs={{0,8},{4,12},{8,0},{12,4},{16,24},{20,28},{24,16},{28,20},{1,9},{5... | collective-permute-start | bytes 393224 | tf_op jit(solution)/shard_map/ppermute | solution.py:249
  8.7 0.0 copy-start.2
  8.7 1.6 %collective-permute-start.2 = (bf16[2,2,128,128]{3,2,1,0:T(8,128)(2,1)S(1)}, bf16[2,2,128,128]{3,2,1,0:T(8,128)(2,1)S(1)}, u32[]{:S(2)}, u32[]{:S(2)}) collective-permute-start(bf16[2,2,128,128]{3,2,1,0:T(8,128)(2,1)S(1)} %pad_maximum_fusion.1), channel_id=1, source_target_pairs={{0,16},{4,20},{8,24},{12,28},{16,0},{20,4},{24,8},{28,12},{1,17},{... | collective-permute-start | bytes 393224 | tf_op jit(solution)/shard_map/ppermute | solution.py:249
  10.3 0.0 collective-permute-done.3.refs_2_
  10.3 2.2 %collective-permute-done.4.refs_3_ = bf16[2,128,128]{2,1,0:T(8,128)(2,1)S(1)} collective-permute-done((bf16[2,128,128]{2,1,0:T(8,128)(2,1)S(1)}, bf16[2,128,128]{2,1,0:T(8,128)(2,1)S(1)}, u32[]{:S(2)}, u32[]{:S(2)}) %collective-permute-start.4) | collective-permute-done | bytes 65568 | tf_op jit(solution)/shard_map/ppermute | solution.py:249
  12.4 0.4 %early.1.refs_2_ = f32[2,2,128,512]{3,2,1,0:T(8,128)S(1)} custom-call(bf16[4,2,128,128]{3,2,1,0:T(8,128)(2,1)S(1)} %get-tuple-element.21.refs_0_, bf16[4,2,128,128]{3,2,1,0:T(8,128)(2,1)S(1)} %collective-permute-done.refs_1_, bf16[2,128,128]{2,1,0:T(8,128)(2,1)S(1)} %collective-permute-done.3.refs_2_, ...), custom_call_target="tpu_custom_call" | custom-call | flops 2000000000 | tf_op jit(solution)/shard_map/early/pallas_call | solution.py:236
  12.9 0.7 %collective-permute-done.1.refs_0_ = bf16[2,2,128,128]{3,2,1,0:T(8,128)(2,1)S(1)} collective-permute-done((bf16[2,2,128,128]{3,2,1,0:T(8,128)(2,1)S(1)}, bf16[2,2,128,128]{3,2,1,0:T(8,128)(2,1)S(1)}, u32[]{:S(2)}, u32[]{:S(2)}) %collective-permute-start.1) | collective-permute-done | bytes 131104 | tf_op jit(solution)/shard_map/ppermute | solution.py:249
  13.6 0.9 %collective-permute-done.2.refs_1_ = bf16[2,2,128,128]{3,2,1,0:T(8,128)(2,1)S(1)} collective-permute-done((bf16[2,2,128,128]{3,2,1,0:T(8,128)(2,1)S(1)}, bf16[2,2,128,128]{3,2,1,0:T(8,128)(2,1)S(1)}, u32[]{:S(2)}, u32[]{:S(2)}) %collective-permute-start.2) | collective-permute-done | bytes 131104 | tf_op jit(solution)/shard_map/ppermute | solution.py:249
  14.5 0.0 copy-done.2
  14.5 1.6 %sides.1 = (bf16[4,2,128,128]{3,2,1,0:T(8,128)(2,1)S(1)}, bf16[4,2,128,128]{3,2,1,0:T(8,128)(2,1)S(1)}, f32[4,128,512]{2,1,0:T(8,128)S(1)}, f32[4,128,512]{2,1,0:T(8,128)S(1)}) custom-call(bf16[2,2,128,128]{3,2,1,0:T(8,128)(2,1)S(1)} %collective-permute-done.1.refs_0_, bf16[2,2,128,128]{3,2,1,0:T(8,128)(2,1)S(1)} %collective-permute-done.2.refs_1_, ...), custom_call_target="tpu_custom_call" | custom-call | tf_op jit(solution)/shard_map/sides/pallas_call | solution.py:236
  16.1 0.1 collective-permute-start.5
  16.2 0.6 %lag.1 = bf16[4,128,256]{2,1,0:T(8,128)(2,1)S(1)} custom-call(f32[4,128,512]{2,1,0:T(8,128)S(1)} %get-tuple-element.29.refs_0_, f32[4,128,512]{2,1,0:T(8,128)S(1)} %get-tuple-element.30.refs_1_, bf16[512,256]{1,0:T(8,128)(2,1)S(1)} %copy-done.2, bf16[4,2,128,128]{3,2,1,0:T(8,128)(2,1)S(1)} %get-tuple-element.23.refs_3_), custom_call_target="tpu_custom_call" | custom-call | tf_op jit(solution)/shard_map/lag/pallas_call | solution.py:236
  16.9 0.8 %collective-permute-done.5 = bf16[4,2,128,128]{3,2,1,0:T(8,128)(2,1)S(1)} collective-permute-done((bf16[4,2,128,128]{3,2,1,0:T(8,128)(2,1)S(1)}, bf16[4,2,128,128]{3,2,1,0:T(8,128)(2,1)S(1)}, u32[]{:S(2)}, u32[]{:S(2)}) %collective-permute-start.5) | collective-permute-done | bytes 262176 | tf_op jit(solution)/shard_map/ppermute | solution.py:249
  17.8 1.6 %collective-permute-start.9 = (bf16[2,128,256]{2,1,0:T(8,128)(2,1)S(1)}, bf16[2,128,256]{2,1,0:T(8,128)(2,1)S(1)}, u32[]{:S(2)}, u32[]{:S(2)}) collective-permute-start(bf16[2,128,256]{2,1,0:T(8,128)(2,1)S(1)} %slice.70), channel_id=1, source_target_pairs={{0,1},{1,0},{2,3},{3,2},{4,5},{5,4},{6,7},{7,6},{8,9},{9,8},{10,11... | collective-permute-start | bytes 393224 | tf_op jit(solution)/shard_map/ppermute | solution.py:249
  19.4 1.3 %collective-permute-start.6 = (bf16[2,2,128,128]{3,2,1,0:T(8,128)(2,1)S(1)}, bf16[2,2,128,128]{3,2,1,0:T(8,128)(2,1)S(1)}, u32[]{:S(2)}, u32[]{:S(2)}) collective-permute-start(bf16[2,2,128,128]{3,2,1,0:T(8,128)(2,1)S(1)} %pad_maximum_fusion.2), channel_id=1, source_target_pairs={{0,24},{4,28},{8,16},{12,20},{16,8},{20,12},{24,0},{28,4},{1,25},{... | collective-permute-start | bytes 393224 | tf_op jit(solution)/shard_map/ppermute | solution.py:249
  20.7 0.9 %collective-permute-start.7 = (bf16[2,2,128,128]{3,2,1,0:T(8,128)(2,1)S(1)}, bf16[2,2,128,128]{3,2,1,0:T(8,128)(2,1)S(1)}, u32[]{:S(2)}, u32[]{:S(2)}) collective-permute-start(bf16[2,2,128,128]{3,2,1,0:T(8,128)(2,1)S(1)} %pad_maximum_fusion.3), channel_id=1, source_target_pairs={{0,16},{4,20},{8,24},{12,28},{16,0},{20,4},{24,8},{28,12},{1,17},{... | collective-permute-start | bytes 393224 | tf_op jit(solution)/shard_map/ppermute | solution.py:249
  21.6 1.5 %collective-permute-start.8 = (bf16[2,2,128,128]{3,2,1,0:T(8,128)(2,1)S(1)}, bf16[2,2,128,128]{3,2,1,0:T(8,128)(2,1)S(1)}, u32[]{:S(2)}, u32[]{:S(2)}) collective-permute-start(bf16[2,2,128,128]{3,2,1,0:T(8,128)(2,1)S(1)} %pad_maximum_fusion.4), channel_id=1, source_target_pairs={{0,8},{4,12},{8,0},{12,4},{16,24},{20,28},{24,16},{28,20},{1,9},{5... | collective-permute-start | bytes 393224 | tf_op jit(solution)/shard_map/ppermute | solution.py:249
  23.1 0.2 collective-permute-done.9
  23.4 2.6 %collective-permute-start.10 = (bf16[1,128,256]{2,1,0:T(8,128)(2,1)S(1)}, bf16[1,128,256]{2,1,0:T(8,128)(2,1)S(1)}, u32[]{:S(2)}, u32[]{:S(2)}) collective-permute-start(bf16[1,128,256]{2,1,0:T(8,128)(2,1)S(1)} %slice.86), channel_id=1, source_target_pairs={{0,2},{1,3},{2,0},{3,1},{4,6},{5,7},{6,4},{7,5},{8,10},{9,11},{10,... | collective-permute-start | bytes 196616 | tf_op jit(solution)/shard_map/ppermute | solution.py:249
  26.1 0.7 %collective-permute-done.6.refs_0_ = bf16[2,2,128,128]{3,2,1,0:T(8,128)(2,1)S(1)} collective-permute-done((bf16[2,2,128,128]{3,2,1,0:T(8,128)(2,1)S(1)}, bf16[2,2,128,128]{3,2,1,0:T(8,128)(2,1)S(1)}, u32[]{:S(2)}, u32[]{:S(2)}) %collective-permute-start.6) | collective-permute-done | bytes 131104 | tf_op jit(solution)/shard_map/ppermute | solution.py:249
  26.8 1.7 %collective-permute-done.7.refs_1_ = bf16[2,2,128,128]{3,2,1,0:T(8,128)(2,1)S(1)} collective-permute-done((bf16[2,2,128,128]{3,2,1,0:T(8,128)(2,1)S(1)}, bf16[2,2,128,128]{3,2,1,0:T(8,128)(2,1)S(1)}, u32[]{:S(2)}, u32[]{:S(2)}) %collective-permute-start.7) | collective-permute-done | bytes 131104 | tf_op jit(solution)/shard_map/ppermute | solution.py:249
  28.5 0.0 collective-permute-done.8.refs_2_
  28.5 0.2 collective-permute-done.10.refs_9_
  28.7 1.2 %grads.1 = (bf16[8,128,128]{2,1,0:T(8,128)(2,1)}, bf16[8,128,128]{2,1,0:T(8,128)(2,1)}, bf16[8,128,128]{2,1,0:T(8,128)(2,1)}, bf16[8,128,128]{2,1,0:T(8,128)(2,1)}, f32[128,256]{1,0:T(8,128)}) custom-call(bf16[2,2,128,128]{3,2,1,0:T(8,128)(2,1)S(1)} %collective-permute-done.6.refs_0_, bf16[2,2,128,128]{3,2,1,0:T(8,128)(2,1)S(1)} %collective-permute-done.7.refs_1_, ...), custom_call_target="tpu_custom_call" | custom-call | tf_op jit(solution)/shard_map/grads/pallas_call | solution.py:236
  (14 shorter events, 0.2 us)
Async XLA Ops:
  0.6 5.4 %copy-start.1 = (bf16[256,512]{1,0:T(8,128)(2,1)S(1)}, bf16[256,512]{1,0:T(8,128)(2,1)}, u32[]{:S(2)}) copy-start(bf16[256,512]{1,0:T(8,128)(2,1)} %constant.6.clone.refs_4_.refs_1_) | copy-start | bytes 786436
  0.6 5.4 %copy-start.3 = (bf16[128,1024]{1,0:T(8,128)(2,1)S(1)}, bf16[128,1024]{1,0:T(8,128)(2,1)}, u32[]{:S(2)}) copy-start(bf16[128,1024]{1,0:T(8,128)(2,1)} %refs_0_.1) | copy-start | bytes 786436
  2.0 4.1 %copy-start = (bf16[256,512]{1,0:T(8,128)(2,1)S(1)}, bf16[256,512]{1,0:T(8,128)(2,1)}, u32[]{:S(2)}) copy-start(bf16[256,512]{1,0:T(8,128)(2,1)} %constant.7.clone.refs_5_.refs_2_) | copy-start | bytes 786436
  2.0 4.5 %collective-permute-start = (bf16[4,2,128,128]{3,2,1,0:T(8,128)(2,1)S(1)}, bf16[4,2,128,128]{3,2,1,0:T(8,128)(2,1)S(1)}, u32[]{:S(2)}, u32[]{:S(2)}) collective-permute-start(bf16[4,2,128,128]{3,2,1,0:T(8,128)(2,1)S(1)} %get-tuple-element.22), channel_id=1, source_target_pairs={{0,4},{4,0},{8,12},{12,8},{16,20},{20,16},{24,28},{28,24},{1,5},{5... | collective-permute-start | bytes 786440 | tf_op jit(solution)/shard_map/ppermute | solution.py:249
  2.5 7.7 %collective-permute-start.3 = (bf16[2,128,128]{2,1,0:T(8,128)(2,1)S(1)}, bf16[2,128,128]{2,1,0:T(8,128)(2,1)S(1)}, u32[]{:S(2)}, u32[]{:S(2)}) collective-permute-start(bf16[2,128,128]{2,1,0:T(8,128)(2,1)S(1)} %get-tuple-element.48), channel_id=1, source_target_pairs={{0,24},{4,28},{8,16},{12,20},{16,8},{20,12},{24,0},{28,4},{1,25},{... | collective-permute-start | bytes 196616 | tf_op jit(solution)/shard_map/ppermute | solution.py:249
  6.6 5.9 %collective-permute-start.4 = (bf16[2,128,128]{2,1,0:T(8,128)(2,1)S(1)}, bf16[2,128,128]{2,1,0:T(8,128)(2,1)S(1)}, u32[]{:S(2)}, u32[]{:S(2)}) collective-permute-start(bf16[2,128,128]{2,1,0:T(8,128)(2,1)S(1)} %get-tuple-element.45), channel_id=1, source_target_pairs={{0,24},{4,28},{8,16},{12,20},{16,8},{20,12},{24,0},{28,4},{1,25},{... | collective-permute-start | bytes 196616 | tf_op jit(solution)/shard_map/ppermute | solution.py:249
  7.6 6.0 %collective-permute-start.1 = (bf16[2,2,128,128]{3,2,1,0:T(8,128)(2,1)S(1)}, bf16[2,2,128,128]{3,2,1,0:T(8,128)(2,1)S(1)}, u32[]{:S(2)}, u32[]{:S(2)}) collective-permute-start(bf16[2,2,128,128]{3,2,1,0:T(8,128)(2,1)S(1)} %pad_maximum_fusion), channel_id=1, source_target_pairs={{0,8},{4,12},{8,0},{12,4},{16,24},{20,28},{24,16},{28,20},{1,9},{5... | collective-permute-start | bytes 393224 | tf_op jit(solution)/shard_map/ppermute | solution.py:249
  8.7 5.8 %copy-start.2 = (bf16[512,256]{1,0:T(8,128)(2,1)S(1)}, bf16[512,256]{1,0:T(8,128)(2,1)}, u32[]{:S(2)}) copy-start(bf16[512,256]{1,0:T(8,128)(2,1)} %constant.8.clone.refs_6_.refs_2_) | copy-start | bytes 786436
  8.7 5.8 %collective-permute-start.2 = (bf16[2,2,128,128]{3,2,1,0:T(8,128)(2,1)S(1)}, bf16[2,2,128,128]{3,2,1,0:T(8,128)(2,1)S(1)}, u32[]{:S(2)}, u32[]{:S(2)}) collective-permute-start(bf16[2,2,128,128]{3,2,1,0:T(8,128)(2,1)S(1)} %pad_maximum_fusion.1), channel_id=1, source_target_pairs={{0,16},{4,20},{8,24},{12,28},{16,0},{20,4},{24,8},{28,12},{1,17},{... | collective-permute-start | bytes 393224 | tf_op jit(solution)/shard_map/ppermute | solution.py:249
  16.1 1.6 %collective-permute-start.5 = (bf16[4,2,128,128]{3,2,1,0:T(8,128)(2,1)S(1)}, bf16[4,2,128,128]{3,2,1,0:T(8,128)(2,1)S(1)}, u32[]{:S(2)}, u32[]{:S(2)}) collective-permute-start(bf16[4,2,128,128]{3,2,1,0:T(8,128)(2,1)S(1)} %get-tuple-element.24), channel_id=1, source_target_pairs={{0,4},{4,0},{8,12},{12,8},{16,20},{20,16},{24,28},{28,24},{1,5},{5... | collective-permute-start | bytes 786440 | tf_op jit(solution)/shard_map/ppermute | solution.py:249
  17.8 5.6 %collective-permute-start.9 = (bf16[2,128,256]{2,1,0:T(8,128)(2,1)S(1)}, bf16[2,128,256]{2,1,0:T(8,128)(2,1)S(1)}, u32[]{:S(2)}, u32[]{:S(2)}) collective-permute-start(bf16[2,128,256]{2,1,0:T(8,128)(2,1)S(1)} %slice.70), channel_id=1, source_target_pairs={{0,1},{1,0},{2,3},{3,2},{4,5},{5,4},{6,7},{7,6},{8,9},{9,8},{10,11... | collective-permute-start | bytes 393224 | tf_op jit(solution)/shard_map/ppermute | solution.py:249
  19.4 7.4 %collective-permute-start.6 = (bf16[2,2,128,128]{3,2,1,0:T(8,128)(2,1)S(1)}, bf16[2,2,128,128]{3,2,1,0:T(8,128)(2,1)S(1)}, u32[]{:S(2)}, u32[]{:S(2)}) collective-permute-start(bf16[2,2,128,128]{3,2,1,0:T(8,128)(2,1)S(1)} %pad_maximum_fusion.2), channel_id=1, source_target_pairs={{0,24},{4,28},{8,16},{12,20},{16,8},{20,12},{24,0},{28,4},{1,25},{... | collective-permute-start | bytes 393224 | tf_op jit(solution)/shard_map/ppermute | solution.py:249
  20.7 7.7 %collective-permute-start.7 = (bf16[2,2,128,128]{3,2,1,0:T(8,128)(2,1)S(1)}, bf16[2,2,128,128]{3,2,1,0:T(8,128)(2,1)S(1)}, u32[]{:S(2)}, u32[]{:S(2)}) collective-permute-start(bf16[2,2,128,128]{3,2,1,0:T(8,128)(2,1)S(1)} %pad_maximum_fusion.3), channel_id=1, source_target_pairs={{0,16},{4,20},{8,24},{12,28},{16,0},{20,4},{24,8},{28,12},{1,17},{... | collective-permute-start | bytes 393224 | tf_op jit(solution)/shard_map/ppermute | solution.py:249
  21.6 6.8 %collective-permute-start.8 = (bf16[2,2,128,128]{3,2,1,0:T(8,128)(2,1)S(1)}, bf16[2,2,128,128]{3,2,1,0:T(8,128)(2,1)S(1)}, u32[]{:S(2)}, u32[]{:S(2)}) collective-permute-start(bf16[2,2,128,128]{3,2,1,0:T(8,128)(2,1)S(1)} %pad_maximum_fusion.4), channel_id=1, source_target_pairs={{0,8},{4,12},{8,0},{12,4},{16,24},{20,28},{24,16},{28,20},{1,9},{5... | collective-permute-start | bytes 393224 | tf_op jit(solution)/shard_map/ppermute | solution.py:249
  23.4 5.3 %collective-permute-start.10 = (bf16[1,128,256]{2,1,0:T(8,128)(2,1)S(1)}, bf16[1,128,256]{2,1,0:T(8,128)(2,1)S(1)}, u32[]{:S(2)}, u32[]{:S(2)}) collective-permute-start(bf16[1,128,256]{2,1,0:T(8,128)(2,1)S(1)} %slice.86), channel_id=1, source_target_pairs={{0,2},{1,3},{2,0},{3,1},{4,6},{5,7},{6,4},{7,5},{8,10},{9,11},{10,... | collective-permute-start | bytes 196616 | tf_op jit(solution)/shard_map/ppermute | solution.py:249

commit v4 on v3

--- a/solution.py
+++ b/solution.py
@@ -110,11 +110,6 @@
             other_ref[k, i] = left[theirs] * right[theirs]
 
 
-def taps_kernel(taps_ref, high_ref, low_ref, filt_ref):
-    for a in range(filt_ref.shape[0]):
-        filt_ref[a] = forward(taps_ref[:, a * BLOCK : (a + 1) * BLOCK], high_ref, low_ref)
-
-
 def far(k):
     return k.bit_count() > 1
 
@@ -147,7 +142,9 @@
 
 
 def early_kernel(count, *refs):
-    pieces, (high_ref, low_ref, wave_ref) = early_pieces(refs, count)
+    pieces, (taps_ref, high_ref, low_ref, wave_ref, filt_ref) = early_pieces(refs, count)
+    for a in range(count):
+        filt_ref[a] = forward(taps_ref[:, a * BLOCK : (a + 1) * BLOCK], high_ref, low_ref)
     for at, (k, pair) in enumerate(pieces):
         for i in range(2):
             wave_ref[at, i] = transform(pair, i, high_ref, low_ref)
@@ -291,9 +288,8 @@
         HBM,
     )
     first, rest = exchange(own, other, True)
-    (filt,) = call(taps_kernel, (taps, high, low), (wave,), [], "taps")
     waves = ((len(early(count)), 2, chans, 2 * BLOCK), jnp.float32)
-    (begun,) = call(functools.partial(early_kernel, count), (*first, high, low), (waves,), [], "early", flops=int(2e+09))
+    begun, filt = call(functools.partial(early_kernel, count), (*first, taps, high, low), (waves, wave), [], "early", flops=int(2e+09))
     own, other, mix_wave, pull_wave = call(
         functools.partial(sides_kernel, count),
         (*rest, begun, filt, high, low, inverse),

time: 30 us -> 29.5 us (0.983)
    ppermute x11, waiting for transfers between devices: 7.45 us -> 7.15 us  [swap(): lax.ppermute(array, axis, [(i, i ^ k) for i in range(lax.axis_size(axis))])]
    pallas_call x6 -> x5, Pallas kernels: 5.65 us -> 5.43 us  [call(): pl.pallas_call(body, out_shape=tuple((jax.ShapeDtypeStruct(shape, kind) f...]
where the time goes in v4:
time: 29.5 us; the launch traced here: 29.3 us
  starting transfers between devices  15.8 us (54%)
  waiting for transfers between devices  7.15 us (24%)
  Pallas kernels  5.43 us (18%)
  between operations  0.76 us (3%)
    ppermute x11, starting transfers between devices, swap(): lax.ppermute(array, axis, [(i, i ^ k) for i in range(lax.axis_size(axis))])  15.8 us
    ppermute x11, waiting for transfers between devices, swap(): lax.ppermute(array, axis, [(i, i ^ k) for i in range(lax.axis_size(axis))])  7.15 us
    pallas_call x5, Pallas kernels, call(): pl.pallas_call(body, out_shape=tuple((jax.ShapeDtypeStruct(shape, kind) f...  5.43 us
  transfers between devices with their start and end apart: 11, of which 8 were waited for; matrix products, arithmetic and copies ran while one was open for 1% of the time, Pallas kernels for 5%

profile of v4, /device:TPU:0, one launch (start us, length us, event | category | flops | bytes accessed | tf_op | source)
XLA Modules:
  0.0 29.3 jit_solution(7486117769491108371)
XLA Ops:
  0.6 1.3 %gate.1 = (bf16[8,128,128]{2,1,0:T(8,128)(2,1)S(1)}, bf16[8,128,128]{2,1,0:T(8,128)(2,1)S(1)}, bf16[8,128,128]{2,1,0:T(8,128)(2,1)S(1)}, bf16[8,128,128]{2,1,0:T...) custom-call(bf16[8,128,128]{2,1,0:T(8,128)(2,1)} %bitcast.12, ...), custom_call_target="tpu_custom_call" | custom-call | tf_op jit(solution)/shard_map/gate/pallas_call | solution.py:233
  1.9 0.5 %collective-permute-start = (bf16[4,2,128,128]{3,2,1,0:T(8,128)(2,1)S(1)}, bf16[4,2,128,128]{3,2,1,0:T(8,128)(2,1)S(1)}, u32[]{:S(2)}, u32[]{:S(2)}) collective-permute-start(bf16[4,2,128,128]{3,2,1,0:T(8,128)(2,1)S(1)} %get-tuple-element.24), channel_id=1, source_target_pairs={{0,4},{4,0},{8,12},{12,8},{16,20},{20,16},{24,28},{28,24},{1,5},{5... | collective-permute-start | bytes 786440 | tf_op jit(solution)/shard_map/ppermute | solution.py:246
  2.5 3.5 %collective-permute-start.3 = (bf16[2,128,128]{2,1,0:T(8,128)(2,1)S(1)}, bf16[2,128,128]{2,1,0:T(8,128)(2,1)S(1)}, u32[]{:S(2)}, u32[]{:S(2)}) collective-permute-start(bf16[2,128,128]{2,1,0:T(8,128)(2,1)S(1)} %get-tuple-element.52), channel_id=1, source_target_pairs={{0,24},{4,28},{8,16},{12,20},{16,8},{20,12},{24,0},{28,4},{1,25},{... | collective-permute-start | bytes 196616 | tf_op jit(solution)/shard_map/ppermute | solution.py:246
  6.0 0.0 collective-permute-done.refs_1_
  6.0 0.0 copy-start.3
  6.0 1.5 %collective-permute-start.4 = (bf16[2,128,128]{2,1,0:T(8,128)(2,1)S(1)}, bf16[2,128,128]{2,1,0:T(8,128)(2,1)S(1)}, u32[]{:S(2)}, u32[]{:S(2)}) collective-permute-start(bf16[2,128,128]{2,1,0:T(8,128)(2,1)S(1)} %get-tuple-element.49), channel_id=1, source_target_pairs={{0,24},{4,28},{8,16},{12,20},{16,8},{20,12},{24,0},{28,4},{1,25},{... | collective-permute-start | bytes 196616 | tf_op jit(solution)/shard_map/ppermute | solution.py:246
  7.5 0.0 copy-start.1
  7.5 0.0 copy-start.2
  7.5 0.6 %collective-permute-start.1 = (bf16[2,2,128,128]{3,2,1,0:T(8,128)(2,1)S(1)}, bf16[2,2,128,128]{3,2,1,0:T(8,128)(2,1)S(1)}, u32[]{:S(2)}, u32[]{:S(2)}) collective-permute-start(bf16[2,2,128,128]{3,2,1,0:T(8,128)(2,1)S(1)} %pad_maximum_fusion), channel_id=1, source_target_pairs={{0,8},{4,12},{8,0},{12,4},{16,24},{20,28},{24,16},{28,20},{1,9},{5... | collective-permute-start | bytes 393224 | tf_op jit(solution)/shard_map/ppermute | solution.py:246
  8.1 0.0 copy-start
  8.2 1.6 %collective-permute-start.2 = (bf16[2,2,128,128]{3,2,1,0:T(8,128)(2,1)S(1)}, bf16[2,2,128,128]{3,2,1,0:T(8,128)(2,1)S(1)}, u32[]{:S(2)}, u32[]{:S(2)}) collective-permute-start(bf16[2,2,128,128]{3,2,1,0:T(8,128)(2,1)S(1)} %pad_maximum_fusion.1), channel_id=1, source_target_pairs={{0,16},{4,20},{8,24},{12,28},{16,0},{20,4},{24,8},{28,12},{1,17},{... | collective-permute-start | bytes 393224 | tf_op jit(solution)/shard_map/ppermute | solution.py:246
  9.7 0.0 collective-permute-done.3.refs_2_
  9.7 2.2 %collective-permute-done.4.refs_3_ = bf16[2,128,128]{2,1,0:T(8,128)(2,1)S(1)} collective-permute-done((bf16[2,128,128]{2,1,0:T(8,128)(2,1)S(1)}, bf16[2,128,128]{2,1,0:T(8,128)(2,1)S(1)}, u32[]{:S(2)}, u32[]{:S(2)}) %collective-permute-start.4) | collective-permute-done | bytes 65568 | tf_op jit(solution)/shard_map/ppermute | solution.py:246
  11.9 0.0 copy-done.3
  11.9 0.0 copy-done.1
  11.9 0.0 copy-done.2
  11.9 0.7 %early.1 = (f32[2,2,128,512]{3,2,1,0:T(8,128)S(1)}, f32[4,128,512]{2,1,0:T(8,128)S(1)}) custom-call(bf16[4,2,128,128]{3,2,1,0:T(8,128)(2,1)S(1)} %get-tuple-element.23.refs_0_, bf16[4,2,128,128]{3,2,1,0:T(8,128)(2,1)S(1)} %collective-permute-done.refs_1_, bf16[2,128,128]{2,1,0:T(8,128)(2,1)S(1)} %collective-permute-done.3.refs_2_, ...), custom_call_target="tpu_custom_call" | custom-call | flops 2000000000 | tf_op jit(solution)/shard_map/early/pallas_call | solution.py:233
  12.6 0.6 %collective-permute-done.1.refs_0_ = bf16[2,2,128,128]{3,2,1,0:T(8,128)(2,1)S(1)} collective-permute-done((bf16[2,2,128,128]{3,2,1,0:T(8,128)(2,1)S(1)}, bf16[2,2,128,128]{3,2,1,0:T(8,128)(2,1)S(1)}, u32[]{:S(2)}, u32[]{:S(2)}) %collective-permute-start.1) | collective-permute-done | bytes 131104 | tf_op jit(solution)/shard_map/ppermute | solution.py:246
  13.2 0.8 %collective-permute-done.2.refs_1_ = bf16[2,2,128,128]{3,2,1,0:T(8,128)(2,1)S(1)} collective-permute-done((bf16[2,2,128,128]{3,2,1,0:T(8,128)(2,1)S(1)}, bf16[2,2,128,128]{3,2,1,0:T(8,128)(2,1)S(1)}, u32[]{:S(2)}, u32[]{:S(2)}) %collective-permute-start.2) | collective-permute-done | bytes 131104 | tf_op jit(solution)/shard_map/ppermute | solution.py:246
  14.0 0.0 copy-done
  14.0 1.6 %sides.1 = (bf16[4,2,128,128]{3,2,1,0:T(8,128)(2,1)S(1)}, bf16[4,2,128,128]{3,2,1,0:T(8,128)(2,1)S(1)}, f32[4,128,512]{2,1,0:T(8,128)S(1)}, f32[4,128,512]{2,1,0:T(8,128)S(1)}) custom-call(bf16[2,2,128,128]{3,2,1,0:T(8,128)(2,1)S(1)} %collective-permute-done.1.refs_0_, bf16[2,2,128,128]{3,2,1,0:T(8,128)(2,1)S(1)} %collective-permute-done.2.refs_1_, ...), custom_call_target="tpu_custom_call" | custom-call | tf_op jit(solution)/shard_map/sides/pallas_call | solution.py:233
  15.6 0.1 collective-permute-start.5
  15.7 0.6 %lag.1 = bf16[4,128,256]{2,1,0:T(8,128)(2,1)S(1)} custom-call(f32[4,128,512]{2,1,0:T(8,128)S(1)} %get-tuple-element.33.refs_0_, f32[4,128,512]{2,1,0:T(8,128)S(1)} %get-tuple-element.34.refs_1_, bf16[512,256]{1,0:T(8,128)(2,1)S(1)} %copy-done, bf16[4,2,128,128]{3,2,1,0:T(8,128)(2,1)S(1)} %get-tuple-element.27.refs_3_), custom_call_target="tpu_custom_call" | custom-call | tf_op jit(solution)/shard_map/lag/pallas_call | solution.py:233
  16.3 0.8 %collective-permute-done.5 = bf16[4,2,128,128]{3,2,1,0:T(8,128)(2,1)S(1)} collective-permute-done((bf16[4,2,128,128]{3,2,1,0:T(8,128)(2,1)S(1)}, bf16[4,2,128,128]{3,2,1,0:T(8,128)(2,1)S(1)}, u32[]{:S(2)}, u32[]{:S(2)}) %collective-permute-start.5) | collective-permute-done | bytes 262176 | tf_op jit(solution)/shard_map/ppermute | solution.py:246
  17.2 1.6 %collective-permute-start.9 = (bf16[2,128,256]{2,1,0:T(8,128)(2,1)S(1)}, bf16[2,128,256]{2,1,0:T(8,128)(2,1)S(1)}, u32[]{:S(2)}, u32[]{:S(2)}) collective-permute-start(bf16[2,128,256]{2,1,0:T(8,128)(2,1)S(1)} %slice.70), channel_id=1, source_target_pairs={{0,1},{1,0},{2,3},{3,2},{4,5},{5,4},{6,7},{7,6},{8,9},{9,8},{10,11... | collective-permute-start | bytes 393224 | tf_op jit(solution)/shard_map/ppermute | solution.py:246
  18.9 1.7 %collective-permute-start.6 = (bf16[2,2,128,128]{3,2,1,0:T(8,128)(2,1)S(1)}, bf16[2,2,128,128]{3,2,1,0:T(8,128)(2,1)S(1)}, u32[]{:S(2)}, u32[]{:S(2)}) collective-permute-start(bf16[2,2,128,128]{3,2,1,0:T(8,128)(2,1)S(1)} %pad_maximum_fusion.2), channel_id=1, source_target_pairs={{0,24},{4,28},{8,16},{12,20},{16,8},{20,12},{24,0},{28,4},{1,25},{... | collective-permute-start | bytes 393224 | tf_op jit(solution)/shard_map/ppermute | solution.py:246
  20.6 0.7 %collective-permute-start.7 = (bf16[2,2,128,128]{3,2,1,0:T(8,128)(2,1)S(1)}, bf16[2,2,128,128]{3,2,1,0:T(8,128)(2,1)S(1)}, u32[]{:S(2)}, u32[]{:S(2)}) collective-permute-start(bf16[2,2,128,128]{3,2,1,0:T(8,128)(2,1)S(1)} %pad_maximum_fusion.3), channel_id=1, source_target_pairs={{0,16},{4,20},{8,24},{12,28},{16,0},{20,4},{24,8},{28,12},{1,17},{... | collective-permute-start | bytes 393224 | tf_op jit(solution)/shard_map/ppermute | solution.py:246
  21.3 1.3 %collective-permute-start.8 = (bf16[2,2,128,128]{3,2,1,0:T(8,128)(2,1)S(1)}, bf16[2,2,128,128]{3,2,1,0:T(8,128)(2,1)S(1)}, u32[]{:S(2)}, u32[]{:S(2)}) collective-permute-start(bf16[2,2,128,128]{3,2,1,0:T(8,128)(2,1)S(1)} %pad_maximum_fusion.4), channel_id=1, source_target_pairs={{0,8},{4,12},{8,0},{12,4},{16,24},{20,28},{24,16},{28,20},{1,9},{5... | collective-permute-start | bytes 393224 | tf_op jit(solution)/shard_map/ppermute | solution.py:246
  22.6 0.2 collective-permute-done.9
  22.8 2.7 %collective-permute-start.10 = (bf16[1,128,256]{2,1,0:T(8,128)(2,1)S(1)}, bf16[1,128,256]{2,1,0:T(8,128)(2,1)S(1)}, u32[]{:S(2)}, u32[]{:S(2)}) collective-permute-start(bf16[1,128,256]{2,1,0:T(8,128)(2,1)S(1)} %slice.86), channel_id=1, source_target_pairs={{0,2},{1,3},{2,0},{3,1},{4,6},{5,7},{6,4},{7,5},{8,10},{9,11},{10,... | collective-permute-start | bytes 196616 | tf_op jit(solution)/shard_map/ppermute | solution.py:246
  25.5 0.7 %collective-permute-done.6.refs_0_ = bf16[2,2,128,128]{3,2,1,0:T(8,128)(2,1)S(1)} collective-permute-done((bf16[2,2,128,128]{3,2,1,0:T(8,128)(2,1)S(1)}, bf16[2,2,128,128]{3,2,1,0:T(8,128)(2,1)S(1)}, u32[]{:S(2)}, u32[]{:S(2)}) %collective-permute-start.6) | collective-permute-done | bytes 131104 | tf_op jit(solution)/shard_map/ppermute | solution.py:246
  26.2 1.7 %collective-permute-done.7.refs_1_ = bf16[2,2,128,128]{3,2,1,0:T(8,128)(2,1)S(1)} collective-permute-done((bf16[2,2,128,128]{3,2,1,0:T(8,128)(2,1)S(1)}, bf16[2,2,128,128]{3,2,1,0:T(8,128)(2,1)S(1)}, u32[]{:S(2)}, u32[]{:S(2)}) %collective-permute-start.7) | collective-permute-done | bytes 131104 | tf_op jit(solution)/shard_map/ppermute | solution.py:246
  27.9 0.0 collective-permute-done.8.refs_2_
  27.9 0.2 collective-permute-done.10.refs_9_
  28.1 1.2 %grads.1 = (bf16[8,128,128]{2,1,0:T(8,128)(2,1)}, bf16[8,128,128]{2,1,0:T(8,128)(2,1)}, bf16[8,128,128]{2,1,0:T(8,128)(2,1)}, bf16[8,128,128]{2,1,0:T(8,128)(2,1)}, f32[128,256]{1,0:T(8,128)}) custom-call(bf16[2,2,128,128]{3,2,1,0:T(8,128)(2,1)S(1)} %collective-permute-done.6.refs_0_, bf16[2,2,128,128]{3,2,1,0:T(8,128)(2,1)S(1)} %collective-permute-done.7.refs_1_, ...), custom_call_target="tpu_custom_call" | custom-call | tf_op jit(solution)/shard_map/grads/pallas_call | solution.py:233
  (14 shorter events, 0.2 us)
Async XLA Ops:
  1.9 4.1 %collective-permute-start = (bf16[4,2,128,128]{3,2,1,0:T(8,128)(2,1)S(1)}, bf16[4,2,128,128]{3,2,1,0:T(8,128)(2,1)S(1)}, u32[]{:S(2)}, u32[]{:S(2)}) collective-permute-start(bf16[4,2,128,128]{3,2,1,0:T(8,128)(2,1)S(1)} %get-tuple-element.24), channel_id=1, source_target_pairs={{0,4},{4,0},{8,12},{12,8},{16,20},{20,16},{24,28},{28,24},{1,5},{5... | collective-permute-start | bytes 786440 | tf_op jit(solution)/shard_map/ppermute | solution.py:246
  2.5 7.3 %collective-permute-start.3 = (bf16[2,128,128]{2,1,0:T(8,128)(2,1)S(1)}, bf16[2,128,128]{2,1,0:T(8,128)(2,1)S(1)}, u32[]{:S(2)}, u32[]{:S(2)}) collective-permute-start(bf16[2,128,128]{2,1,0:T(8,128)(2,1)S(1)} %get-tuple-element.52), channel_id=1, source_target_pairs={{0,24},{4,28},{8,16},{12,20},{16,8},{20,12},{24,0},{28,4},{1,25},{... | collective-permute-start | bytes 196616 | tf_op jit(solution)/shard_map/ppermute | solution.py:246
  6.0 5.9 %copy-start.3 = (bf16[128,1024]{1,0:T(8,128)(2,1)S(1)}, bf16[128,1024]{1,0:T(8,128)(2,1)}, u32[]{:S(2)}) copy-start(bf16[128,1024]{1,0:T(8,128)(2,1)} %refs_4_.2) | copy-start | bytes 786436
  6.0 5.9 %collective-permute-start.4 = (bf16[2,128,128]{2,1,0:T(8,128)(2,1)S(1)}, bf16[2,128,128]{2,1,0:T(8,128)(2,1)S(1)}, u32[]{:S(2)}, u32[]{:S(2)}) collective-permute-start(bf16[2,128,128]{2,1,0:T(8,128)(2,1)S(1)} %get-tuple-element.49), channel_id=1, source_target_pairs={{0,24},{4,28},{8,16},{12,20},{16,8},{20,12},{24,0},{28,4},{1,25},{... | collective-permute-start | bytes 196616 | tf_op jit(solution)/shard_map/ppermute | solution.py:246
  7.5 4.4 %copy-start.1 = (bf16[256,512]{1,0:T(8,128)(2,1)S(1)}, bf16[256,512]{1,0:T(8,128)(2,1)}, u32[]{:S(2)}) copy-start(bf16[256,512]{1,0:T(8,128)(2,1)} %constant.7.clone.refs_6_.refs_5_) | copy-start | bytes 786436
  7.5 4.4 %copy-start.2 = (bf16[256,512]{1,0:T(8,128)(2,1)S(1)}, bf16[256,512]{1,0:T(8,128)(2,1)}, u32[]{:S(2)}) copy-start(bf16[256,512]{1,0:T(8,128)(2,1)} %constant.6.clone.refs_5_.refs_4_) | copy-start | bytes 786436
  7.5 5.7 %collective-permute-start.1 = (bf16[2,2,128,128]{3,2,1,0:T(8,128)(2,1)S(1)}, bf16[2,2,128,128]{3,2,1,0:T(8,128)(2,1)S(1)}, u32[]{:S(2)}, u32[]{:S(2)}) collective-permute-start(bf16[2,2,128,128]{3,2,1,0:T(8,128)(2,1)S(1)} %pad_maximum_fusion), channel_id=1, source_target_pairs={{0,8},{4,12},{8,0},{12,4},{16,24},{20,28},{24,16},{28,20},{1,9},{5... | collective-permute-start | bytes 393224 | tf_op jit(solution)/shard_map/ppermute | solution.py:246
  8.1 5.8 %copy-start = (bf16[512,256]{1,0:T(8,128)(2,1)S(1)}, bf16[512,256]{1,0:T(8,128)(2,1)}, u32[]{:S(2)}) copy-start(bf16[512,256]{1,0:T(8,128)(2,1)} %constant.8.clone.refs_6_.refs_2_) | copy-start | bytes 786436
  8.2 5.8 %collective-permute-start.2 = (bf16[2,2,128,128]{3,2,1,0:T(8,128)(2,1)S(1)}, bf16[2,2,128,128]{3,2,1,0:T(8,128)(2,1)S(1)}, u32[]{:S(2)}, u32[]{:S(2)}) collective-permute-start(bf16[2,2,128,128]{3,2,1,0:T(8,128)(2,1)S(1)} %pad_maximum_fusion.1), channel_id=1, source_target_pairs={{0,16},{4,20},{8,24},{12,28},{16,0},{20,4},{24,8},{28,12},{1,17},{... | collective-permute-start | bytes 393224 | tf_op jit(solution)/shard_map/ppermute | solution.py:246
  15.6 1.6 %collective-permute-start.5 = (bf16[4,2,128,128]{3,2,1,0:T(8,128)(2,1)S(1)}, bf16[4,2,128,128]{3,2,1,0:T(8,128)(2,1)S(1)}, u32[]{:S(2)}, u32[]{:S(2)}) collective-permute-start(bf16[4,2,128,128]{3,2,1,0:T(8,128)(2,1)S(1)} %get-tuple-element.28), channel_id=1, source_target_pairs={{0,4},{4,0},{8,12},{12,8},{16,20},{20,16},{24,28},{28,24},{1,5},{5... | collective-permute-start | bytes 786440 | tf_op jit(solution)/shard_map/ppermute | solution.py:246
  17.2 5.6 %collective-permute-start.9 = (bf16[2,128,256]{2,1,0:T(8,128)(2,1)S(1)}, bf16[2,128,256]{2,1,0:T(8,128)(2,1)S(1)}, u32[]{:S(2)}, u32[]{:S(2)}) collective-permute-start(bf16[2,128,256]{2,1,0:T(8,128)(2,1)S(1)} %slice.70), channel_id=1, source_target_pairs={{0,1},{1,0},{2,3},{3,2},{4,5},{5,4},{6,7},{7,6},{8,9},{9,8},{10,11... | collective-permute-start | bytes 393224 | tf_op jit(solution)/shard_map/ppermute | solution.py:246
  18.9 7.3 %collective-permute-start.6 = (bf16[2,2,128,128]{3,2,1,0:T(8,128)(2,1)S(1)}, bf16[2,2,128,128]{3,2,1,0:T(8,128)(2,1)S(1)}, u32[]{:S(2)}, u32[]{:S(2)}) collective-permute-start(bf16[2,2,128,128]{3,2,1,0:T(8,128)(2,1)S(1)} %pad_maximum_fusion.2), channel_id=1, source_target_pairs={{0,24},{4,28},{8,16},{12,20},{16,8},{20,12},{24,0},{28,4},{1,25},{... | collective-permute-start | bytes 393224 | tf_op jit(solution)/shard_map/ppermute | solution.py:246
  20.6 7.4 %collective-permute-start.7 = (bf16[2,2,128,128]{3,2,1,0:T(8,128)(2,1)S(1)}, bf16[2,2,128,128]{3,2,1,0:T(8,128)(2,1)S(1)}, u32[]{:S(2)}, u32[]{:S(2)}) collective-permute-start(bf16[2,2,128,128]{3,2,1,0:T(8,128)(2,1)S(1)} %pad_maximum_fusion.3), channel_id=1, source_target_pairs={{0,16},{4,20},{8,24},{12,28},{16,0},{20,4},{24,8},{28,12},{1,17},{... | collective-permute-start | bytes 393224 | tf_op jit(solution)/shard_map/ppermute | solution.py:246
  21.3 6.6 %collective-permute-start.8 = (bf16[2,2,128,128]{3,2,1,0:T(8,128)(2,1)S(1)}, bf16[2,2,128,128]{3,2,1,0:T(8,128)(2,1)S(1)}, u32[]{:S(2)}, u32[]{:S(2)}) collective-permute-start(bf16[2,2,128,128]{3,2,1,0:T(8,128)(2,1)S(1)} %pad_maximum_fusion.4), channel_id=1, source_target_pairs={{0,8},{4,12},{8,0},{12,4},{16,24},{20,28},{24,16},{28,20},{1,9},{5... | collective-permute-start | bytes 393224 | tf_op jit(solution)/shard_map/ppermute | solution.py:246
  22.8 5.3 %collective-permute-start.10 = (bf16[1,128,256]{2,1,0:T(8,128)(2,1)S(1)}, bf16[1,128,256]{2,1,0:T(8,128)(2,1)S(1)}, u32[]{:S(2)}, u32[]{:S(2)}) collective-permute-start(bf16[1,128,256]{2,1,0:T(8,128)(2,1)S(1)} %slice.86), channel_id=1, source_target_pairs={{0,2},{1,3},{2,0},{3,1},{4,6},{5,7},{6,4},{7,5},{8,10},{9,11},{10,... | collective-permute-start | bytes 196616 | tf_op jit(solution)/shard_map/ppermute | solution.py:246

commit v5 on v4

--- a/solution.py
+++ b/solution.py
@@ -66,24 +66,34 @@
     lax.fori_loop(0, chans // tile, step, 0, unroll=True)
 
 
-def spectra(ref, rows, re, im):
-    return [(ref[a, rows, re], ref[a, rows, im]) for a in range(ref.shape[0])]
-
-
-def convolve_tile(signal, taps, sign, put):
-    before = None
-    for c in range(len(signal)):
-        here = total([times(signal[a], taps[c - a]) for a in range(c + 1)])
-        put(c, here if c == 0 else (here[0] - sign * before[1], here[1] + sign * before[0]))
-        before = here
-
-
-def correlate_tile(signal, other, sign, put):
-    after = None
-    for c in reversed(range(len(signal))):
-        here = total([times_conj(signal[a], other[a - c]) for a in range(c, len(signal))])
-        put(c, here if after is None else (here[0] + sign * after[1], here[1] - sign * after[0]))
-        after = here
+def spectrum(ref, rows, re, im, *at):
+    return ref[(*at, rows, re)], ref[(*at, rows, im)]
+
+
+def convolved(c, signal, taps):
+    return [times(signal[a], taps[c - a]) for a in signal if a <= c]
+
+
+def correlated(c, signal, other):
+    return [times_conj(signal[a], other[a - c]) for a in signal if a >= c]
+
+
+def plus(left, right, sign):
+    return left + right if sign > 0 else left - right
+
+
+def put_convolution(sums, sign, put):
+    for c in range(len(sums)):
+        here, before = sums[c], sums[c - 1]
+        put(c, here if c == 0 else (plus(here[0], before[1], -sign), plus(here[1], before[0], sign)))
+
+
+def put_correlation(sums, sign, put):
+    for c in range(len(sums)):
+        here = sums[c]
+        if c + 1 < len(sums):
+            here = plus(here[0], sums[c + 1][1], sign), plus(here[1], sums[c + 1][0], -sign)
+        put(c, here)
 
 
 def putter(prod, rows, re, im):
@@ -110,28 +120,44 @@
             other_ref[k, i] = left[theirs] * right[theirs]
 
 
-def far(k):
-    return k.bit_count() > 1
-
-
 def early(count):
-    return [k for k in range(count) if k == 0 or far(k)]
+    return [0, 3] if count == 4 else []
 
 
 def late(count):
-    return [k for k in range(count) if k and not far(k)]
-
-
-def early_pieces(refs, count):
-    size = len(early(count))
-    pieces = [(refs[2 * i], refs[2 * i + 1]) for i in range(size)]
-    pieces[0] = pieces[0][0].at[0], pieces[0][1].at[0]
-    return list(zip(early(count), pieces)), refs[2 * size :]
-
-
-def late_pieces(refs, count):
-    size = len(late(count))
-    return [(k, (refs[i].at[0], refs[i].at[1])) for i, k in enumerate(late(count))], refs[size:]
+    return [k for k in range(count) if k not in early(count)]
+
+
+def on_cases(count, work):
+    if count != 4:
+        return work((), tuple(range(count)))
+    chip, _ = place()
+    for ahead, rest in (((0, 3), (1, 2)), ((1, 2), (0, 3))):
+
+        @pl.when((chip == ahead[0]) | (chip == ahead[1]))
+        def _():
+            work(ahead, rest)
+
+
+def early_at(a):
+    return jnp.where(place()[0] == a, 0, 1)
+
+
+def late_at(a, count):
+    return jnp.where(place()[0] ^ 1 == a, 0, 1) if count == 4 else a
+
+
+def pieces_of(refs, count, chips):
+    pieces, at = [], 0
+    for k in chips:
+        if k == 0:
+            pieces.append((k, (refs[at].at[0], refs[at + 1].at[0])))
+        elif k in early(count):
+            pieces.append((k, (refs[at], refs[at + 1])))
+        else:
+            pieces.append((k, (refs[at].at[0], refs[at].at[1])))
+        at += 2 if k == 0 or k in early(count) else 1
+    return pieces, refs[at:]
 
 
 def transform(pair, i, high_ref, low_ref):
@@ -142,30 +168,57 @@
 
 
 def early_kernel(count, *refs):
-    pieces, (taps_ref, high_ref, low_ref, wave_ref, filt_ref) = early_pieces(refs, count)
+    pieces, refs = pieces_of(refs, count, early(count))
+    taps_ref, high_ref, low_ref, filt_ref, *refs = refs
     for a in range(count):
         filt_ref[a] = forward(taps_ref[:, a * BLOCK : (a + 1) * BLOCK], high_ref, low_ref)
+    if not pieces:
+        return
+    wave_ref, conv_ref, back_ref = refs
+    for at, (_, pair) in enumerate(pieces):
+        for i in range(2):
+            wave_ref[at, i] = transform(pair, i, high_ref, low_ref)
+
+    def work(ahead, rest):
+        def body(rows, re, im, sign):
+            taps = [spectrum(filt_ref, rows, re, im, a) for a in range(count)]
+            mixed, pulled = ({a: spectrum(wave_ref, rows, re, im, early_at(a), i) for a in ahead} for i in range(2))
+            for c in range(count):
+                for ref, terms in ((conv_ref, convolved(c, mixed, taps)), (back_ref, correlated(c, pulled, taps))):
+                    if terms:
+                        ref[c, rows, re], ref[c, rows, im] = total(terms)
+
+        tiles(filt_ref.shape[1], body)
+
+    on_cases(count, work)
+
+
+def sides_kernel(count, *refs):
+    pieces, refs = pieces_of(refs, count, late(count))
+    filt_ref, high_ref, low_ref, inv_ref, *refs = refs
+    parts, (own_ref, other_ref, wave_ref, prod) = refs[:-4], refs[-4:]
+    chip, core = place()
     for at, (k, pair) in enumerate(pieces):
         for i in range(2):
-            wave_ref[at, i] = transform(pair, i, high_ref, low_ref)
-
-
-def sides_kernel(count, *refs):
-    pieces, refs = late_pieces(refs, count)
-    wave_ref, filt_ref, high_ref, low_ref, inv_ref, own_ref, other_ref, mix_ref, pull_ref, prod = refs
-    chip, core = place()
-    for i, spec_ref in enumerate((mix_ref, pull_ref)):
-        for at, k in enumerate(early(count)):
-            spec_ref[chip ^ k] = wave_ref[at, i]
-        for k, pair in pieces:
-            spec_ref[chip ^ k] = transform(pair, i, high_ref, low_ref)
-
-    def body(rows, re, im, sign):
-        taps = spectra(filt_ref, rows, re, im)
-        convolve_tile(spectra(mix_ref, rows, re, im), taps, sign, putter(prod.at[0], rows, re, im))
-        correlate_tile(spectra(pull_ref, rows, re, im), taps, sign, putter(prod.at[1], rows, re, im))
-
-    tiles(filt_ref.shape[1], body)
+            wave_ref[at if early(count) else chip ^ k, i] = transform(pair, i, high_ref, low_ref)
+
+    def work(ahead, rest):
+        def body(rows, re, im, sign):
+            taps = [spectrum(filt_ref, rows, re, im, a) for a in range(count)]
+
+            def sums(i, terms, has_part):
+                signal = {a: spectrum(wave_ref, rows, re, im, late_at(a, count), i) for a in rest}
+                begun = [[spectrum(parts[i], rows, re, im, c)] if has_part(c) else [] for c in range(count)]
+                return [total(begun[c] + terms(c, signal, taps)) for c in range(count)]
+
+            conv = sums(0, convolved, lambda c: any(a <= c for a in ahead))
+            put_convolution(conv, sign, putter(prod.at[0], rows, re, im))
+            back = sums(1, correlated, lambda c: any(a >= c for a in ahead))
+            put_correlation(back, sign, putter(prod.at[1], rows, re, im))
+
+        tiles(filt_ref.shape[1], body)
+
+    on_cases(count, work)
     for k in range(count):
         for i in range(2):
             result = dot(prod[i, chip ^ k], inv_ref[...]).astype(jnp.bfloat16)
@@ -179,14 +232,24 @@
     return sum((number // 2**i % 2) * 2 ** (bits - 1 - i) for i in range(bits))
 
 
-def lag_kernel(pull_ref, mix_ref, inv_ref, lag_ref, prod):
+def lag_kernel(count, *refs):
+    *early_refs, late_ref, inv_ref, lag_ref, prod = refs
     width = lag_ref.shape[2]
     slot = lax.axis_index("chan")
 
-    def body(rows, re, im, sign):
-        correlate_tile(spectra(pull_ref, rows, re, im), spectra(mix_ref, rows, re, im), sign, putter(prod, rows, re, im))
-
-    tiles(prod.shape[1], body)
+    def work(ahead, rest):
+        def body(rows, re, im, sign):
+            mixed, pulled = (
+                {a: spectrum(early_refs[0], rows, re, im, early_at(a), i) for a in ahead}
+                | {a: spectrum(late_ref, rows, re, im, late_at(a, count), i) for a in rest}
+                for i in range(2)
+            )
+            sums = [total(correlated(c, pulled, mixed)) for c in range(count)]
+            put_correlation(sums, sign, putter(prod, rows, re, im))
+
+        tiles(prod.shape[1], body)
+
+    on_cases(count, work)
     for c in range(prod.shape[0]):
         result = dot(prod[c], inv_ref[...]).astype(jnp.bfloat16)
         for u in range(BLOCK // LANES):
@@ -196,11 +259,11 @@
 
 
 def grads_kernel(count, *refs):
-    rows_refs, (query_ref, key_ref, value_ref, upstream_ref) = refs[:count][::-1], refs[count : count + 4]
-    kept_ref, got_ref = refs[count + 4 : count + 6]
-    outs, filter_out, (held, sems, sums, sum_sem) = refs[-9:-5], refs[-5], refs[-4:]
+    rows_refs = refs[:count][::-1]
+    query_ref, key_ref, value_ref, upstream_ref, kept_ref, sum_ref, *outs = refs[count:-5]
+    filter_out, held, sems, sums, sum_sem = refs[-5:]
     chip, core = place()
-    sums[...] = kept_ref[0].astype(jnp.float32) + got_ref[0].astype(jnp.float32)
+    sums[...] = kept_ref[0].astype(jnp.float32) + sum_ref[0].astype(jnp.float32)
     copies = [pltpu.make_async_copy(sums, filter_out, sum_sem)]
     copies[0].start()
     for k in range(count):
@@ -246,16 +309,14 @@
     return lax.ppermute(array, axis, [(i, i ^ k) for i in range(lax.axis_size(axis))])
 
 
-def exchange(own, other, split):
+def exchange(own, other, ahead):
     count = own.shape[0]
     got = swap(other, "seq", 1)
-    if not split:
-        parts = [jnp.stack([own[k], got[k]]) for k in range(count)]
-        return [*(swap(parts[k], "seq", 2 * k) for k in reversed(range(1, count))), parts[0]], got
     first = [own, got]
-    for k in early(count)[1:]:
+    for k in ahead:
         first += [swap(own[k], "seq", 2 * k), swap(got[k], "seq", 2 * k)]
-    return first, [swap(jnp.stack([own[k], got[k]]), "seq", 2 * k) for k in late(count)]
+    rest = [k for k in reversed(range(1, count)) if k not in ahead]
+    return first, [swap(jnp.stack([own[k], got[k]]), "seq", 2 * k) for k in rest]
 
 
 def scatter_sum(pieces):
@@ -287,26 +348,44 @@
         "gate",
         HBM,
     )
-    first, rest = exchange(own, other, True)
+    first, rest = exchange(own, other, early(count)[1:])
+    rest = rest[::-1]
+    if not early(count):
+        first, rest = [], first + rest
     waves = ((len(early(count)), 2, chans, 2 * BLOCK), jnp.float32)
-    begun, filt = call(functools.partial(early_kernel, count), (*first, taps, high, low), (waves, wave), [], "early", flops=int(2e+09))
-    own, other, mix_wave, pull_wave = call(
+    filt, *begun = call(
+        functools.partial(early_kernel, count),
+        (*first, taps, high, low),
+        (wave, *((waves, wave, wave) if early(count) else ())),
+        [],
+        "early",
+        flops=int(2e9),
+    )
+    waves = ((len(late(count)), 2, chans, 2 * BLOCK), jnp.float32)
+    prod = pltpu.VMEM((count, chans, 2 * BLOCK), jnp.bfloat16)
+    own, other, late_waves = call(
         functools.partial(sides_kernel, count),
-        (*rest, begun, filt, high, low, inverse),
-        (half, half, wave, wave),
+        (*rest, filt, high, low, inverse, *begun[1:]),
+        (half, half, waves),
         [pltpu.VMEM((2, count, chans, 2 * BLOCK), jnp.bfloat16)],
         "sides",
     )
-    rows, swapped = exchange(own, other, False)
+    stay, rows = exchange(own, other, [])
     pieces = ((chan, chans, length // chan), jnp.bfloat16)
-    prod = pltpu.VMEM((count, chans, 2 * BLOCK), jnp.bfloat16)
-    (lag,) = call(lag_kernel, (pull_wave, mix_wave, inverse), (pieces,), [prod], "lag", after=(own,))
-    lag, _ = lax.optimization_barrier((lag, swapped))
+    (lag,) = call(
+        functools.partial(lag_kernel, count),
+        (*begun[:1], late_waves, inverse),
+        (pieces,),
+        [prod],
+        "lag",
+        after=(own,),
+    )
+    lag, _ = lax.optimization_barrier((lag, stay[1]))
     kept, got = scatter_sum(lag)
     sums = ((chans, length // chan), jnp.float32)
     *outs, filter_grad = call(
         functools.partial(grads_kernel, count),
-        (*rows, query, key, value, upstream, kept, got),
+        (*rows, jnp.stack([stay[0][0], stay[1][0]]), query, key, value, upstream, kept, got),
         (whole,) * 4 + (sums,),
         [
             pltpu.VMEM((4, seq, chans, positions), jnp.bfloat16),

time: 29.5 us -> 29.3 us (level)
  waiting for transfers between devices: 7.15 us -> 6.78 us
    ppermute x11, waiting for transfers between devices: 7.15 us -> 6.78 us  [swap(): lax.ppermute(array, axis, [(i, i ^ k) for i in range(lax.axis_size(axis))])]
  transfers between devices with their start and end apart: 11 -> 11, of which waited for: 8 -> 8; matrix products, arithmetic and copies ran while one was open for 1% -> 1% of each run, Pallas kernels for 5% -> 6%
where the time goes in v5:
time: 29.3 us; the launch traced here: 29.1 us
  starting transfers between devices  15.8 us (54%)
  waiting for transfers between devices  6.78 us (23%)
  Pallas kernels  5.59 us (19%)
  between operations  0.75 us (3%)
    ppermute x11, starting transfers between devices, swap(): lax.ppermute(array, axis, [(i, i ^ k) for i in range(lax.axis_size(axis))])  15.8 us
    ppermute x11, waiting for transfers between devices, swap(): lax.ppermute(array, axis, [(i, i ^ k) for i in range(lax.axis_size(axis))])  6.78 us
    pallas_call x5, Pallas kernels, call(): pl.pallas_call(body, out_shape=tuple((jax.ShapeDtypeStruct(shape, kind) f...  5.59 us
  transfers between devices with their start and end apart: 11, of which 8 were waited for; matrix products, arithmetic and copies ran while one was open for 1% of the time, Pallas kernels for 6%

profile of v5, /device:TPU:0, one launch (start us, length us, event | category | flops | bytes accessed | tf_op | source)
XLA Modules:
  0.0 29.1 jit_solution(11891559405179083356)
XLA Ops:
  0.6 1.3 %gate.1 = (bf16[8,128,128]{2,1,0:T(8,128)(2,1)S(1)}, bf16[8,128,128]{2,1,0:T(8,128)(2,1)S(1)}, bf16[8,128,128]{2,1,0:T(8,128)(2,1)S(1)}, bf16[8,128,128]{2,1,0:T...) custom-call(bf16[8,128,128]{2,1,0:T(8,128)(2,1)} %bitcast.12, ...), custom_call_target="tpu_custom_call" | custom-call | tf_op jit(solution)/shard_map/gate/pallas_call | solution.py:296
  1.9 0.5 %collective-permute-start = (bf16[4,2,128,128]{3,2,1,0:T(8,128)(2,1)S(1)}, bf16[4,2,128,128]{3,2,1,0:T(8,128)(2,1)S(1)}, u32[]{:S(2)}, u32[]{:S(2)}) collective-permute-start(bf16[4,2,128,128]{3,2,1,0:T(8,128)(2,1)S(1)} %get-tuple-element.25), channel_id=1, source_target_pairs={{0,4},{4,0},{8,12},{12,8},{16,20},{20,16},{24,28},{28,24},{1,5},{5... | collective-permute-start | bytes 786440 | tf_op jit(solution)/shard_map/ppermute | solution.py:309
  2.5 3.5 %collective-permute-start.3 = (bf16[2,128,128]{2,1,0:T(8,128)(2,1)S(1)}, bf16[2,128,128]{2,1,0:T(8,128)(2,1)S(1)}, u32[]{:S(2)}, u32[]{:S(2)}) collective-permute-start(bf16[2,128,128]{2,1,0:T(8,128)(2,1)S(1)} %get-tuple-element.54), channel_id=1, source_target_pairs={{0,24},{4,28},{8,16},{12,20},{16,8},{20,12},{24,0},{28,4},{1,25},{... | collective-permute-start | bytes 196616 | tf_op jit(solution)/shard_map/ppermute | solution.py:309
  6.0 0.0 collective-permute-done.refs_1_
  6.0 0.0 copy-start.3
  6.0 1.5 %collective-permute-start.4 = (bf16[2,128,128]{2,1,0:T(8,128)(2,1)S(1)}, bf16[2,128,128]{2,1,0:T(8,128)(2,1)S(1)}, u32[]{:S(2)}, u32[]{:S(2)}) collective-permute-start(bf16[2,128,128]{2,1,0:T(8,128)(2,1)S(1)} %get-tuple-element.51), channel_id=1, source_target_pairs={{0,24},{4,28},{8,16},{12,20},{16,8},{20,12},{24,0},{28,4},{1,25},{... | collective-permute-start | bytes 196616 | tf_op jit(solution)/shard_map/ppermute | solution.py:309
  7.5 0.0 copy-start.1
  7.5 0.0 copy-start.2
  7.5 0.6 %collective-permute-start.1 = (bf16[2,2,128,128]{3,2,1,0:T(8,128)(2,1)S(1)}, bf16[2,2,128,128]{3,2,1,0:T(8,128)(2,1)S(1)}, u32[]{:S(2)}, u32[]{:S(2)}) collective-permute-start(bf16[2,2,128,128]{3,2,1,0:T(8,128)(2,1)S(1)} %pad_maximum_fusion), channel_id=1, source_target_pairs={{0,8},{4,12},{8,0},{12,4},{16,24},{20,28},{24,16},{28,20},{1,9},{5... | collective-permute-start | bytes 393224 | tf_op jit(solution)/shard_map/ppermute | solution.py:309
  8.1 0.0 copy-start
  8.2 1.6 %collective-permute-start.2 = (bf16[2,2,128,128]{3,2,1,0:T(8,128)(2,1)S(1)}, bf16[2,2,128,128]{3,2,1,0:T(8,128)(2,1)S(1)}, u32[]{:S(2)}, u32[]{:S(2)}) collective-permute-start(bf16[2,2,128,128]{3,2,1,0:T(8,128)(2,1)S(1)} %pad_maximum_fusion.1), channel_id=1, source_target_pairs={{0,16},{4,20},{8,24},{12,28},{16,0},{20,4},{24,8},{28,12},{1,17},{... | collective-permute-start | bytes 393224 | tf_op jit(solution)/shard_map/ppermute | solution.py:309
  9.7 0.0 collective-permute-done.3.refs_2_
  9.7 2.2 %collective-permute-done.4.refs_3_ = bf16[2,128,128]{2,1,0:T(8,128)(2,1)S(1)} collective-permute-done((bf16[2,128,128]{2,1,0:T(8,128)(2,1)S(1)}, bf16[2,128,128]{2,1,0:T(8,128)(2,1)S(1)}, u32[]{:S(2)}, u32[]{:S(2)}) %collective-permute-start.4) | collective-permute-done | bytes 65568 | tf_op jit(solution)/shard_map/ppermute | solution.py:309
  11.9 0.0 copy-done.3
  11.9 0.0 copy-done.1
  11.9 0.0 copy-done.2
  11.9 1.0 %early.1 = (f32[4,128,512]{2,1,0:T(8,128)S(1)}, f32[2,2,128,512]{3,2,1,0:T(8,128)S(1)}, f32[4,128,512]{2,1,0:T(8,128)S(1)}, f32[4,128,512]{2,1,0:T(8,128)S(1)}) custom-call(bf16[4,2,128,128]{3,2,1,0:T(8,128)(2,1)S(1)} %get-tuple-element.24.refs_0_, bf16[4,2,128,128]{3,2,1,0:T(8,128)(2,1)S(1)} %collective-permute-done.refs_1_, ...), custom_call_target="tpu_custom_call" | custom-call | flops 2000000000 | tf_op jit(solution)/shard_map/early/pallas_call | solution.py:296
  12.9 0.3 collective-permute-done.1.refs_0_
  13.2 0.8 %collective-permute-done.2.refs_1_ = bf16[2,2,128,128]{3,2,1,0:T(8,128)(2,1)S(1)} collective-permute-done((bf16[2,2,128,128]{3,2,1,0:T(8,128)(2,1)S(1)}, bf16[2,2,128,128]{3,2,1,0:T(8,128)(2,1)S(1)}, u32[]{:S(2)}, u32[]{:S(2)}) %collective-permute-start.2) | collective-permute-done | bytes 131104 | tf_op jit(solution)/shard_map/ppermute | solution.py:309
  14.0 0.0 copy-done
  14.0 1.4 %sides.1 = (bf16[4,2,128,128]{3,2,1,0:T(8,128)(2,1)S(1)}, bf16[4,2,128,128]{3,2,1,0:T(8,128)(2,1)S(1)}, f32[2,2,128,512]{3,2,1,0:T(8,128)S(1)}) custom-call(bf16[2,2,128,128]{3,2,1,0:T(8,128)(2,1)S(1)} %collective-permute-done.1.refs_0_, bf16[2,2,128,128]{3,2,1,0:T(8,128)(2,1)S(1)} %collective-permute-done.2.refs_1_, ...), custom_call_target="tpu_custom_call" | custom-call | tf_op jit(solution)/shard_map/sides/pallas_call | solution.py:296
  15.4 0.1 collective-permute-start.5
  15.4 0.7 %lag.1 = bf16[4,128,256]{2,1,0:T(8,128)(2,1)S(1)} custom-call(f32[2,2,128,512]{3,2,1,0:T(8,128)S(1)} %get-tuple-element.35.refs_0_, f32[2,2,128,512]{3,2,1,0:T(8,128)S(1)} %get-tuple-element.36.refs_1_, bf16[512,256]{1,0:T(8,128)(2,1)S(1)} %copy-done, bf16[4,2,128,128]{3,2,1,0:T(8,128)(2,1)S(1)} %get-tuple-element.29.refs_3_), custom_call_target="tpu_custom_call" | custom-call | tf_op jit(solution)/shard_map/lag/pallas_call | solution.py:296
  16.2 0.8 %collective-permute-done.5 = bf16[4,2,128,128]{3,2,1,0:T(8,128)(2,1)S(1)} collective-permute-done((bf16[4,2,128,128]{3,2,1,0:T(8,128)(2,1)S(1)}, bf16[4,2,128,128]{3,2,1,0:T(8,128)(2,1)S(1)}, u32[]{:S(2)}, u32[]{:S(2)}) %collective-permute-start.5) | collective-permute-done | bytes 262176 | tf_op jit(solution)/shard_map/ppermute | solution.py:309
  17.0 1.6 %collective-permute-start.9 = (bf16[2,128,256]{2,1,0:T(8,128)(2,1)S(1)}, bf16[2,128,256]{2,1,0:T(8,128)(2,1)S(1)}, u32[]{:S(2)}, u32[]{:S(2)}) collective-permute-start(bf16[2,128,256]{2,1,0:T(8,128)(2,1)S(1)} %slice.70), channel_id=1, source_target_pairs={{0,1},{1,0},{2,3},{3,2},{4,5},{5,4},{6,7},{7,6},{8,9},{9,8},{10,11... | collective-permute-start | bytes 393224 | tf_op jit(solution)/shard_map/ppermute | solution.py:309
  18.7 1.7 %collective-permute-start.6 = (bf16[2,2,128,128]{3,2,1,0:T(8,128)(2,1)S(1)}, bf16[2,2,128,128]{3,2,1,0:T(8,128)(2,1)S(1)}, u32[]{:S(2)}, u32[]{:S(2)}) collective-permute-start(bf16[2,2,128,128]{3,2,1,0:T(8,128)(2,1)S(1)} %pad_maximum_fusion.2), channel_id=1, source_target_pairs={{0,24},{4,28},{8,16},{12,20},{16,8},{20,12},{24,0},{28,4},{1,25},{... | collective-permute-start | bytes 393224 | tf_op jit(solution)/shard_map/ppermute | solution.py:309
  20.3 0.7 %collective-permute-start.7 = (bf16[2,2,128,128]{3,2,1,0:T(8,128)(2,1)S(1)}, bf16[2,2,128,128]{3,2,1,0:T(8,128)(2,1)S(1)}, u32[]{:S(2)}, u32[]{:S(2)}) collective-permute-start(bf16[2,2,128,128]{3,2,1,0:T(8,128)(2,1)S(1)} %pad_maximum_fusion.3), channel_id=1, source_target_pairs={{0,16},{4,20},{8,24},{12,28},{16,0},{20,4},{24,8},{28,12},{1,17},{... | collective-permute-start | bytes 393224 | tf_op jit(solution)/shard_map/ppermute | solution.py:309
  21.1 1.3 %collective-permute-start.8 = (bf16[2,2,128,128]{3,2,1,0:T(8,128)(2,1)S(1)}, bf16[2,2,128,128]{3,2,1,0:T(8,128)(2,1)S(1)}, u32[]{:S(2)}, u32[]{:S(2)}) collective-permute-start(bf16[2,2,128,128]{3,2,1,0:T(8,128)(2,1)S(1)} %pad_maximum_fusion.4), channel_id=1, source_target_pairs={{0,8},{4,12},{8,0},{12,4},{16,24},{20,28},{24,16},{28,20},{1,9},{5... | collective-permute-start | bytes 393224 | tf_op jit(solution)/shard_map/ppermute | solution.py:309
  22.4 0.2 collective-permute-done.9
  22.6 2.7 %collective-permute-start.10 = (bf16[1,128,256]{2,1,0:T(8,128)(2,1)S(1)}, bf16[1,128,256]{2,1,0:T(8,128)(2,1)S(1)}, u32[]{:S(2)}, u32[]{:S(2)}) collective-permute-start(bf16[1,128,256]{2,1,0:T(8,128)(2,1)S(1)} %slice.86), channel_id=1, source_target_pairs={{0,2},{1,3},{2,0},{3,1},{4,6},{5,7},{6,4},{7,5},{8,10},{9,11},{10,... | collective-permute-start | bytes 196616 | tf_op jit(solution)/shard_map/ppermute | solution.py:309
  25.3 0.7 %collective-permute-done.6.refs_0_ = bf16[2,2,128,128]{3,2,1,0:T(8,128)(2,1)S(1)} collective-permute-done((bf16[2,2,128,128]{3,2,1,0:T(8,128)(2,1)S(1)}, bf16[2,2,128,128]{3,2,1,0:T(8,128)(2,1)S(1)}, u32[]{:S(2)}, u32[]{:S(2)}) %collective-permute-start.6) | collective-permute-done | bytes 131104 | tf_op jit(solution)/shard_map/ppermute | solution.py:309
  26.0 1.7 %collective-permute-done.7.refs_1_ = bf16[2,2,128,128]{3,2,1,0:T(8,128)(2,1)S(1)} collective-permute-done((bf16[2,2,128,128]{3,2,1,0:T(8,128)(2,1)S(1)}, bf16[2,2,128,128]{3,2,1,0:T(8,128)(2,1)S(1)}, u32[]{:S(2)}, u32[]{:S(2)}) %collective-permute-start.7) | collective-permute-done | bytes 131104 | tf_op jit(solution)/shard_map/ppermute | solution.py:309
  27.7 0.0 collective-permute-done.8.refs_2_
  27.7 0.2 collective-permute-done.10.refs_9_
  27.9 1.2 %grads.1 = (bf16[8,128,128]{2,1,0:T(8,128)(2,1)}, bf16[8,128,128]{2,1,0:T(8,128)(2,1)}, bf16[8,128,128]{2,1,0:T(8,128)(2,1)}, bf16[8,128,128]{2,1,0:T(8,128)(2,1)}, f32[128,256]{1,0:T(8,128)}) custom-call(bf16[2,2,128,128]{3,2,1,0:T(8,128)(2,1)S(1)} %collective-permute-done.6.refs_0_, bf16[2,2,128,128]{3,2,1,0:T(8,128)(2,1)S(1)} %collective-permute-done.7.refs_1_, ...), custom_call_target="tpu_custom_call" | custom-call | tf_op jit(solution)/shard_map/grads/pallas_call | solution.py:296
  (14 shorter events, 0.2 us)
Async XLA Ops:
  1.9 4.1 %collective-permute-start = (bf16[4,2,128,128]{3,2,1,0:T(8,128)(2,1)S(1)}, bf16[4,2,128,128]{3,2,1,0:T(8,128)(2,1)S(1)}, u32[]{:S(2)}, u32[]{:S(2)}) collective-permute-start(bf16[4,2,128,128]{3,2,1,0:T(8,128)(2,1)S(1)} %get-tuple-element.25), channel_id=1, source_target_pairs={{0,4},{4,0},{8,12},{12,8},{16,20},{20,16},{24,28},{28,24},{1,5},{5... | collective-permute-start | bytes 786440 | tf_op jit(solution)/shard_map/ppermute | solution.py:309
  2.5 7.3 %collective-permute-start.3 = (bf16[2,128,128]{2,1,0:T(8,128)(2,1)S(1)}, bf16[2,128,128]{2,1,0:T(8,128)(2,1)S(1)}, u32[]{:S(2)}, u32[]{:S(2)}) collective-permute-start(bf16[2,128,128]{2,1,0:T(8,128)(2,1)S(1)} %get-tuple-element.54), channel_id=1, source_target_pairs={{0,24},{4,28},{8,16},{12,20},{16,8},{20,12},{24,0},{28,4},{1,25},{... | collective-permute-start | bytes 196616 | tf_op jit(solution)/shard_map/ppermute | solution.py:309
  6.0 5.9 %copy-start.3 = (bf16[128,1024]{1,0:T(8,128)(2,1)S(1)}, bf16[128,1024]{1,0:T(8,128)(2,1)}, u32[]{:S(2)}) copy-start(bf16[128,1024]{1,0:T(8,128)(2,1)} %refs_4_.2) | copy-start | bytes 786436
  6.0 5.9 %collective-permute-start.4 = (bf16[2,128,128]{2,1,0:T(8,128)(2,1)S(1)}, bf16[2,128,128]{2,1,0:T(8,128)(2,1)S(1)}, u32[]{:S(2)}, u32[]{:S(2)}) collective-permute-start(bf16[2,128,128]{2,1,0:T(8,128)(2,1)S(1)} %get-tuple-element.51), channel_id=1, source_target_pairs={{0,24},{4,28},{8,16},{12,20},{16,8},{20,12},{24,0},{28,4},{1,25},{... | collective-permute-start | bytes 196616 | tf_op jit(solution)/shard_map/ppermute | solution.py:309
  7.5 4.4 %copy-start.1 = (bf16[256,512]{1,0:T(8,128)(2,1)S(1)}, bf16[256,512]{1,0:T(8,128)(2,1)}, u32[]{:S(2)}) copy-start(bf16[256,512]{1,0:T(8,128)(2,1)} %constant.7.clone.refs_6_.refs_4_) | copy-start | bytes 786436
  7.5 4.4 %copy-start.2 = (bf16[256,512]{1,0:T(8,128)(2,1)S(1)}, bf16[256,512]{1,0:T(8,128)(2,1)}, u32[]{:S(2)}) copy-start(bf16[256,512]{1,0:T(8,128)(2,1)} %constant.6.clone.refs_5_.refs_3_) | copy-start | bytes 786436
  7.5 5.7 %collective-permute-start.1 = (bf16[2,2,128,128]{3,2,1,0:T(8,128)(2,1)S(1)}, bf16[2,2,128,128]{3,2,1,0:T(8,128)(2,1)S(1)}, u32[]{:S(2)}, u32[]{:S(2)}) collective-permute-start(bf16[2,2,128,128]{3,2,1,0:T(8,128)(2,1)S(1)} %pad_maximum_fusion), channel_id=1, source_target_pairs={{0,8},{4,12},{8,0},{12,4},{16,24},{20,28},{24,16},{28,20},{1,9},{5... | collective-permute-start | bytes 393224 | tf_op jit(solution)/shard_map/ppermute | solution.py:309
  8.1 5.8 %copy-start = (bf16[512,256]{1,0:T(8,128)(2,1)S(1)}, bf16[512,256]{1,0:T(8,128)(2,1)}, u32[]{:S(2)}) copy-start(bf16[512,256]{1,0:T(8,128)(2,1)} %constant.8.clone.refs_5_.refs_2_) | copy-start | bytes 786436
  8.2 5.8 %collective-permute-start.2 = (bf16[2,2,128,128]{3,2,1,0:T(8,128)(2,1)S(1)}, bf16[2,2,128,128]{3,2,1,0:T(8,128)(2,1)S(1)}, u32[]{:S(2)}, u32[]{:S(2)}) collective-permute-start(bf16[2,2,128,128]{3,2,1,0:T(8,128)(2,1)S(1)} %pad_maximum_fusion.1), channel_id=1, source_target_pairs={{0,16},{4,20},{8,24},{12,28},{16,0},{20,4},{24,8},{28,12},{1,17},{... | collective-permute-start | bytes 393224 | tf_op jit(solution)/shard_map/ppermute | solution.py:309
  15.4 1.6 %collective-permute-start.5 = (bf16[4,2,128,128]{3,2,1,0:T(8,128)(2,1)S(1)}, bf16[4,2,128,128]{3,2,1,0:T(8,128)(2,1)S(1)}, u32[]{:S(2)}, u32[]{:S(2)}) collective-permute-start(bf16[4,2,128,128]{3,2,1,0:T(8,128)(2,1)S(1)} %get-tuple-element.30), channel_id=1, source_target_pairs={{0,4},{4,0},{8,12},{12,8},{16,20},{20,16},{24,28},{28,24},{1,5},{5... | collective-permute-start | bytes 786440 | tf_op jit(solution)/shard_map/ppermute | solution.py:309
  17.0 5.6 %collective-permute-start.9 = (bf16[2,128,256]{2,1,0:T(8,128)(2,1)S(1)}, bf16[2,128,256]{2,1,0:T(8,128)(2,1)S(1)}, u32[]{:S(2)}, u32[]{:S(2)}) collective-permute-start(bf16[2,128,256]{2,1,0:T(8,128)(2,1)S(1)} %slice.70), channel_id=1, source_target_pairs={{0,1},{1,0},{2,3},{3,2},{4,5},{5,4},{6,7},{7,6},{8,9},{9,8},{10,11... | collective-permute-start | bytes 393224 | tf_op jit(solution)/shard_map/ppermute | solution.py:309
  18.7 7.3 %collective-permute-start.6 = (bf16[2,2,128,128]{3,2,1,0:T(8,128)(2,1)S(1)}, bf16[2,2,128,128]{3,2,1,0:T(8,128)(2,1)S(1)}, u32[]{:S(2)}, u32[]{:S(2)}) collective-permute-start(bf16[2,2,128,128]{3,2,1,0:T(8,128)(2,1)S(1)} %pad_maximum_fusion.2), channel_id=1, source_target_pairs={{0,24},{4,28},{8,16},{12,20},{16,8},{20,12},{24,0},{28,4},{1,25},{... | collective-permute-start | bytes 393224 | tf_op jit(solution)/shard_map/ppermute | solution.py:309
  20.3 7.4 %collective-permute-start.7 = (bf16[2,2,128,128]{3,2,1,0:T(8,128)(2,1)S(1)}, bf16[2,2,128,128]{3,2,1,0:T(8,128)(2,1)S(1)}, u32[]{:S(2)}, u32[]{:S(2)}) collective-permute-start(bf16[2,2,128,128]{3,2,1,0:T(8,128)(2,1)S(1)} %pad_maximum_fusion.3), channel_id=1, source_target_pairs={{0,16},{4,20},{8,24},{12,28},{16,0},{20,4},{24,8},{28,12},{1,17},{... | collective-permute-start | bytes 393224 | tf_op jit(solution)/shard_map/ppermute | solution.py:309
  21.1 6.6 %collective-permute-start.8 = (bf16[2,2,128,128]{3,2,1,0:T(8,128)(2,1)S(1)}, bf16[2,2,128,128]{3,2,1,0:T(8,128)(2,1)S(1)}, u32[]{:S(2)}, u32[]{:S(2)}) collective-permute-start(bf16[2,2,128,128]{3,2,1,0:T(8,128)(2,1)S(1)} %pad_maximum_fusion.4), channel_id=1, source_target_pairs={{0,8},{4,12},{8,0},{12,4},{16,24},{20,28},{24,16},{28,20},{1,9},{5... | collective-permute-start | bytes 393224 | tf_op jit(solution)/shard_map/ppermute | solution.py:309
  22.6 5.3 %collective-permute-start.10 = (bf16[1,128,256]{2,1,0:T(8,128)(2,1)S(1)}, bf16[1,128,256]{2,1,0:T(8,128)(2,1)S(1)}, u32[]{:S(2)}, u32[]{:S(2)}) collective-permute-start(bf16[1,128,256]{2,1,0:T(8,128)(2,1)S(1)} %slice.86), channel_id=1, source_target_pairs={{0,2},{1,3},{2,0},{3,1},{4,6},{5,7},{6,4},{7,5},{8,10},{9,11},{10,... | collective-permute-start | bytes 196616 | tf_op jit(solution)/shard_map/ppermute | solution.py:309

commit v6 on v5

--- a/solution.py
+++ b/solution.py
@@ -260,10 +260,10 @@
 
 def grads_kernel(count, *refs):
     rows_refs = refs[:count][::-1]
-    query_ref, key_ref, value_ref, upstream_ref, kept_ref, sum_ref, *outs = refs[count:-5]
-    filter_out, held, sems, sums, sum_sem = refs[-5:]
+    query_ref, key_ref, value_ref, upstream_ref, *term_refs = refs[count:-9]
+    outs, (filter_out, held, sems, sums, sum_sem) = refs[-9:-5], refs[-5:]
     chip, core = place()
-    sums[...] = kept_ref[0].astype(jnp.float32) + sum_ref[0].astype(jnp.float32)
+    sums[...] = sum(ref[0].astype(jnp.float32) for ref in term_refs)
     copies = [pltpu.make_async_copy(sums, filter_out, sum_sem)]
     copies[0].start()
     for k in range(count):
@@ -319,15 +319,18 @@
     return first, [swap(jnp.stack([own[k], got[k]]), "seq", 2 * k) for k in rest]
 
 
-def scatter_sum(pieces):
+def scatter_sum(pieces, behind):
     size, step = pieces.shape[0], 1
-    while True:
+    if size == 4:
+        passed = swap(pieces[3:], "chan", 1)
+        stays = swap(pieces[2:3], "chan", 1)
+        onward = pieces[1:2].astype(jnp.float32) + passed.astype(jnp.float32)
+        return [pieces[:1], stays, swap(onward.astype(jnp.bfloat16), "chan", 2)]
+    while size > 2:
         kept, sent = pieces[: size // 2], pieces[size // 2 :].astype(jnp.bfloat16)
-        got = swap(sent, "chan", step)
-        if size == 2:
-            return kept, got
-        pieces = kept.astype(jnp.float32) + got.astype(jnp.float32)
+        pieces = kept.astype(jnp.float32) + swap(sent, "chan", step).astype(jnp.float32)
         size, step = size // 2, step * 2
+    return [pieces[:1], swap(pieces[1:].astype(jnp.bfloat16), "chan", step)]
 
 
 def on_device(query, key, value, upstream, taps):
@@ -380,12 +383,11 @@
         "lag",
         after=(own,),
     )
-    lag, _ = lax.optimization_barrier((lag, stay[1]))
-    kept, got = scatter_sum(lag)
+    terms = scatter_sum(lag, stay[1])
     sums = ((chans, length // chan), jnp.float32)
     *outs, filter_grad = call(
         functools.partial(grads_kernel, count),
-        (*rows, jnp.stack([stay[0][0], stay[1][0]]), query, key, value, upstream, kept, got),
+        (*rows, jnp.stack([stay[0][0], stay[1][0]]), query, key, value, upstream, *terms),
         (whole,) * 4 + (sums,),
         [
             pltpu.VMEM((4, seq, chans, positions), jnp.bfloat16),

time: 29.3 us -> 28.8 us (0.983)
  waiting for transfers between devices: 6.78 us -> 5.88 us
  starting transfers between devices: 15.8 us -> 16.2 us
    ppermute x11 -> x12, waiting for transfers between devices: 6.78 us -> 5.88 us  [swap(): lax.ppermute(array, axis, [(i, i ^ k) for i in range(lax.axis_size(axis))])]
    ppermute x11 -> x12, starting transfers between devices: 15.8 us -> 16.2 us  [swap(): lax.ppermute(array, axis, [(i, i ^ k) for i in range(lax.axis_size(axis))])]
  transfers between devices with their start and end apart: 11 -> 12, of which waited for: 8 -> 5; matrix products, arithmetic and copies ran while one was open for 1% -> 1% of each run, Pallas kernels for 6% -> 6%
where the time goes in v6:
time: 28.8 us; the launch traced here: 28.7 us
  starting transfers between devices  16.2 us (56%)
  waiting for transfers between devices  5.88 us (20%)
  Pallas kernels  5.59 us (19%)
  between operations  0.76 us (3%)
    ppermute x12, starting transfers between devices, swap(): lax.ppermute(array, axis, [(i, i ^ k) for i in range(lax.axis_size(axis))])  16.2 us
    ppermute x12, waiting for transfers between devices, swap(): lax.ppermute(array, axis, [(i, i ^ k) for i in range(lax.axis_size(axis))])  5.88 us
    pallas_call x5, Pallas kernels, call(): pl.pallas_call(body, out_shape=tuple((jax.ShapeDtypeStruct(shape, kind) f...  5.59 us
  transfers between devices with their start and end apart: 12, of which 5 were waited for; matrix products, arithmetic and copies ran while one was open for 1% of the time, Pallas kernels for 6%

profile of v6, /device:TPU:0, one launch (start us, length us, event | category | flops | bytes accessed | tf_op | source)
XLA Modules:
  0.0 28.7 jit_solution(16265041099765939016)
XLA Ops:
  0.6 1.3 %gate.1 = (bf16[8,128,128]{2,1,0:T(8,128)(2,1)S(1)}, bf16[8,128,128]{2,1,0:T(8,128)(2,1)S(1)}, bf16[8,128,128]{2,1,0:T(8,128)(2,1)S(1)}, bf16[8,128,128]{2,1,0:T...) custom-call(bf16[8,128,128]{2,1,0:T(8,128)(2,1)} %bitcast.12, ...), custom_call_target="tpu_custom_call" | custom-call | tf_op jit(solution)/shard_map/gate/pallas_call | solution.py:296
  1.9 0.5 %collective-permute-start = (bf16[4,2,128,128]{3,2,1,0:T(8,128)(2,1)S(1)}, bf16[4,2,128,128]{3,2,1,0:T(8,128)(2,1)S(1)}, u32[]{:S(2)}, u32[]{:S(2)}) collective-permute-start(bf16[4,2,128,128]{3,2,1,0:T(8,128)(2,1)S(1)} %get-tuple-element.24), channel_id=1, source_target_pairs={{0,4},{4,0},{8,12},{12,8},{16,20},{20,16},{24,28},{28,24},{1,5},{5... | collective-permute-start | bytes 786440 | tf_op jit(solution)/shard_map/ppermute | solution.py:309
  2.5 3.5 %collective-permute-start.3 = (bf16[2,128,128]{2,1,0:T(8,128)(2,1)S(1)}, bf16[2,128,128]{2,1,0:T(8,128)(2,1)S(1)}, u32[]{:S(2)}, u32[]{:S(2)}) collective-permute-start(bf16[2,128,128]{2,1,0:T(8,128)(2,1)S(1)} %get-tuple-element.55), channel_id=1, source_target_pairs={{0,24},{4,28},{8,16},{12,20},{16,8},{20,12},{24,0},{28,4},{1,25},{... | collective-permute-start | bytes 196616 | tf_op jit(solution)/shard_map/ppermute | solution.py:309
  6.0 0.0 collective-permute-done.refs_1_
  6.0 0.0 copy-start.3
  6.0 1.5 %collective-permute-start.4 = (bf16[2,128,128]{2,1,0:T(8,128)(2,1)S(1)}, bf16[2,128,128]{2,1,0:T(8,128)(2,1)S(1)}, u32[]{:S(2)}, u32[]{:S(2)}) collective-permute-start(bf16[2,128,128]{2,1,0:T(8,128)(2,1)S(1)} %get-tuple-element.52), channel_id=1, source_target_pairs={{0,24},{4,28},{8,16},{12,20},{16,8},{20,12},{24,0},{28,4},{1,25},{... | collective-permute-start | bytes 196616 | tf_op jit(solution)/shard_map/ppermute | solution.py:309
  7.5 0.0 copy-start.1
  7.5 0.0 copy-start.2
  7.5 0.6 %collective-permute-start.1 = (bf16[2,2,128,128]{3,2,1,0:T(8,128)(2,1)S(1)}, bf16[2,2,128,128]{3,2,1,0:T(8,128)(2,1)S(1)}, u32[]{:S(2)}, u32[]{:S(2)}) collective-permute-start(bf16[2,2,128,128]{3,2,1,0:T(8,128)(2,1)S(1)} %pad_maximum_fusion), channel_id=1, source_target_pairs={{0,8},{4,12},{8,0},{12,4},{16,24},{20,28},{24,16},{28,20},{1,9},{5... | collective-permute-start | bytes 393224 | tf_op jit(solution)/shard_map/ppermute | solution.py:309
  8.1 0.0 copy-start
  8.2 1.6 %collective-permute-start.2 = (bf16[2,2,128,128]{3,2,1,0:T(8,128)(2,1)S(1)}, bf16[2,2,128,128]{3,2,1,0:T(8,128)(2,1)S(1)}, u32[]{:S(2)}, u32[]{:S(2)}) collective-permute-start(bf16[2,2,128,128]{3,2,1,0:T(8,128)(2,1)S(1)} %pad_maximum_fusion.1), channel_id=1, source_target_pairs={{0,16},{4,20},{8,24},{12,28},{16,0},{20,4},{24,8},{28,12},{1,17},{... | collective-permute-start | bytes 393224 | tf_op jit(solution)/shard_map/ppermute | solution.py:309
  9.7 0.0 collective-permute-done.3.refs_2_
  9.7 2.2 %collective-permute-done.4.refs_3_ = bf16[2,128,128]{2,1,0:T(8,128)(2,1)S(1)} collective-permute-done((bf16[2,128,128]{2,1,0:T(8,128)(2,1)S(1)}, bf16[2,128,128]{2,1,0:T(8,128)(2,1)S(1)}, u32[]{:S(2)}, u32[]{:S(2)}) %collective-permute-start.4) | collective-permute-done | bytes 65568 | tf_op jit(solution)/shard_map/ppermute | solution.py:309
  11.9 0.0 copy-done.3
  11.9 0.0 copy-done.1
  11.9 0.0 copy-done.2
  11.9 1.0 %early.1 = (f32[4,128,512]{2,1,0:T(8,128)S(1)}, f32[2,2,128,512]{3,2,1,0:T(8,128)S(1)}, f32[4,128,512]{2,1,0:T(8,128)S(1)}, f32[4,128,512]{2,1,0:T(8,128)S(1)}) custom-call(bf16[4,2,128,128]{3,2,1,0:T(8,128)(2,1)S(1)} %get-tuple-element.23.refs_0_, bf16[4,2,128,128]{3,2,1,0:T(8,128)(2,1)S(1)} %collective-permute-done.refs_1_, ...), custom_call_target="tpu_custom_call" | custom-call | flops 2000000000 | tf_op jit(solution)/shard_map/early/pallas_call | solution.py:296
  12.9 0.3 collective-permute-done.1.refs_0_
  13.2 0.8 %collective-permute-done.2.refs_1_ = bf16[2,2,128,128]{3,2,1,0:T(8,128)(2,1)S(1)} collective-permute-done((bf16[2,2,128,128]{3,2,1,0:T(8,128)(2,1)S(1)}, bf16[2,2,128,128]{3,2,1,0:T(8,128)(2,1)S(1)}, u32[]{:S(2)}, u32[]{:S(2)}) %collective-permute-start.2) | collective-permute-done | bytes 131104 | tf_op jit(solution)/shard_map/ppermute | solution.py:309
  14.0 0.0 copy-done
  14.0 1.4 %sides.1 = (bf16[4,2,128,128]{3,2,1,0:T(8,128)(2,1)S(1)}, bf16[4,2,128,128]{3,2,1,0:T(8,128)(2,1)S(1)}, f32[2,2,128,512]{3,2,1,0:T(8,128)S(1)}) custom-call(bf16[2,2,128,128]{3,2,1,0:T(8,128)(2,1)S(1)} %collective-permute-done.1.refs_0_, bf16[2,2,128,128]{3,2,1,0:T(8,128)(2,1)S(1)} %collective-permute-done.2.refs_1_, ...), custom_call_target="tpu_custom_call" | custom-call | tf_op jit(solution)/shard_map/sides/pallas_call | solution.py:296
  15.4 0.1 collective-permute-start.5
  15.4 0.7 %lag.1 = bf16[4,128,256]{2,1,0:T(8,128)(2,1)S(1)} custom-call(f32[2,2,128,512]{3,2,1,0:T(8,128)S(1)} %get-tuple-element.34.refs_0_, f32[2,2,128,512]{3,2,1,0:T(8,128)S(1)} %get-tuple-element.35.refs_1_, bf16[512,256]{1,0:T(8,128)(2,1)S(1)} %copy-done, bf16[4,2,128,128]{3,2,1,0:T(8,128)(2,1)S(1)} %get-tuple-element.28.refs_3_), custom_call_target="tpu_custom_call" | custom-call | tf_op jit(solution)/shard_map/lag/pallas_call | solution.py:296
  16.2 1.6 %collective-permute-start.10 = (bf16[1,128,256]{2,1,0:T(8,128)(2,1)S(1)}, bf16[1,128,256]{2,1,0:T(8,128)(2,1)S(1)}, u32[]{:S(2)}, u32[]{:S(2)}) collective-permute-start(bf16[1,128,256]{2,1,0:T(8,128)(2,1)S(1)} %get-tuple-element.41), channel_id=1, source_target_pairs={{0,1},{1,0},{2,3},{3,2},{4,5},{5,4},{6,7},{7,6},{8,9},{9,8},{10,11... | collective-permute-start | bytes 196616 | tf_op jit(solution)/shard_map/ppermute | solution.py:309
  17.8 0.4 %collective-permute-start.9 = (bf16[1,128,256]{2,1,0:T(8,128)(2,1)S(1)}, bf16[1,128,256]{2,1,0:T(8,128)(2,1)S(1)}, u32[]{:S(2)}, u32[]{:S(2)}) collective-permute-start(bf16[1,128,256]{2,1,0:T(8,128)(2,1)S(1)} %get-tuple-element.42), channel_id=1, source_target_pairs={{0,1},{1,0},{2,3},{3,2},{4,5},{5,4},{6,7},{7,6},{8,9},{9,8},{10,11... | collective-permute-start | bytes 196616 | tf_op jit(solution)/shard_map/ppermute | solution.py:309
  18.3 0.0 collective-permute-done.5
  18.4 1.7 %collective-permute-start.6 = (bf16[2,2,128,128]{3,2,1,0:T(8,128)(2,1)S(1)}, bf16[2,2,128,128]{3,2,1,0:T(8,128)(2,1)S(1)}, u32[]{:S(2)}, u32[]{:S(2)}) collective-permute-start(bf16[2,2,128,128]{3,2,1,0:T(8,128)(2,1)S(1)} %pad_maximum_fusion.2), channel_id=1, source_target_pairs={{0,24},{4,28},{8,16},{12,20},{16,8},{20,12},{24,0},{28,4},{1,25},{... | collective-permute-start | bytes 393224 | tf_op jit(solution)/shard_map/ppermute | solution.py:309
  20.1 0.7 %collective-permute-start.7 = (bf16[2,2,128,128]{3,2,1,0:T(8,128)(2,1)S(1)}, bf16[2,2,128,128]{3,2,1,0:T(8,128)(2,1)S(1)}, u32[]{:S(2)}, u32[]{:S(2)}) collective-permute-start(bf16[2,2,128,128]{3,2,1,0:T(8,128)(2,1)S(1)} %pad_maximum_fusion.3), channel_id=1, source_target_pairs={{0,16},{4,20},{8,24},{12,28},{16,0},{20,4},{24,8},{28,12},{1,17},{... | collective-permute-start | bytes 393224 | tf_op jit(solution)/shard_map/ppermute | solution.py:309
  20.8 1.3 %collective-permute-start.8 = (bf16[2,2,128,128]{3,2,1,0:T(8,128)(2,1)S(1)}, bf16[2,2,128,128]{3,2,1,0:T(8,128)(2,1)S(1)}, u32[]{:S(2)}, u32[]{:S(2)}) collective-permute-start(bf16[2,2,128,128]{3,2,1,0:T(8,128)(2,1)S(1)} %pad_maximum_fusion.4), channel_id=1, source_target_pairs={{0,8},{4,12},{8,0},{12,4},{16,24},{20,28},{24,16},{28,20},{1,9},{5... | collective-permute-start | bytes 393224 | tf_op jit(solution)/shard_map/ppermute | solution.py:309
  22.1 0.0 collective-permute-done.10
  22.1 2.7 %collective-permute-start.11 = (bf16[1,128,256]{2,1,0:T(8,128)(2,1)S(1)}, bf16[1,128,256]{2,1,0:T(8,128)(2,1)S(1)}, u32[]{:S(2)}, u32[]{:S(2)}) collective-permute-start(bf16[1,128,256]{2,1,0:T(8,128)(2,1)S(1)} %add_convert_fusion), channel_id=1, source_target_pairs={{0,2},{1,3},{2,0},{3,1},{4,6},{5,7},{6,4},{7,5},{8,10},{9,11},{10,... | collective-permute-start | bytes 196616 | tf_op jit(solution)/shard_map/ppermute | solution.py:309
  24.8 0.0 collective-permute-done.9.refs_9_
  24.8 2.5 %collective-permute-done.11.refs_10_ = bf16[1,128,256]{2,1,0:T(8,128)(2,1)S(1)} collective-permute-done((bf16[1,128,256]{2,1,0:T(8,128)(2,1)S(1)}, bf16[1,128,256]{2,1,0:T(8,128)(2,1)S(1)}, u32[]{:S(2)}, u32[]{:S(2)}) %collective-permute-start.11) | collective-permute-done | bytes 65568 | tf_op jit(solution)/shard_map/ppermute | solution.py:309
  27.3 0.0 collective-permute-done.6.refs_0_
  27.3 0.1 collective-permute-done.7.refs_1_
  27.4 0.0 collective-permute-done.8.refs_2_
  27.5 1.2 %grads.1 = (bf16[8,128,128]{2,1,0:T(8,128)(2,1)}, bf16[8,128,128]{2,1,0:T(8,128)(2,1)}, bf16[8,128,128]{2,1,0:T(8,128)(2,1)}, bf16[8,128,128]{2,1,0:T(8,128)(2,1)}, f32[128,256]{1,0:T(8,128)}) custom-call(bf16[2,2,128,128]{3,2,1,0:T(8,128)(2,1)S(1)} %collective-permute-done.6.refs_0_, bf16[2,2,128,128]{3,2,1,0:T(8,128)(2,1)S(1)} %collective-permute-done.7.refs_1_, ...), custom_call_target="tpu_custom_call" | custom-call | tf_op jit(solution)/shard_map/grads/pallas_call | solution.py:296
  (12 shorter events, 0.2 us)
Async XLA Ops:
  1.9 4.1 %collective-permute-start = (bf16[4,2,128,128]{3,2,1,0:T(8,128)(2,1)S(1)}, bf16[4,2,128,128]{3,2,1,0:T(8,128)(2,1)S(1)}, u32[]{:S(2)}, u32[]{:S(2)}) collective-permute-start(bf16[4,2,128,128]{3,2,1,0:T(8,128)(2,1)S(1)} %get-tuple-element.24), channel_id=1, source_target_pairs={{0,4},{4,0},{8,12},{12,8},{16,20},{20,16},{24,28},{28,24},{1,5},{5... | collective-permute-start | bytes 786440 | tf_op jit(solution)/shard_map/ppermute | solution.py:309
  2.5 7.3 %collective-permute-start.3 = (bf16[2,128,128]{2,1,0:T(8,128)(2,1)S(1)}, bf16[2,128,128]{2,1,0:T(8,128)(2,1)S(1)}, u32[]{:S(2)}, u32[]{:S(2)}) collective-permute-start(bf16[2,128,128]{2,1,0:T(8,128)(2,1)S(1)} %get-tuple-element.55), channel_id=1, source_target_pairs={{0,24},{4,28},{8,16},{12,20},{16,8},{20,12},{24,0},{28,4},{1,25},{... | collective-permute-start | bytes 196616 | tf_op jit(solution)/shard_map/ppermute | solution.py:309
  6.0 5.9 %copy-start.3 = (bf16[128,1024]{1,0:T(8,128)(2,1)S(1)}, bf16[128,1024]{1,0:T(8,128)(2,1)}, u32[]{:S(2)}) copy-start(bf16[128,1024]{1,0:T(8,128)(2,1)} %refs_4_.2) | copy-start | bytes 786436
  6.0 5.9 %collective-permute-start.4 = (bf16[2,128,128]{2,1,0:T(8,128)(2,1)S(1)}, bf16[2,128,128]{2,1,0:T(8,128)(2,1)S(1)}, u32[]{:S(2)}, u32[]{:S(2)}) collective-permute-start(bf16[2,128,128]{2,1,0:T(8,128)(2,1)S(1)} %get-tuple-element.52), channel_id=1, source_target_pairs={{0,24},{4,28},{8,16},{12,20},{16,8},{20,12},{24,0},{28,4},{1,25},{... | collective-permute-start | bytes 196616 | tf_op jit(solution)/shard_map/ppermute | solution.py:309
  7.5 4.4 %copy-start.1 = (bf16[256,512]{1,0:T(8,128)(2,1)S(1)}, bf16[256,512]{1,0:T(8,128)(2,1)}, u32[]{:S(2)}) copy-start(bf16[256,512]{1,0:T(8,128)(2,1)} %constant.7.clone.refs_6_.refs_4_) | copy-start | bytes 786436
  7.5 4.4 %copy-start.2 = (bf16[256,512]{1,0:T(8,128)(2,1)S(1)}, bf16[256,512]{1,0:T(8,128)(2,1)}, u32[]{:S(2)}) copy-start(bf16[256,512]{1,0:T(8,128)(2,1)} %constant.6.clone.refs_5_.refs_3_) | copy-start | bytes 786436
  7.5 5.7 %collective-permute-start.1 = (bf16[2,2,128,128]{3,2,1,0:T(8,128)(2,1)S(1)}, bf16[2,2,128,128]{3,2,1,0:T(8,128)(2,1)S(1)}, u32[]{:S(2)}, u32[]{:S(2)}) collective-permute-start(bf16[2,2,128,128]{3,2,1,0:T(8,128)(2,1)S(1)} %pad_maximum_fusion), channel_id=1, source_target_pairs={{0,8},{4,12},{8,0},{12,4},{16,24},{20,28},{24,16},{28,20},{1,9},{5... | collective-permute-start | bytes 393224 | tf_op jit(solution)/shard_map/ppermute | solution.py:309
  8.1 5.8 %copy-start = (bf16[512,256]{1,0:T(8,128)(2,1)S(1)}, bf16[512,256]{1,0:T(8,128)(2,1)}, u32[]{:S(2)}) copy-start(bf16[512,256]{1,0:T(8,128)(2,1)} %constant.8.clone.refs_5_.refs_2_) | copy-start | bytes 786436
  8.2 5.8 %collective-permute-start.2 = (bf16[2,2,128,128]{3,2,1,0:T(8,128)(2,1)S(1)}, bf16[2,2,128,128]{3,2,1,0:T(8,128)(2,1)S(1)}, u32[]{:S(2)}, u32[]{:S(2)}) collective-permute-start(bf16[2,2,128,128]{3,2,1,0:T(8,128)(2,1)S(1)} %pad_maximum_fusion.1), channel_id=1, source_target_pairs={{0,16},{4,20},{8,24},{12,28},{16,0},{20,4},{24,8},{28,12},{1,17},{... | collective-permute-start | bytes 393224 | tf_op jit(solution)/shard_map/ppermute | solution.py:309
  15.4 2.9 %collective-permute-start.5 = (bf16[4,2,128,128]{3,2,1,0:T(8,128)(2,1)S(1)}, bf16[4,2,128,128]{3,2,1,0:T(8,128)(2,1)S(1)}, u32[]{:S(2)}, u32[]{:S(2)}) collective-permute-start(bf16[4,2,128,128]{3,2,1,0:T(8,128)(2,1)S(1)} %get-tuple-element.29), channel_id=1, source_target_pairs={{0,4},{4,0},{8,12},{12,8},{16,20},{20,16},{24,28},{28,24},{1,5},{5... | collective-permute-start | bytes 786440 | tf_op jit(solution)/shard_map/ppermute | solution.py:309
  16.2 5.9 %collective-permute-start.10 = (bf16[1,128,256]{2,1,0:T(8,128)(2,1)S(1)}, bf16[1,128,256]{2,1,0:T(8,128)(2,1)S(1)}, u32[]{:S(2)}, u32[]{:S(2)}) collective-permute-start(bf16[1,128,256]{2,1,0:T(8,128)(2,1)S(1)} %get-tuple-element.41), channel_id=1, source_target_pairs={{0,1},{1,0},{2,3},{3,2},{4,5},{5,4},{6,7},{7,6},{8,9},{9,8},{10,11... | collective-permute-start | bytes 196616 | tf_op jit(solution)/shard_map/ppermute | solution.py:309
  17.8 7.0 %collective-permute-start.9 = (bf16[1,128,256]{2,1,0:T(8,128)(2,1)S(1)}, bf16[1,128,256]{2,1,0:T(8,128)(2,1)S(1)}, u32[]{:S(2)}, u32[]{:S(2)}) collective-permute-start(bf16[1,128,256]{2,1,0:T(8,128)(2,1)S(1)} %get-tuple-element.42), channel_id=1, source_target_pairs={{0,1},{1,0},{2,3},{3,2},{4,5},{5,4},{6,7},{7,6},{8,9},{9,8},{10,11... | collective-permute-start | bytes 196616 | tf_op jit(solution)/shard_map/ppermute | solution.py:309
  18.4 9.0 %collective-permute-start.6 = (bf16[2,2,128,128]{3,2,1,0:T(8,128)(2,1)S(1)}, bf16[2,2,128,128]{3,2,1,0:T(8,128)(2,1)S(1)}, u32[]{:S(2)}, u32[]{:S(2)}) collective-permute-start(bf16[2,2,128,128]{3,2,1,0:T(8,128)(2,1)S(1)} %pad_maximum_fusion.2), channel_id=1, source_target_pairs={{0,24},{4,28},{8,16},{12,20},{16,8},{20,12},{24,0},{28,4},{1,25},{... | collective-permute-start | bytes 393224 | tf_op jit(solution)/shard_map/ppermute | solution.py:309
  20.1 7.4 %collective-permute-start.7 = (bf16[2,2,128,128]{3,2,1,0:T(8,128)(2,1)S(1)}, bf16[2,2,128,128]{3,2,1,0:T(8,128)(2,1)S(1)}, u32[]{:S(2)}, u32[]{:S(2)}) collective-permute-start(bf16[2,2,128,128]{3,2,1,0:T(8,128)(2,1)S(1)} %pad_maximum_fusion.3), channel_id=1, source_target_pairs={{0,16},{4,20},{8,24},{12,28},{16,0},{20,4},{24,8},{28,12},{1,17},{... | collective-permute-start | bytes 393224 | tf_op jit(solution)/shard_map/ppermute | solution.py:309
  20.8 6.7 %collective-permute-start.8 = (bf16[2,2,128,128]{3,2,1,0:T(8,128)(2,1)S(1)}, bf16[2,2,128,128]{3,2,1,0:T(8,128)(2,1)S(1)}, u32[]{:S(2)}, u32[]{:S(2)}) collective-permute-start(bf16[2,2,128,128]{3,2,1,0:T(8,128)(2,1)S(1)} %pad_maximum_fusion.4), channel_id=1, source_target_pairs={{0,8},{4,12},{8,0},{12,4},{16,24},{20,28},{24,16},{28,20},{1,9},{5... | collective-permute-start | bytes 393224 | tf_op jit(solution)/shard_map/ppermute | solution.py:309
  22.1 5.2 %collective-permute-start.11 = (bf16[1,128,256]{2,1,0:T(8,128)(2,1)S(1)}, bf16[1,128,256]{2,1,0:T(8,128)(2,1)S(1)}, u32[]{:S(2)}, u32[]{:S(2)}) collective-permute-start(bf16[1,128,256]{2,1,0:T(8,128)(2,1)S(1)} %add_convert_fusion), channel_id=1, source_target_pairs={{0,2},{1,3},{2,0},{3,1},{4,6},{5,7},{6,4},{7,5},{8,10},{9,11},{10,... | collective-permute-start | bytes 196616 | tf_op jit(solution)/shard_map/ppermute | solution.py:309

commit v7 on v6

--- a/solution.py
+++ b/solution.py
@@ -193,12 +193,20 @@
     on_cases(count, work)
 
 
+def next_kernel(part_ref, high_ref, low_ref, wave_ref):
+    for i in range(2):
+        wave_ref[i] = transform((part_ref.at[0], part_ref.at[1]), i, high_ref, low_ref)
+
+
 def sides_kernel(count, *refs):
-    pieces, refs = pieces_of(refs, count, late(count))
+    done = refs[:1] if early(count) else ()
+    pieces, refs = pieces_of(refs[len(done) :], count, late(count)[len(done) :])
     filt_ref, high_ref, low_ref, inv_ref, *refs = refs
     parts, (own_ref, other_ref, wave_ref, prod) = refs[:-4], refs[-4:]
     chip, core = place()
-    for at, (k, pair) in enumerate(pieces):
+    for ref in done:
+        wave_ref[0] = ref[...]
+    for at, (k, pair) in enumerate(pieces, len(done)):
         for i in range(2):
             wave_ref[at if early(count) else chip ^ k, i] = transform(pair, i, high_ref, low_ref)
 
@@ -365,6 +373,8 @@
         flops=int(2e9),
     )
     waves = ((len(late(count)), 2, chans, 2 * BLOCK), jnp.float32)
+    if early(count):
+        rest[:1] = call(next_kernel, (rest[0], high, low), (((2, *waves[0][2:]), jnp.float32),), [], "next", flops=0)
     prod = pltpu.VMEM((count, chans, 2 * BLOCK), jnp.bfloat16)
     own, other, late_waves = call(
         functools.partial(sides_kernel, count),

time: 28.8 us -> 28.7 us (level)
  waiting for transfers between devices: 5.88 us -> 5.58 us
    ppermute x12, waiting for transfers between devices: 5.88 us -> 5.58 us  [swap(): lax.ppermute(array, axis, [(i, i ^ k) for i in range(lax.axis_size(axis))])]
    pallas_call x5 -> x6, Pallas kernels: 5.59 us -> 5.8 us  [call(): pl.pallas_call(body, out_shape=tuple((jax.ShapeDtypeStruct(shape, kind) f...]
  transfers between devices with their start and end apart: 12 -> 12, of which waited for: 5 -> 5; matrix products, arithmetic and copies ran while one was open for 1% -> 1% of each run, Pallas kernels for 6% -> 7%
where the time goes in v7:
time: 28.7 us; the launch traced here: 28.6 us
  starting transfers between devices  16.2 us (56%)
  Pallas kernels  5.8 us (20%)
  waiting for transfers between devices  5.58 us (19%)
  between operations  0.77 us (3%)
    ppermute x12, starting transfers between devices, swap(): lax.ppermute(array, axis, [(i, i ^ k) for i in range(lax.axis_size(axis))])  16.2 us
    pallas_call x6, Pallas kernels, call(): pl.pallas_call(body, out_shape=tuple((jax.ShapeDtypeStruct(shape, kind) f...  5.8 us
    ppermute x12, waiting for transfers between devices, swap(): lax.ppermute(array, axis, [(i, i ^ k) for i in range(lax.axis_size(axis))])  5.58 us
  transfers between devices with their start and end apart: 12, of which 5 were waited for; matrix products, arithmetic and copies ran while one was open for 1% of the time, Pallas kernels for 7%

profile of v7, /device:TPU:0, one launch (start us, length us, event | category | flops | bytes accessed | tf_op | source)
XLA Modules:
  0.0 28.6 jit_solution(18387108643956587999)
XLA Ops:
  0.6 1.3 %gate.1 = (bf16[8,128,128]{2,1,0:T(8,128)(2,1)S(1)}, bf16[8,128,128]{2,1,0:T(8,128)(2,1)S(1)}, bf16[8,128,128]{2,1,0:T(8,128)(2,1)S(1)}, bf16[8,128,128]{2,1,0:T...) custom-call(bf16[8,128,128]{2,1,0:T(8,128)(2,1)} %bitcast.12, ...), custom_call_target="tpu_custom_call" | custom-call | tf_op jit(solution)/shard_map/gate/pallas_call | solution.py:304
  1.9 0.5 %collective-permute-start = (bf16[4,2,128,128]{3,2,1,0:T(8,128)(2,1)S(1)}, bf16[4,2,128,128]{3,2,1,0:T(8,128)(2,1)S(1)}, u32[]{:S(2)}, u32[]{:S(2)}) collective-permute-start(bf16[4,2,128,128]{3,2,1,0:T(8,128)(2,1)S(1)} %get-tuple-element.24), channel_id=1, source_target_pairs={{0,4},{4,0},{8,12},{12,8},{16,20},{20,16},{24,28},{28,24},{1,5},{5... | collective-permute-start | bytes 786440 | tf_op jit(solution)/shard_map/ppermute | solution.py:317
  2.5 3.5 %collective-permute-start.3 = (bf16[2,128,128]{2,1,0:T(8,128)(2,1)S(1)}, bf16[2,128,128]{2,1,0:T(8,128)(2,1)S(1)}, u32[]{:S(2)}, u32[]{:S(2)}) collective-permute-start(bf16[2,128,128]{2,1,0:T(8,128)(2,1)S(1)} %get-tuple-element.55), channel_id=1, source_target_pairs={{0,24},{4,28},{8,16},{12,20},{16,8},{20,12},{24,0},{28,4},{1,25},{... | collective-permute-start | bytes 196616 | tf_op jit(solution)/shard_map/ppermute | solution.py:317
  6.0 0.0 collective-permute-done.refs_1_
  6.0 0.0 copy-start.3
  6.0 1.5 %collective-permute-start.4 = (bf16[2,128,128]{2,1,0:T(8,128)(2,1)S(1)}, bf16[2,128,128]{2,1,0:T(8,128)(2,1)S(1)}, u32[]{:S(2)}, u32[]{:S(2)}) collective-permute-start(bf16[2,128,128]{2,1,0:T(8,128)(2,1)S(1)} %get-tuple-element.52), channel_id=1, source_target_pairs={{0,24},{4,28},{8,16},{12,20},{16,8},{20,12},{24,0},{28,4},{1,25},{... | collective-permute-start | bytes 196616 | tf_op jit(solution)/shard_map/ppermute | solution.py:317
  7.5 0.0 copy-start
  7.5 0.0 copy-start.1
  7.5 0.6 %collective-permute-start.1 = (bf16[2,2,128,128]{3,2,1,0:T(8,128)(2,1)S(1)}, bf16[2,2,128,128]{3,2,1,0:T(8,128)(2,1)S(1)}, u32[]{:S(2)}, u32[]{:S(2)}) collective-permute-start(bf16[2,2,128,128]{3,2,1,0:T(8,128)(2,1)S(1)} %pad_maximum_fusion), channel_id=1, source_target_pairs={{0,8},{4,12},{8,0},{12,4},{16,24},{20,28},{24,16},{28,20},{1,9},{5... | collective-permute-start | bytes 393224 | tf_op jit(solution)/shard_map/ppermute | solution.py:317
  8.1 1.6 %collective-permute-start.2 = (bf16[2,2,128,128]{3,2,1,0:T(8,128)(2,1)S(1)}, bf16[2,2,128,128]{3,2,1,0:T(8,128)(2,1)S(1)}, u32[]{:S(2)}, u32[]{:S(2)}) collective-permute-start(bf16[2,2,128,128]{3,2,1,0:T(8,128)(2,1)S(1)} %pad_maximum_fusion.1), channel_id=1, source_target_pairs={{0,16},{4,20},{8,24},{12,28},{16,0},{20,4},{24,8},{28,12},{1,17},{... | collective-permute-start | bytes 393224 | tf_op jit(solution)/shard_map/ppermute | solution.py:317
  9.7 0.0 collective-permute-done.3.refs_2_
  9.7 2.2 %collective-permute-done.4.refs_3_ = bf16[2,128,128]{2,1,0:T(8,128)(2,1)S(1)} collective-permute-done((bf16[2,128,128]{2,1,0:T(8,128)(2,1)S(1)}, bf16[2,128,128]{2,1,0:T(8,128)(2,1)S(1)}, u32[]{:S(2)}, u32[]{:S(2)}) %collective-permute-start.4) | collective-permute-done | bytes 65568 | tf_op jit(solution)/shard_map/ppermute | solution.py:317
  11.9 0.0 copy-done.3
  11.9 0.0 copy-done
  11.9 0.0 copy-done.1
  11.9 1.0 %early.1 = (f32[4,128,512]{2,1,0:T(8,128)S(1)}, f32[2,2,128,512]{3,2,1,0:T(8,128)S(1)}, f32[4,128,512]{2,1,0:T(8,128)S(1)}, f32[4,128,512]{2,1,0:T(8,128)S(1)}) custom-call(bf16[4,2,128,128]{3,2,1,0:T(8,128)(2,1)S(1)} %get-tuple-element.23.refs_0_, bf16[4,2,128,128]{3,2,1,0:T(8,128)(2,1)S(1)} %collective-permute-done.refs_1_, ...), custom_call_target="tpu_custom_call" | custom-call | flops 2000000000 | tf_op jit(solution)/shard_map/early/pallas_call | solution.py:304
  12.9 0.0 copy-start.2
  12.9 0.3 collective-permute-done.1.refs_0_
  13.2 0.3 %next.1.refs_0_ = f32[2,128,512]{2,1,0:T(8,128)S(1)} custom-call(bf16[2,2,128,128]{3,2,1,0:T(8,128)(2,1)S(1)} %collective-permute-done.1.refs_0_, bf16[256,512]{1,0:T(8,128)(2,1)S(1)} %copy-done.1, bf16[256,512]{1,0:T(8,128)(2,1)S(1)} %copy-done), custom_call_target="tpu_custom_call" | custom-call | tf_op jit(solution)/shard_map/next/pallas_call | solution.py:304
  13.5 0.5 %collective-permute-done.2.refs_1_ = bf16[2,2,128,128]{3,2,1,0:T(8,128)(2,1)S(1)} collective-permute-done((bf16[2,2,128,128]{3,2,1,0:T(8,128)(2,1)S(1)}, bf16[2,2,128,128]{3,2,1,0:T(8,128)(2,1)S(1)}, u32[]{:S(2)}, u32[]{:S(2)}) %collective-permute-start.2) | collective-permute-done | bytes 131104 | tf_op jit(solution)/shard_map/ppermute | solution.py:317
  14.0 0.0 copy-done.2
  14.0 1.3 %sides.1 = (bf16[4,2,128,128]{3,2,1,0:T(8,128)(2,1)S(1)}, bf16[4,2,128,128]{3,2,1,0:T(8,128)(2,1)S(1)}, f32[2,2,128,512]{3,2,1,0:T(8,128)S(1)}) custom-call(f32[2,128,512]{2,1,0:T(8,128)S(1)} %next.1.refs_0_, bf16[2,2,128,128]{3,2,1,0:T(8,128)(2,1)S(1)} %collective-permute-done.2.refs_1_, f32[4,128,512]{2,1,0:T(8,128)S(1)} %get-tuple-element.25.refs_2_, ...), custom_call_target="tpu_custom_call" | custom-call | tf_op jit(solution)/shard_map/sides/pallas_call | solution.py:304
  15.3 0.1 collective-permute-start.5
  15.3 0.7 %lag.1 = bf16[4,128,256]{2,1,0:T(8,128)(2,1)S(1)} custom-call(f32[2,2,128,512]{3,2,1,0:T(8,128)S(1)} %get-tuple-element.34.refs_0_, f32[2,2,128,512]{3,2,1,0:T(8,128)S(1)} %get-tuple-element.35.refs_1_, bf16[512,256]{1,0:T(8,128)(2,1)S(1)} %copy-done.2, bf16[4,2,128,128]{3,2,1,0:T(8,128)(2,1)S(1)} %get-tuple-element.28.refs_3_), custom_call_target="tpu_custom_call" | custom-call | tf_op jit(solution)/shard_map/lag/pallas_call | solution.py:304
  16.1 1.6 %collective-permute-start.10 = (bf16[1,128,256]{2,1,0:T(8,128)(2,1)S(1)}, bf16[1,128,256]{2,1,0:T(8,128)(2,1)S(1)}, u32[]{:S(2)}, u32[]{:S(2)}) collective-permute-start(bf16[1,128,256]{2,1,0:T(8,128)(2,1)S(1)} %get-tuple-element.41), channel_id=1, source_target_pairs={{0,1},{1,0},{2,3},{3,2},{4,5},{5,4},{6,7},{7,6},{8,9},{9,8},{10,11... | collective-permute-start | bytes 196616 | tf_op jit(solution)/shard_map/ppermute | solution.py:317
  17.7 0.4 %collective-permute-start.9 = (bf16[1,128,256]{2,1,0:T(8,128)(2,1)S(1)}, bf16[1,128,256]{2,1,0:T(8,128)(2,1)S(1)}, u32[]{:S(2)}, u32[]{:S(2)}) collective-permute-start(bf16[1,128,256]{2,1,0:T(8,128)(2,1)S(1)} %get-tuple-element.42), channel_id=1, source_target_pairs={{0,1},{1,0},{2,3},{3,2},{4,5},{5,4},{6,7},{7,6},{8,9},{9,8},{10,11... | collective-permute-start | bytes 196616 | tf_op jit(solution)/shard_map/ppermute | solution.py:317
  18.2 0.0 collective-permute-done.5
  18.3 1.7 %collective-permute-start.6 = (bf16[2,2,128,128]{3,2,1,0:T(8,128)(2,1)S(1)}, bf16[2,2,128,128]{3,2,1,0:T(8,128)(2,1)S(1)}, u32[]{:S(2)}, u32[]{:S(2)}) collective-permute-start(bf16[2,2,128,128]{3,2,1,0:T(8,128)(2,1)S(1)} %pad_maximum_fusion.2), channel_id=1, source_target_pairs={{0,24},{4,28},{8,16},{12,20},{16,8},{20,12},{24,0},{28,4},{1,25},{... | collective-permute-start | bytes 393224 | tf_op jit(solution)/shard_map/ppermute | solution.py:317
  19.9 0.9 %collective-permute-start.7 = (bf16[2,2,128,128]{3,2,1,0:T(8,128)(2,1)S(1)}, bf16[2,2,128,128]{3,2,1,0:T(8,128)(2,1)S(1)}, u32[]{:S(2)}, u32[]{:S(2)}) collective-permute-start(bf16[2,2,128,128]{3,2,1,0:T(8,128)(2,1)S(1)} %pad_maximum_fusion.3), channel_id=1, source_target_pairs={{0,16},{4,20},{8,24},{12,28},{16,0},{20,4},{24,8},{28,12},{1,17},{... | collective-permute-start | bytes 393224 | tf_op jit(solution)/shard_map/ppermute | solution.py:317
  20.9 1.1 %collective-permute-start.8 = (bf16[2,2,128,128]{3,2,1,0:T(8,128)(2,1)S(1)}, bf16[2,2,128,128]{3,2,1,0:T(8,128)(2,1)S(1)}, u32[]{:S(2)}, u32[]{:S(2)}) collective-permute-start(bf16[2,2,128,128]{3,2,1,0:T(8,128)(2,1)S(1)} %pad_maximum_fusion.4), channel_id=1, source_target_pairs={{0,8},{4,12},{8,0},{12,4},{16,24},{20,28},{24,16},{28,20},{1,9},{5... | collective-permute-start | bytes 393224 | tf_op jit(solution)/shard_map/ppermute | solution.py:317
  22.0 0.0 collective-permute-done.10
  22.0 2.7 %collective-permute-start.11 = (bf16[1,128,256]{2,1,0:T(8,128)(2,1)S(1)}, bf16[1,128,256]{2,1,0:T(8,128)(2,1)S(1)}, u32[]{:S(2)}, u32[]{:S(2)}) collective-permute-start(bf16[1,128,256]{2,1,0:T(8,128)(2,1)S(1)} %add_convert_fusion), channel_id=1, source_target_pairs={{0,2},{1,3},{2,0},{3,1},{4,6},{5,7},{6,4},{7,5},{8,10},{9,11},{10,... | collective-permute-start | bytes 196616 | tf_op jit(solution)/shard_map/ppermute | solution.py:317
  24.7 0.0 collective-permute-done.9.refs_9_
  24.7 2.5 %collective-permute-done.11.refs_10_ = bf16[1,128,256]{2,1,0:T(8,128)(2,1)S(1)} collective-permute-done((bf16[1,128,256]{2,1,0:T(8,128)(2,1)S(1)}, bf16[1,128,256]{2,1,0:T(8,128)(2,1)S(1)}, u32[]{:S(2)}, u32[]{:S(2)}) %collective-permute-start.11) | collective-permute-done | bytes 65568 | tf_op jit(solution)/shard_map/ppermute | solution.py:317
  27.2 0.0 collective-permute-done.6.refs_0_
  27.3 0.1 collective-permute-done.7.refs_1_
  27.4 0.0 collective-permute-done.8.refs_2_
  27.4 1.2 %grads.1 = (bf16[8,128,128]{2,1,0:T(8,128)(2,1)}, bf16[8,128,128]{2,1,0:T(8,128)(2,1)}, bf16[8,128,128]{2,1,0:T(8,128)(2,1)}, bf16[8,128,128]{2,1,0:T(8,128)(2,1)}, f32[128,256]{1,0:T(8,128)}) custom-call(bf16[2,2,128,128]{3,2,1,0:T(8,128)(2,1)S(1)} %collective-permute-done.6.refs_0_, bf16[2,2,128,128]{3,2,1,0:T(8,128)(2,1)S(1)} %collective-permute-done.7.refs_1_, ...), custom_call_target="tpu_custom_call" | custom-call | tf_op jit(solution)/shard_map/grads/pallas_call | solution.py:304
  (12 shorter events, 0.2 us)
Async XLA Ops:
  1.9 4.1 %collective-permute-start = (bf16[4,2,128,128]{3,2,1,0:T(8,128)(2,1)S(1)}, bf16[4,2,128,128]{3,2,1,0:T(8,128)(2,1)S(1)}, u32[]{:S(2)}, u32[]{:S(2)}) collective-permute-start(bf16[4,2,128,128]{3,2,1,0:T(8,128)(2,1)S(1)} %get-tuple-element.24), channel_id=1, source_target_pairs={{0,4},{4,0},{8,12},{12,8},{16,20},{20,16},{24,28},{28,24},{1,5},{5... | collective-permute-start | bytes 786440 | tf_op jit(solution)/shard_map/ppermute | solution.py:317
  2.5 7.3 %collective-permute-start.3 = (bf16[2,128,128]{2,1,0:T(8,128)(2,1)S(1)}, bf16[2,128,128]{2,1,0:T(8,128)(2,1)S(1)}, u32[]{:S(2)}, u32[]{:S(2)}) collective-permute-start(bf16[2,128,128]{2,1,0:T(8,128)(2,1)S(1)} %get-tuple-element.55), channel_id=1, source_target_pairs={{0,24},{4,28},{8,16},{12,20},{16,8},{20,12},{24,0},{28,4},{1,25},{... | collective-permute-start | bytes 196616 | tf_op jit(solution)/shard_map/ppermute | solution.py:317
  6.0 5.9 %copy-start.3 = (bf16[128,1024]{1,0:T(8,128)(2,1)S(1)}, bf16[128,1024]{1,0:T(8,128)(2,1)}, u32[]{:S(2)}) copy-start(bf16[128,1024]{1,0:T(8,128)(2,1)} %refs_4_.2) | copy-start | bytes 786436
  6.0 5.9 %collective-permute-start.4 = (bf16[2,128,128]{2,1,0:T(8,128)(2,1)S(1)}, bf16[2,128,128]{2,1,0:T(8,128)(2,1)S(1)}, u32[]{:S(2)}, u32[]{:S(2)}) collective-permute-start(bf16[2,128,128]{2,1,0:T(8,128)(2,1)S(1)} %get-tuple-element.52), channel_id=1, source_target_pairs={{0,24},{4,28},{8,16},{12,20},{16,8},{20,12},{24,0},{28,4},{1,25},{... | collective-permute-start | bytes 196616 | tf_op jit(solution)/shard_map/ppermute | solution.py:317
  7.5 4.4 %copy-start = (bf16[256,512]{1,0:T(8,128)(2,1)S(1)}, bf16[256,512]{1,0:T(8,128)(2,1)}, u32[]{:S(2)}) copy-start(bf16[256,512]{1,0:T(8,128)(2,1)} %constant.7.clone.refs_2_.refs_6_.refs_4_) | copy-start | bytes 786436
  7.5 4.4 %copy-start.1 = (bf16[256,512]{1,0:T(8,128)(2,1)S(1)}, bf16[256,512]{1,0:T(8,128)(2,1)}, u32[]{:S(2)}) copy-start(bf16[256,512]{1,0:T(8,128)(2,1)} %constant.6.clone.refs_1_.refs_5_.refs_3_) | copy-start | bytes 786436
  7.5 5.7 %collective-permute-start.1 = (bf16[2,2,128,128]{3,2,1,0:T(8,128)(2,1)S(1)}, bf16[2,2,128,128]{3,2,1,0:T(8,128)(2,1)S(1)}, u32[]{:S(2)}, u32[]{:S(2)}) collective-permute-start(bf16[2,2,128,128]{3,2,1,0:T(8,128)(2,1)S(1)} %pad_maximum_fusion), channel_id=1, source_target_pairs={{0,8},{4,12},{8,0},{12,4},{16,24},{20,28},{24,16},{28,20},{1,9},{5... | collective-permute-start | bytes 393224 | tf_op jit(solution)/shard_map/ppermute | solution.py:317
  8.1 5.8 %collective-permute-start.2 = (bf16[2,2,128,128]{3,2,1,0:T(8,128)(2,1)S(1)}, bf16[2,2,128,128]{3,2,1,0:T(8,128)(2,1)S(1)}, u32[]{:S(2)}, u32[]{:S(2)}) collective-permute-start(bf16[2,2,128,128]{3,2,1,0:T(8,128)(2,1)S(1)} %pad_maximum_fusion.1), channel_id=1, source_target_pairs={{0,16},{4,20},{8,24},{12,28},{16,0},{20,4},{24,8},{28,12},{1,17},{... | collective-permute-start | bytes 393224 | tf_op jit(solution)/shard_map/ppermute | solution.py:317
  12.9 1.1 %copy-start.2 = (bf16[512,256]{1,0:T(8,128)(2,1)S(1)}, bf16[512,256]{1,0:T(8,128)(2,1)}, u32[]{:S(2)}) copy-start(bf16[512,256]{1,0:T(8,128)(2,1)} %constant.8.clone.refs_5_.refs_2_) | copy-start | bytes 786436
  15.3 2.9 %collective-permute-start.5 = (bf16[4,2,128,128]{3,2,1,0:T(8,128)(2,1)S(1)}, bf16[4,2,128,128]{3,2,1,0:T(8,128)(2,1)S(1)}, u32[]{:S(2)}, u32[]{:S(2)}) collective-permute-start(bf16[4,2,128,128]{3,2,1,0:T(8,128)(2,1)S(1)} %get-tuple-element.29), channel_id=1, source_target_pairs={{0,4},{4,0},{8,12},{12,8},{16,20},{20,16},{24,28},{28,24},{1,5},{5... | collective-permute-start | bytes 786440 | tf_op jit(solution)/shard_map/ppermute | solution.py:317
  16.1 5.9 %collective-permute-start.10 = (bf16[1,128,256]{2,1,0:T(8,128)(2,1)S(1)}, bf16[1,128,256]{2,1,0:T(8,128)(2,1)S(1)}, u32[]{:S(2)}, u32[]{:S(2)}) collective-permute-start(bf16[1,128,256]{2,1,0:T(8,128)(2,1)S(1)} %get-tuple-element.41), channel_id=1, source_target_pairs={{0,1},{1,0},{2,3},{3,2},{4,5},{5,4},{6,7},{7,6},{8,9},{9,8},{10,11... | collective-permute-start | bytes 196616 | tf_op jit(solution)/shard_map/ppermute | solution.py:317
  17.7 7.0 %collective-permute-start.9 = (bf16[1,128,256]{2,1,0:T(8,128)(2,1)S(1)}, bf16[1,128,256]{2,1,0:T(8,128)(2,1)S(1)}, u32[]{:S(2)}, u32[]{:S(2)}) collective-permute-start(bf16[1,128,256]{2,1,0:T(8,128)(2,1)S(1)} %get-tuple-element.42), channel_id=1, source_target_pairs={{0,1},{1,0},{2,3},{3,2},{4,5},{5,4},{6,7},{7,6},{8,9},{9,8},{10,11... | collective-permute-start | bytes 196616 | tf_op jit(solution)/shard_map/ppermute | solution.py:317
  18.3 9.0 %collective-permute-start.6 = (bf16[2,2,128,128]{3,2,1,0:T(8,128)(2,1)S(1)}, bf16[2,2,128,128]{3,2,1,0:T(8,128)(2,1)S(1)}, u32[]{:S(2)}, u32[]{:S(2)}) collective-permute-start(bf16[2,2,128,128]{3,2,1,0:T(8,128)(2,1)S(1)} %pad_maximum_fusion.2), channel_id=1, source_target_pairs={{0,24},{4,28},{8,16},{12,20},{16,8},{20,12},{24,0},{28,4},{1,25},{... | collective-permute-start | bytes 393224 | tf_op jit(solution)/shard_map/ppermute | solution.py:317
  19.9 7.4 %collective-permute-start.7 = (bf16[2,2,128,128]{3,2,1,0:T(8,128)(2,1)S(1)}, bf16[2,2,128,128]{3,2,1,0:T(8,128)(2,1)S(1)}, u32[]{:S(2)}, u32[]{:S(2)}) collective-permute-start(bf16[2,2,128,128]{3,2,1,0:T(8,128)(2,1)S(1)} %pad_maximum_fusion.3), channel_id=1, source_target_pairs={{0,16},{4,20},{8,24},{12,28},{16,0},{20,4},{24,8},{28,12},{1,17},{... | collective-permute-start | bytes 393224 | tf_op jit(solution)/shard_map/ppermute | solution.py:317
  20.9 6.5 %collective-permute-start.8 = (bf16[2,2,128,128]{3,2,1,0:T(8,128)(2,1)S(1)}, bf16[2,2,128,128]{3,2,1,0:T(8,128)(2,1)S(1)}, u32[]{:S(2)}, u32[]{:S(2)}) collective-permute-start(bf16[2,2,128,128]{3,2,1,0:T(8,128)(2,1)S(1)} %pad_maximum_fusion.4), channel_id=1, source_target_pairs={{0,8},{4,12},{8,0},{12,4},{16,24},{20,28},{24,16},{28,20},{1,9},{5... | collective-permute-start | bytes 393224 | tf_op jit(solution)/shard_map/ppermute | solution.py:317
  22.0 5.2 %collective-permute-start.11 = (bf16[1,128,256]{2,1,0:T(8,128)(2,1)S(1)}, bf16[1,128,256]{2,1,0:T(8,128)(2,1)S(1)}, u32[]{:S(2)}, u32[]{:S(2)}) collective-permute-start(bf16[1,128,256]{2,1,0:T(8,128)(2,1)S(1)} %add_convert_fusion), channel_id=1, source_target_pairs={{0,2},{1,3},{2,0},{3,1},{4,6},{5,7},{6,4},{7,5},{8,10},{9,11},{10,... | collective-permute-start | bytes 196616 | tf_op jit(solution)/shard_map/ppermute | solution.py:317
